TPU v7x, 1024 devices: a whole 8x8x8 slice. The times are simulated.
1024 devices in a mesh: dp: 64 (over x, y), tensor: 8 (over z_hi, core), replica: 2 (over z_lo).
Axes of the slice: x: 8, y: 8, z: 8 (z_hi: 4, z_lo: 2; z = z_hi * 2 + z_lo), core: 2. Of those that a mesh axis runs over, the one named last changes fastest.
Arguments:
- tokens: bfloat16 [16384, 3072], P(('dp', 'replica')), may hold values from -6 to 6
- queries: bfloat16 [16384, 3072], P(('dp', 'replica'), 'tensor'), may hold values from -172 to 172
- key_rows: bfloat16 [16384, 3072], P(('dp', 'replica'), 'tensor'), may hold values from -4.5 to 4.5
- value_rows: bfloat16 [16384, 3072], P(('dp', 'replica'), 'tensor'), may hold values from -6 to 6
- cotangent: bfloat16 [16384, 3072], P(('dp', 'replica'), 'tensor'), may hold values from -0.23925781 to 0.23925781
- probe_shards: bfloat16 [8, 1327104], P('tensor', 'dp'), may hold values from -4 to 4
- hess_old: float32 [8, 1327104], P('tensor', 'dp'), may hold values from -1.5 to 1.5
- shard_counts: int32 [64], replicated, may hold values from 16128 to 20736, as said below
Outputs:
- hess_new: float32 [8, 1327104], P('tensor', 'dp')
Inputs may be any that keep to these rules, and one draw needn't show every extreme that they name: `shard_counts`: every entry is a multiple of 128, the entries sum to 1179648, and the largest is exactly 20736; slots of a shard past its count are not read.
All inputs are finite; a program needn't handle non-finite values.
Results may differ from a plain program's by a relative error of at most 0.0035.
Values may be sent and summed in bfloat16 or wider, within the bound.
No kernel may reach another device: no remote copies, remote signals or barrier semaphores. Data moves between devices by JAX's collectives and lax.ppermute only.
A program may use at most 32 MiB of HBM per device.

v0:
```python
import math

import jax
import jax.numpy as jnp
from jax import lax
from jax.sharding import PartitionSpec as P

HEAD = 96


decay_rate = 0.99


def shard_tables(counts):
    block_sizes = counts // 128
    starts = jnp.cumsum(block_sizes) - block_sizes
    return (block_sizes, starts)


def spread_probe(gathered, block_sizes, starts, cap_blocks, total_blocks, width, columns):
    inner_slot = lax.iota(jnp.int32, cap_blocks)
    in_use = inner_slot[None, :] < block_sizes[:, None]
    target = jnp.where(in_use, starts[:, None] + inner_slot[None, :], total_blocks).reshape(-1)
    slab_blocks = (
        jnp.zeros((total_blocks, 128), gathered.dtype)
        .at[target]
        .set(gathered.reshape(-1, 128), mode="drop")
    )
    return slab_blocks.reshape(width, columns)


def pick_slots(hessian_blocks, block_sizes, starts, first_slot, slot_count):
    inner_slot = first_slot + lax.iota(jnp.int32, slot_count)
    in_use = inner_slot[None, :] < block_sizes[:, None]
    source = jnp.where(in_use, starts[:, None] + inner_slot[None, :], 0)
    return jnp.where(in_use[:, :, None], hessian_blocks[source], jnp.float32(0.0))


def second_order(query, key_head, value_head, cot_head, tangent_head):
    inv_root = 1.0 / math.sqrt(query.shape[1])
    length = query.shape[0]
    scores = inv_root * jnp.dot(query, key_head.T, preferred_element_type=jnp.float32)
    causal = lax.iota(jnp.int32, length)[:, None] >= lax.iota(jnp.int32, length)[None, :]
    scores = jnp.where(causal, scores, jnp.float32(-1e30))
    row_peak = jnp.max(scores, axis=1, keepdims=True)
    expo_terms = jnp.exp(scores - row_peak)
    attn_weights = expo_terms / jnp.sum(expo_terms, axis=1, keepdims=True)
    score_tangent = inv_root * jnp.dot(tangent_head, key_head.T, preferred_element_type=jnp.float32)
    back_scores = jnp.dot(cot_head, value_head.T, preferred_element_type=jnp.float32)
    row_delta = jnp.sum(attn_weights * back_scores, axis=1, keepdims=True)
    mean_tangent = jnp.sum(attn_weights * score_tangent, axis=1, keepdims=True)
    weight_tangent = attn_weights * (score_tangent - mean_tangent)
    delta_tangent = jnp.sum(weight_tangent * back_scores, axis=1, keepdims=True)
    grad_tangent = (
        weight_tangent * (back_scores - row_delta) - attn_weights * delta_tangent
    ).astype(jnp.bfloat16)
    return (inv_root * jnp.dot(grad_tangent, key_head, preferred_element_type=jnp.float32)).astype(
        jnp.bfloat16
    )


def head_rows(query, key_part, value_part, cot_part, tangent_part, head_size):
    length, columns = query.shape

    def by_head(array):
        return array.reshape(length, columns // head_size, head_size).transpose(1, 0, 2)

    result = lax.map(
        lambda bundle: second_order(*bundle),
        (
            by_head(query),
            by_head(key_part),
            by_head(value_part),
            by_head(cot_part),
            by_head(tangent_part),
        ),
    )
    return result.transpose(1, 0, 2).reshape(length, columns)


def body(tokens, queries, key_rows, value_rows, cotangent, probe_shards, hess_old, shard_counts):
    width = tokens.shape[1]
    columns = queries.shape[1]
    cap_blocks = probe_shards.shape[1] // 128
    half_blocks = cap_blocks // 2
    total_blocks = width * columns // 128
    copy_index = lax.axis_index("replica")
    block_sizes, starts = shard_tables(shard_counts)
    gathered = lax.all_gather(probe_shards[0], "dp", axis=0, tiled=True)
    probe_full = spread_probe(
        gathered, block_sizes, starts, cap_blocks, total_blocks, width, columns
    )
    tangent = jnp.dot(tokens, probe_full, preferred_element_type=jnp.float32).astype(jnp.bfloat16)
    scaled = head_rows(queries, key_rows, value_rows, cotangent, tangent, HEAD)
    pair_tokens, pair_scaled = (
        lax.all_gather(tokens, "replica", axis=0, tiled=True),
        lax.all_gather(scaled, "replica", axis=0, tiled=True),
    )
    group_term = jnp.einsum(
        "td,tc->dc", pair_tokens, pair_scaled, preferred_element_type=jnp.float32
    ).astype(jnp.bfloat16)
    group_term = lax.optimization_barrier(group_term)
    hessian_probe = group_term.astype(jnp.float32)
    first_slot = copy_index * half_blocks
    picked = pick_slots(
        hessian_probe.reshape(-1, 128), block_sizes, starts, first_slot, half_blocks
    ).reshape(-1)
    summed = lax.psum_scatter(picked, "dp", scatter_dimension=0, tiled=True)
    own_shard = lax.all_gather(summed, "replica", axis=0, tiled=True)
    updated = (
        decay_rate * hess_old[0]
        + (1.0 - decay_rate) * probe_shards[0].astype(jnp.float32) * own_shard
    )
    return updated[None, :]


def solution(mesh):
    placed = (
        P(("dp", "replica"), None),
        P(("dp", "replica"), "tensor"),
        P(("dp", "replica"), "tensor"),
        P(("dp", "replica"), "tensor"),
        P(("dp", "replica"), "tensor"),
        P("tensor", "dp"),
        P("tensor", "dp"),
        P(),
    )
    return jax.shard_map(
        body, mesh=mesh, in_specs=placed, out_specs=P("tensor", "dp"), check_vma=False
    )
```

profile of v0, /device:TPU:4, one launch (start us, length us, event | category | flops | bytes accessed | tf_op | source)
XLA Modules:
  0.0 452.6 jit_solution(8631383486914397662)
XLA Ops:
  6.5 0.0 all-gather.7.cloned.1.call-start
  6.5 0.7 all-gather.7.cloned.1.call-update
  7.3 0.0 all-gather.5.cloned.1.call-start
  7.3 0.7 all-gather.5.cloned.1.call-update
  8.0 0.0 all-reduce.3.cloned.1.call-start
  8.1 0.7 fusion.40
  8.7 0.7 and_select_fusion
  9.4 0.1 copy.24
  9.5 0.1 reduce-window.9
  9.6 0.1 reduce.2
  9.7 0.7 fusion.39
  10.4 0.1 add_select_fusion
  10.5 0.1 compare_select_fusion.1
  10.5 0.1 broadcast_compare_fusion
  10.6 0.3 select_n.65
  10.9 0.1 fusion.33
  11.0 1.6 copy.26
  12.6 1.6 copy.27
  14.3 1.0 copy.22
  15.3 1.0 copy.23
  16.3 0.1 reshape.267
  16.5 100.5 %all-gather.7.cloned.1.call-done = bf16[1,1327104]{1,0:T(2,128)(2,1)} async-done(((bf16[1,20736]{1,0:T(2,128)(2,1)}), bf16[1,1327104]{1,0:T(2,128)(2,1)}) %all-gather.7.cloned.1.call-update) | async-done | bytes 2654224 | tf_op jit(solution)/shard_map/all_gather | solution.py:89
  116.9 56.2 %reduce.4 = bf16[1327104]{0:T(1024)(128)(2,1)S(1)} reduce(bf16[1,1327104]{1,0:T(2,128)(2,1)} %all-gather.7.cloned.1.call-done, bf16[]{:T(256)} %constant.73), dimensions={0}, to_apply=%all-gather.reduce_sub_computation | reduce | bytes 5308418 | tf_op jit(solution)/shard_map/all_gather | solution.py:89
  173.1 43.7 %scatter_custom_fusion = bf16[9216,128]{1,0:T(8,128)(2,1)} fusion(s32[10368]{0:T(1024)S(1)} %fusion.33, bf16[1327104]{0:T(1024)(128)(2,1)S(1)} %reduce.4, bf16[]{:T(256)} %constant.60.clone.1), kind=kCustom, calls=%fused_computation.42 | custom fusion | bytes 5013506 | tf_op jit(solution)/shard_map/scatter | solution.py:27
  216.8 3.8 reshape.256
  220.5 0.0 copy-done
  220.6 0.8 convolution_convert_fusion.1
  221.4 0.1 copy.25
  221.5 9.1 %while.10 = (s32[]{:T(128)}, bf16[4,128,96]{1,2,0:T(8,128)(2,1)}, bf16[4,128,96]{1,2,0:T(8,128)(2,1)S(1)}, bf16[4,128,96]{1,2,0:T(8,128)(2,1)S(1)}, bf16[4,128,9...) while((s32[]{:T(128)}, bf16[4,128,96]{1,2,0:T(8,128)(2,1)}, ...), condition=%wide.region_8.9_spmd, body=%wide.region_2.8_spmd.sunk | while | flops 13065602 | bytes 872533 | solution.py:68
  221.5 0.2 fusion.46
  221.8 0.2 multiply_reduce_fusion.7
  222.0 1.0 multiply_reduce_fusion.8
  223.0 0.8 fusion.48
  223.8 0.2 fusion.46
  224.1 0.2 multiply_reduce_fusion.7
  224.3 1.0 multiply_reduce_fusion.8
  225.3 0.8 fusion.48
  226.1 0.2 fusion.46
  226.3 0.2 multiply_reduce_fusion.7
  226.6 1.0 multiply_reduce_fusion.8
  227.6 0.8 fusion.48
  228.4 0.2 fusion.46
  228.6 0.2 multiply_reduce_fusion.7
  228.9 1.0 multiply_reduce_fusion.8
  229.9 0.8 fusion.48
  230.6 5.7 %all_gather.13 = bf16[256,384]{0,1:T(8,128)(2,1)S(1)} all-gather(bf16[128,384]{0,1:T(8,128)(2,1)} %bitcast.96), channel_id=1, replica_groups=mesh['dp'=64,'tensor'=8,'replica'=2] {'replica'}, dimensions={0}, use_global_device_ids=true | all-gather | bytes 294912 | tf_op jit(solution)/shard_map/all_gather | solution.py:97
  236.3 2.2 fusion.29
  238.5 3.0 copy.32
  241.5 5.8 %reshape.264 = f32[9216,128]{1,0:T(8,128)} reshape(f32[3072,384]{1,0:T(8,128)} %copy.32) | data formatting | bytes 9437184 | tf_op jit(solution)/shard_map/reshape | solution.py:106
  247.3 11.0 %gather_fusion = f32[5184,128]{1,0:T(8,128)S(1)} fusion(f32[9216,128]{1,0:T(8,128)} %reshape.264, s32[6144]{0:T(1024)S(1)} %pad_clamp_fusion), kind=kCustom, calls=%fused_computation | custom fusion | bytes 5329152 | tf_op jit(solution)/shard_map/gather | solution.py:36
  258.3 1.7 reshape.266
  260.0 3.1 broadcast_select_fusion
  263.0 1.7 select_n.70
  264.7 0.0 all-reduce.3.cloned.1.call-update
  264.8 1.3 dynamic-slice
  266.7 0.0 copy-done.2
  266.7 0.2 multiply_reduce_fusion.4
  267.0 0.3 multiply_reduce_fusion.3
  267.3 172.1 %all-reduce.3.cloned.1.call-done = f32[663552]{0:T(1024)} async-done(((f32[663552]{0:T(1024)}), f32[663552]{0:T(1024)}) %all-reduce.3.cloned.1.call-update) | async-done | bytes 2654224
  439.4 0.9 dynamic-slice.1
  440.3 4.7 %all-gather.1 = f32[2,1,10368]{2,1,0:T(1,128)S(1)} all-gather(f32[1,1,10368]{2,1,0:T(1,128)S(1)} %reshape.287), channel_id=1, replica_groups=mesh['dp'=64,'tensor'=8,'replica'=2] {'replica'}, dimensions={0}, use_global_device_ids=true | all-gather | bytes 124416 | tf_op jit(solution)/shard_map/all_gather | solution.py:109
  445.0 0.3 reduce.5
  445.2 0.1 reshape.288
  445.3 0.7 broadcast_in_dim.64
  (14 shorter events, 0.2 us)
Async XLA Ops:
  6.5 110.4 %all-gather.7.cloned.1.call-start = ((), (), s32[]{:S(2)}) async-start(), calls=%async_computation.1 | async-start | bytes 5391360 | tf_op jit(solution)/shard_map/all_gather | solution.py:89
  7.3 229.1 %all-gather.5.cloned.1.call-start = ((), (), s32[]{:S(2)}) async-start(), calls=%async_computation | async-start | bytes 2359296 | tf_op jit(solution)/shard_map/all_gather | solution.py:96
  8.0 431.4 %all-reduce.3.cloned.1.call-start = ((), (), s32[]{:S(2)}) async-start(), calls=%async_computation.2 | async-start | bytes 5308416
  216.8 3.8 copy-start
  264.7 2.0 copy-start.2
  264.7 2.3 copy-start.1
Sparse Core Ops, SparseCore 0:
  11.6 105.2 all-gather.6
  119.6 35.9 all-gather.4
  264.9 174.4 all-reduce.2
where the time goes:
time: 454 us; the launch traced here: 453 us
  waiting for transfers between devices  274 us (60%)
  local copies, waits for them, and re-layouts  79.5 us (18%)
  other arithmetic  62.8 us (14%)
  between operations  13.9 us (3%)
  matrix products  11.9 us (3%)
  blocking collectives  10.4 us (2%)
    unnamed x4, waiting for transfers between devices  174 us
    all_gather x1, waiting for transfers between devices, body(): gathered = lax.all_gather(probe_shards[0], 'dp', axis=0, tiled=True)  100 us
    all_gather x1, other arithmetic, body(): gathered = lax.all_gather(probe_shards[0], 'dp', axis=0, tiled=True)  56.2 us
    scatter x1, local copies, waits for them, and re-layouts, spread_probe(): slab_blocks = jnp.zeros((total_blocks, 128), gathered.dtype).at[target].s...  43.7 us
    gather x2, local copies, waits for them, and re-layouts, pick_slots(): hessian_blocks[source]  12.7 us
  transfers between devices with their start and end apart: 3, of which 2 were waited for; matrix products, arithmetic and copies ran while one was open for 27% of the time, Pallas kernels for 0%

commit v1 on v0

v1 whole, which is shorter than its diff:
```python
import math

import jax
import jax.numpy as jnp
from jax import lax
from jax.experimental import pallas as pl
from jax.experimental.pallas import tpu as pltpu
from jax.sharding import PartitionSpec as P

HEAD = 96
LANES = 128
HALF = LANES // 2
decay_rate = 0.99

BLOCKS = 3
OUTER = 56
PAIRED = 32
WINDOW = OUTER + PAIRED

VMEM = pl.BlockSpec(memory_space=pltpu.VMEM)
SMEM = pl.BlockSpec(memory_space=pltpu.SMEM)


def params():
    return pltpu.CompilerParams(vmem_limit_bytes=48 * 1024 * 1024)


def left_lanes(rows):
    return lax.broadcasted_iota(jnp.int32, (rows, LANES), 1) < HALF


def first_block(counts_ref, shard):
    return lax.fori_loop(0, shard, lambda at, total: total + counts_ref[at] // LANES, jnp.int32(0))


def pack_shard(place_ref, counts_ref, probe_ref, out_ref, rows):
    copy = place_ref[0]
    shift = lax.rem(first_block(counts_ref, place_ref[1]), BLOCKS)
    rows[...] = jnp.zeros_like(rows)
    for block in range(probe_ref.shape[1] // LANES):
        rows[pl.ds(shift + block, 1), :] = probe_ref[0:1, block * LANES : (block + 1) * LANES].astype(jnp.float32)
    outer = rows[pl.ds(2 * copy, OUTER, stride=BLOCKS), :]
    middle = rows[pl.ds(1, OUTER, stride=BLOCKS), :]
    turned = pltpu.roll(middle, HALF, 1)
    near = jnp.where(copy == 0, middle, turned)
    far = jnp.where(copy == 0, turned, middle)
    far = jnp.concatenate([far[PAIRED:], jnp.zeros((2 * PAIRED - OUTER, LANES), jnp.float32)], axis=0)
    paired = jnp.where(left_lanes(PAIRED), near[:PAIRED], far)
    window = jnp.concatenate([outer, paired], axis=0).astype(jnp.bfloat16)

    def store(shard, carry):
        out_ref[shard] = window
        return carry

    lax.fori_loop(0, out_ref.shape[0], store, 0, unroll=8)


def split_heads(place_ref, query_ref, key_ref, value_ref, cot_ref, keep_ref, send_ref):
    copy = place_ref[0]
    width = query_ref.shape[1] // 2

    def fill(first_ref, second_ref):
        for at, ref in enumerate((query_ref, key_ref, value_ref, cot_ref)):
            first_ref[:, at * width : (at + 1) * width] = ref[:, :width]
            second_ref[:, at * width : (at + 1) * width] = ref[:, width:]

    @pl.when(copy == 0)
    def _():
        fill(keep_ref, send_ref)

    @pl.when(copy == 1)
    def _():
        fill(send_ref, keep_ref)


def transpose_tokens(own_ref, other_ref, out_ref):
    length = own_ref.shape[0]
    out_ref[:, :length] = own_ref[...].T
    out_ref[:, length:] = other_ref[...].T


def second_order(query, key_head, value_head, cot_head, tangent):
    length = query.shape[0]
    inv_root = 1.0 / math.sqrt(HEAD)
    causal = lax.broadcasted_iota(jnp.int32, (length, length), 0) >= lax.broadcasted_iota(
        jnp.int32, (length, length), 1
    )

    def times_transposed(left, right):
        return lax.dot_general(left, right, (((1,), (1,)), ((), ())), preferred_element_type=jnp.float32)

    scores = inv_root * times_transposed(query, key_head)
    scores = jnp.where(causal, scores, jnp.float32(-1e30))
    expo_terms = jnp.exp(scores - jnp.max(scores, axis=1, keepdims=True))
    attn = expo_terms / jnp.sum(expo_terms, axis=1, keepdims=True)
    score_tangent = inv_root * times_transposed(tangent, key_head)
    back = times_transposed(cot_head, value_head)
    delta = jnp.sum(attn * back, axis=1, keepdims=True)
    mean_tangent = jnp.sum(attn * score_tangent, axis=1, keepdims=True)
    weight_tangent = attn * (score_tangent - mean_tangent)
    delta_tangent = jnp.sum(weight_tangent * back, axis=1, keepdims=True)
    grad_tangent = (weight_tangent * (back - delta) - attn * delta_tangent).astype(jnp.bfloat16)
    return (inv_root * jnp.dot(grad_tangent, key_head, preferred_element_type=jnp.float32)).astype(jnp.bfloat16)


def middle_part(
    place_ref,
    counts_ref,
    pieces_ref,
    own_tokens_ref,
    other_tokens_ref,
    turned_ref,
    own_heads_ref,
    other_heads_ref,
    out_ref,
    outer,
    middle,
    probe,
    tangent,
    scaled,
    spread,
):
    copy = place_ref[0]
    length, features = own_tokens_ref.shape
    shards = pieces_ref.shape[0]
    columns = tangent.shape[1]
    left = left_lanes(PAIRED)
    top_row = lax.broadcasted_iota(jnp.int32, (8, LANES), 0) == 0

    def place(shard, start):
        first = start // BLOCKS
        shift = start - first * BLOCKS
        piece = pieces_ref[shard].astype(jnp.float32)
        paired = piece[OUTER:]
        for slab, block, values in (
            (outer, 2 * copy, piece[:OUTER]),
            (
                middle,
                1,
                jnp.concatenate(
                    [jnp.where(left, paired, 0.0), jnp.where(left, 0.0, paired)[: OUTER - PAIRED]], axis=0
                ),
            ),
        ):
            before = slab[pl.ds(first, 8), :]
            slab[pl.ds(first, 8), :] = jnp.where(top_row & (block < shift), before, values[:8])
            slab[pl.ds(first + 8, OUTER - 8), :] = values[8:]
        return start + counts_ref[shard] // LANES

    lax.fori_loop(0, shards, place, jnp.int32(0), unroll=4)
    probe[:, :LANES] = outer[:features, :].astype(jnp.bfloat16)
    probe[:, LANES:] = middle[:features, :].astype(jnp.bfloat16)

    for at, tokens_ref in enumerate((own_tokens_ref, other_tokens_ref)):
        product = jnp.dot(tokens_ref[...], probe[...], preferred_element_type=jnp.float32)
        rows = slice(at * length, (at + 1) * length)
        outer_part = product[:, :LANES].astype(jnp.bfloat16)
        middle_half = (product[:, LANES : LANES + HALF] + product[:, LANES + HALF :]).astype(jnp.bfloat16)

        @pl.when(copy == 0)
        def _():
            tangent[rows, :LANES] = outer_part
            tangent[rows, LANES:] = middle_half

        @pl.when(copy == 1)
        def _():
            tangent[rows, :HALF] = middle_half
            tangent[rows, HALF:] = outer_part

    for at, heads_ref in enumerate((own_heads_ref, other_heads_ref)):
        rows = slice(at * length, (at + 1) * length)
        for head in range(columns // HEAD):
            cuts = [slice(part * columns + head * HEAD, part * columns + (head + 1) * HEAD) for part in range(4)]
            cut = slice(head * HEAD, (head + 1) * HEAD)
            scaled[rows, cut] = second_order(*(heads_ref[:, one] for one in cuts), tangent[rows, cut])

    @pl.when(copy == 0)
    def _():
        spread[:, :LANES] = scaled[:, :LANES]
        spread[:, LANES : LANES + HALF] = scaled[:, LANES:]
        spread[:, LANES + HALF :] = scaled[:, LANES:]

    @pl.when(copy == 1)
    def _():
        spread[:, :LANES] = scaled[:, HALF:]
        spread[:, LANES : LANES + HALF] = scaled[:, :HALF]
        spread[:, LANES + HALF :] = scaled[:, :HALF]

    term = jnp.dot(turned_ref[...], spread[...], preferred_element_type=jnp.float32)
    outer[:features, :] = term[:, :LANES]
    middle[:features, :] = term[:, LANES:]

    def cut_out(shard, start):
        first = start // BLOCKS
        paired = jnp.where(left, middle[pl.ds(first, PAIRED), :], middle[pl.ds(first + PAIRED, PAIRED), :])
        out_ref[shard] = jnp.concatenate([outer[pl.ds(first, OUTER), :], paired], axis=0).astype(jnp.bfloat16)
        return start + counts_ref[shard] // LANES

    lax.fori_loop(0, shards, cut_out, jnp.int32(0), unroll=4)


def add_groups(terms_ref, out_ref):
    def add(group, total):
        return total + terms_ref[group].astype(jnp.float32)

    out_ref[...] = lax.fori_loop(0, terms_ref.shape[0], add, jnp.zeros(out_ref.shape, jnp.float32), unroll=4)


def update_shard(place_ref, counts_ref, own_ref, other_ref, probe_ref, hess_ref, out_ref, rows):
    copy = place_ref[0]
    shard = place_ref[1]
    shift = lax.rem(first_block(counts_ref, shard), BLOCKS)
    blocks = probe_ref.shape[0]
    first = jnp.where(copy == 0, own_ref[...], other_ref[...])
    second = jnp.where(copy == 0, other_ref[...], own_ref[...])
    left = left_lanes(PAIRED)
    low, high = first[OUTER:], second[OUTER:]
    near = jnp.where(left, low, pltpu.roll(high, HALF, 1))
    far = jnp.where(left, pltpu.roll(low, HALF, 1), high)
    rows[pl.ds(0, OUTER, stride=BLOCKS), :] = first[:OUTER]
    rows[pl.ds(1, OUTER, stride=BLOCKS), :] = jnp.concatenate([near, far[: OUTER - PAIRED]], axis=0)
    rows[pl.ds(2, OUTER, stride=BLOCKS), :] = second[:OUTER]
    inner = lax.broadcasted_iota(jnp.int32, (blocks, LANES), 0)
    product = jnp.where(inner < counts_ref[shard] // LANES, rows[pl.ds(shift, blocks), :], 0.0)
    out_ref[...] = decay_rate * hess_ref[...] + (1.0 - decay_rate) * probe_ref[...].astype(jnp.float32) * product


def call(kernel, shape, dtype, operands, scalars, scratch=()):
    return pl.pallas_call(
        kernel,
        out_shape=jax.ShapeDtypeStruct(shape, dtype) if isinstance(shape, tuple) else shape,
        in_specs=[SMEM] * scalars + [VMEM] * (len(operands) - scalars),
        out_specs=VMEM if isinstance(shape, tuple) else [VMEM] * len(shape),
        scratch_shapes=list(scratch),
        compiler_params=params(),
        name=kernel.__name__,
    )(*operands)


def body(tokens, queries, key_rows, value_rows, cotangent, probe_shards, hess_old, shard_counts):
    length, width = tokens.shape
    half = queries.shape[1] // 2
    shards = shard_counts.shape[0]
    blocks = probe_shards.shape[1] // LANES
    slab = pltpu.VMEM((width + 2 * PAIRED, LANES), jnp.float32)
    rows = pltpu.VMEM((BLOCKS * OUTER + 8, LANES), jnp.float32)
    place = jnp.stack([lax.axis_index("replica"), lax.axis_index("dp")]).astype(jnp.int32)
    swap = [(0, 1), (1, 0)]

    packed = call(
        pack_shard, (shards, WINDOW, LANES), jnp.bfloat16, (place, shard_counts, probe_shards), 2, (rows,)
    )
    pieces = lax.all_to_all(packed, "dp", 0, 0)

    other_tokens = lax.ppermute(tokens, "replica", swap)
    both = jax.ShapeDtypeStruct((length, 4 * half), jnp.bfloat16)
    own_heads, sent_heads = call(
        split_heads, [both, both], None, (place, queries, key_rows, value_rows, cotangent), 1
    )
    other_heads = lax.ppermute(sent_heads, "replica", swap)
    turned = call(transpose_tokens, (width, 2 * length), jnp.bfloat16, (tokens, other_tokens), 0)

    windows = call(
        middle_part,
        (shards, WINDOW, LANES),
        jnp.bfloat16,
        (place, shard_counts, pieces, tokens, other_tokens, turned, own_heads, other_heads),
        2,
        (
            slab,
            slab,
            pltpu.VMEM((width, 2 * LANES), jnp.bfloat16),
            pltpu.VMEM((2 * length, half), jnp.bfloat16),
            pltpu.VMEM((2 * length, half), jnp.bfloat16),
            pltpu.VMEM((2 * length, 2 * LANES), jnp.bfloat16),
        ),
    )
    terms = lax.all_to_all(windows, "dp", 0, 0)
    summed = call(add_groups, (WINDOW, LANES), jnp.float32, (terms,), 0)
    other_summed = lax.ppermute(summed, "replica", swap)
    updated = call(
        update_shard,
        (blocks, LANES),
        jnp.float32,
        (
            place,
            shard_counts,
            summed,
            other_summed,
            probe_shards.reshape(blocks, LANES),
            hess_old.reshape(blocks, LANES),
        ),
        2,
        (rows,),
    )
    return updated.reshape(1, blocks * LANES)


def solution(mesh):
    placed = (
        P(("dp", "replica"), None),
        P(("dp", "replica"), "tensor"),
        P(("dp", "replica"), "tensor"),
        P(("dp", "replica"), "tensor"),
        P(("dp", "replica"), "tensor"),
        P("tensor", "dp"),
        P("tensor", "dp"),
        P(),
    )
    return jax.shard_map(
        body, mesh=mesh, in_specs=placed, out_specs=P("tensor", "dp"), check_vma=False
    )
```

time: 454 us -> 117 us (0.26)
  the two profiles are of different devices: /device:TPU:4 before, /device:TPU:260 now
where the time goes in v1:
time: 117 us
  blocking collectives  44.3 us (38%)
  waiting for transfers between devices  29.7 us (25%)
  starting transfers between devices  26.4 us (23%)
  Pallas kernels  11.6 us (10%)
  local copies, waits for them, and re-layouts  4.32 us (4%)
    all_to_all x1, blocking collectives, body(): terms = lax.all_to_all(windows, 'dp', 0, 0)  44.3 us
    ppermute x1, waiting for transfers between devices, body(): other_tokens = lax.ppermute(tokens, 'replica', swap)  14.9 us
    all_to_all x1, starting transfers between devices, body(): pieces = lax.all_to_all(packed, 'dp', 0, 0)  13.9 us
    all_to_all x1, waiting for transfers between devices, body(): pieces = lax.all_to_all(packed, 'dp', 0, 0)  12.2 us
    pallas_call x6, Pallas kernels, call(): pl.pallas_call(kernel, out_shape=jax.ShapeDtypeStruct(shape, dtype) if is...  11.6 us
    ppermute x1, starting transfers between devices, body(): other_summed = lax.ppermute(summed, 'replica', swap)  5.41 us
    ppermute x1, starting transfers between devices, body(): other_tokens = lax.ppermute(tokens, 'replica', swap)  5.19 us
    unnamed x23, local copies, waits for them, and re-layouts  4.32 us
  transfers between devices with their start and end apart: 4, of which 4 were waited for; matrix products, arithmetic and copies ran while one was open for 0% of the time, Pallas kernels for 1%

profile of v1, /device:TPU:260, one launch (start us, length us, event | category | flops | bytes accessed | tf_op | source)
XLA Modules:
  0.0 117.0 jit_solution(732705320882119761)
XLA Ops:
  0.0 0.1 pad_add_fusion.place_ref
  0.1 0.0 copy-start.2
  0.1 0.9 copy-done.2
  1.0 0.0 copy-start.8
  1.0 0.7 copy-done.8
  1.6 2.1 %pack_shard.1 = bf16[64,88,128]{2,1,0:T(8,128)(2,1)} custom-call(s32[2]{0:T(128)S(1)} %pad_add_fusion.place_ref, s32[64]{0:T(128)S(1)} %copy-done.8, bf16[1,20736]{1,0:T(2,128)(2,1)S(1)} %copy-done.2), custom_call_target="tpu_custom_call" | custom-call | tf_op jit(solution)/shard_map/pack_shard/pallas_call | solution.py:229
  3.7 0.0 copy-start.1
  3.7 0.0 copy-start.4
  3.7 0.0 copy-start.5
  3.7 0.0 copy-start.6
  3.7 13.9 %all-to-all-start = ((bf16[64,88,128]{2,1,0:T(8,128)(2,1)}), bf16[64,88,128]{2,1,0:T(8,128)(2,1)S(1)}, u32[]{:S(2)}, u32[]{:S(2)}) async-start(bf16[64,88,128]{2,1,0:T(8,128)(2,1)} %pack_shard.1), calls=%async_computation | async-start | bytes 2883584 | tf_op jit(solution)/shard_map/all_to_all | solution.py:253
  17.6 0.0 copy-done.1
  17.6 5.2 %collective-permute-start = (bf16[128,3072]{1,0:T(8,128)(2,1)S(1)}, bf16[128,3072]{1,0:T(8,128)(2,1)S(1)}, u32[]{:S(2)}, u32[]{:S(2)}) collective-permute-start(bf16[128,3072]{1,0:T(8,128)(2,1)S(1)} %copy-done.1), channel_id=1, source_target_pairs={{0,1},{1,0},{2,3},{3,2},{4,5},{5,4},{6,7},{7,6},{8,9},{9,8},{10,11... | collective-permute-start | bytes 2359304 | tf_op jit(solution)/shard_map/ppermute | solution.py:255
  22.8 0.0 copy-done.4
  22.8 0.0 copy-done.5
  22.9 0.0 copy-done.6
  22.9 0.0 copy-start.7
  22.9 0.9 copy-done.7
  23.8 0.7 split_heads.1
  24.4 0.0 copy-start.9
  24.5 1.9 %collective-permute-start.1 = (bf16[128,768]{1,0:T(8,128)(2,1)S(1)}, bf16[128,768]{1,0:T(8,128)(2,1)S(1)}, u32[]{:S(2)}, u32[]{:S(2)}) collective-permute-start(bf16[128,768]{1,0:T(8,128)(2,1)S(1)} %get-tuple-element.8), channel_id=1, source_target_pairs={{0,1},{1,0},{2,3},{3,2},{4,5},{5,4},{6,7},{7,6},{8,9},{9,8},{10,11... | collective-permute-start | bytes 589832 | tf_op jit(solution)/shard_map/ppermute | solution.py:260
  26.4 14.9 %collective-permute-done.other_ref.other_tokens_ref = bf16[128,3072]{1,0:T(8,128)(2,1)S(1)} collective-permute-done((bf16[128,3072]{1,0:T(8,128)(2,1)S(1)}, bf16[128,3072]{1,0:T(8,128)(2,1)S(1)}, u32[]{:S(2)}, u32[]{:S(2)}) %collective-permute-start) | collective-permute-done | bytes 786464 | tf_op jit(solution)/shard_map/ppermute | solution.py:255
  41.3 0.5 transpose_tokens.1.turned_ref
  41.7 0.0 copy-start
  41.7 1.1 copy-done
  42.9 1.1 collective-permute-done.1.other_heads_ref
  44.0 12.2 %all-to-all-done.pieces_ref = bf16[64,88,128]{2,1,0:T(8,128)(2,1)S(1)} async-done(((bf16[64,88,128]{2,1,0:T(8,128)(2,1)}), bf16[64,88,128]{2,1,0:T(8,128)(2,1)S(1)}, u32[]{:S(2)}, u32[]{:S(2)}) %all-to-all-start) | async-done | bytes 1441824 | tf_op jit(solution)/shard_map/all_to_all | solution.py:253
  56.2 0.0 copy-done.9
  56.2 7.3 %middle_part.1 = bf16[64,88,128]{2,1,0:T(8,128)(2,1)S(1)} custom-call(s32[2]{0:T(128)S(1)} %pad_add_fusion.place_ref, s32[64]{0:T(128)S(1)} %copy-done.9, bf16[64,88,128]{2,1,0:T(8,128)(2,1)S(1)} %all-to-all-done.pieces_ref, bf16[128,3072]{1,0:T(8,128)(2,1)S(1)} %copy-done.1, bf16[128,3072]{1,0:T(8,128)(2,1)S(1)} %collective-permute-done.other_ref.other_tokens_ref, ...), custom_call_target="tpu_custom_call" | custom-call | tf_op jit(solution)/shard_map/middle_part/pallas_call | solution.py:229
  63.5 44.3 %all_to_all.10.terms_ref = bf16[64,88,128]{2,1,0:T(8,128)(2,1)S(1)} all-to-all(bf16[64,88,128]{2,1,0:T(8,128)(2,1)S(1)} %middle_part.1), channel_id=1, replica_groups=mesh['dp'=64,'tensor'=8,'replica'=2] {'dp'}, dimensions={0} | all-to-all | bytes 2883584 | tf_op jit(solution)/shard_map/all_to_all | solution.py:278
  107.8 0.0 copy-start.3
  107.8 0.0 copy-start.10
  107.8 0.2 add_groups.1.own_ref
  108.0 5.4 %collective-permute-start.2 = (f32[88,128]{1,0:T(8,128)S(1)}, f32[88,128]{1,0:T(8,128)S(1)}, u32[]{:S(2)}, u32[]{:S(2)}) collective-permute-start(f32[88,128]{1,0:T(8,128)S(1)} %add_groups.1.own_ref), channel_id=1, source_target_pairs={{0,1},{1,0},{2,3},{3,2},{4,5},{5,4},{6,7},{7,6},{8,9},{9,8},{10,11... | collective-permute-start | bytes 135176 | tf_op jit(solution)/shard_map/ppermute | solution.py:280
  113.5 0.0 copy-done.3
  113.5 0.2 reduce
  113.7 0.0 copy-done.10
  113.7 0.2 reduce.1
  113.9 1.5 %collective-permute-done.2.other_ref = f32[88,128]{1,0:T(8,128)S(1)} collective-permute-done((f32[88,128]{1,0:T(8,128)S(1)}, f32[88,128]{1,0:T(8,128)S(1)}, u32[]{:S(2)}, u32[]{:S(2)}) %collective-permute-start.2) | collective-permute-done | bytes 45088 | tf_op jit(solution)/shard_map/ppermute | solution.py:280
  115.5 0.8 update_shard.1
  116.3 0.7 copy.11
Async XLA Ops:
  0.1 0.9 copy-start.2
  1.0 0.7 copy-start.8
  3.7 13.9 %copy-start.1 = (bf16[128,3072]{1,0:T(8,128)(2,1)S(1)}, bf16[128,3072]{1,0:T(8,128)(2,1)}, u32[]{:S(2)}) copy-start(bf16[128,3072]{1,0:T(8,128)(2,1)} %own_tokens_ref.1) | copy-start | bytes 2359300
  3.7 19.1 %copy-start.4 = (bf16[128,384]{1,0:T(8,128)(2,1)S(1)}, bf16[128,384]{1,0:T(8,128)(2,1)}, u32[]{:S(2)}) copy-start(bf16[128,384]{1,0:T(8,128)(2,1)} %query_ref.1) | copy-start | bytes 294916
  3.7 19.1 %copy-start.5 = (bf16[128,384]{1,0:T(8,128)(2,1)S(1)}, bf16[128,384]{1,0:T(8,128)(2,1)}, u32[]{:S(2)}) copy-start(bf16[128,384]{1,0:T(8,128)(2,1)} %key_ref.1) | copy-start | bytes 294916
  3.7 19.1 %copy-start.6 = (bf16[128,384]{1,0:T(8,128)(2,1)S(1)}, bf16[128,384]{1,0:T(8,128)(2,1)}, u32[]{:S(2)}) copy-start(bf16[128,384]{1,0:T(8,128)(2,1)} %value_ref.1) | copy-start | bytes 294916
  3.7 52.5 %all-to-all-start = ((bf16[64,88,128]{2,1,0:T(8,128)(2,1)}), bf16[64,88,128]{2,1,0:T(8,128)(2,1)S(1)}, u32[]{:S(2)}, u32[]{:S(2)}) async-start(bf16[64,88,128]{2,1,0:T(8,128)(2,1)} %pack_shard.1), calls=%async_computation | async-start | bytes 2883584 | tf_op jit(solution)/shard_map/all_to_all | solution.py:253
  17.6 23.6 %collective-permute-start = (bf16[128,3072]{1,0:T(8,128)(2,1)S(1)}, bf16[128,3072]{1,0:T(8,128)(2,1)S(1)}, u32[]{:S(2)}, u32[]{:S(2)}) collective-permute-start(bf16[128,3072]{1,0:T(8,128)(2,1)S(1)} %copy-done.1), channel_id=1, source_target_pairs={{0,1},{1,0},{2,3},{3,2},{4,5},{5,4},{6,7},{7,6},{8,9},{9,8},{10,11... | collective-permute-start | bytes 2359304 | tf_op jit(solution)/shard_map/ppermute | solution.py:255
  22.9 0.9 copy-start.7
  24.4 31.7 %copy-start.9 = (s32[64]{0:T(128)S(1)}, s32[64]{0:T(128)}, u32[]{:S(2)}) copy-start(s32[64]{0:T(128)} %counts_ref.5) | copy-start | bytes 772
  24.5 19.6 %collective-permute-start.1 = (bf16[128,768]{1,0:T(8,128)(2,1)S(1)}, bf16[128,768]{1,0:T(8,128)(2,1)S(1)}, u32[]{:S(2)}, u32[]{:S(2)}) collective-permute-start(bf16[128,768]{1,0:T(8,128)(2,1)S(1)} %get-tuple-element.8), channel_id=1, source_target_pairs={{0,1},{1,0},{2,3},{3,2},{4,5},{5,4},{6,7},{7,6},{8,9},{9,8},{10,11... | collective-permute-start | bytes 589832 | tf_op jit(solution)/shard_map/ppermute | solution.py:260
  41.7 1.2 copy-start
  107.8 5.7 %copy-start.3 = (bf16[1,20736]{1,0:T(2,128)(2,1)S(1)}, bf16[1,20736]{1,0:T(2,128)(2,1)}, u32[]{:S(2)}) copy-start(bf16[1,20736]{1,0:T(2,128)(2,1)} %probe_ref.1) | copy-start | bytes 124420
  107.8 5.9 %copy-start.10 = (f32[1,20736]{1,0:T(1,128)S(1)}, f32[1,20736]{1,0:T(1,128)}, u32[]{:S(2)}) copy-start(f32[1,20736]{1,0:T(1,128)} %param.14) | copy-start | bytes 248836
  108.0 7.4 %collective-permute-start.2 = (f32[88,128]{1,0:T(8,128)S(1)}, f32[88,128]{1,0:T(8,128)S(1)}, u32[]{:S(2)}, u32[]{:S(2)}) collective-permute-start(f32[88,128]{1,0:T(8,128)S(1)} %add_groups.1.own_ref), channel_id=1, source_target_pairs={{0,1},{1,0},{2,3},{3,2},{4,5},{5,4},{6,7},{7,6},{8,9},{9,8},{10,11... | collective-permute-start | bytes 135176 | tf_op jit(solution)/shard_map/ppermute | solution.py:280

commit v2 on v0

v2 whole, which is shorter than its diff:
```python
import math

import jax
import jax.numpy as jnp
from jax import lax
from jax.experimental import pallas as pl
from jax.experimental.pallas import tpu as pltpu
from jax.sharding import PartitionSpec as P

HEAD = 96
LANES = 128
decay_rate = 0.99

ROW = 8

HEADS = 4

BLOCKS = 3
WIDE = ((0, 0), (1, 0), (1, 64), (2, 64))
SLIM = ((0, 64), (0, 96), (2, 0), (2, 32))
SPAN = 64
PAIRS = SPAN // 2
QUADS = SPAN // 4
WINDOW = PAIRS + QUADS
USED = 56
HALF = LANES // 2
QUARTER = LANES // 4

VMEM = pl.BlockSpec(memory_space=pltpu.VMEM)
SMEM = pl.BlockSpec(memory_space=pltpu.SMEM)


def params():
    return pltpu.CompilerParams(vmem_limit_bytes=56 * 1024 * 1024)


def lane_of(rows):
    return lax.broadcasted_iota(jnp.int32, (rows, LANES), 1)


def turn(values, lanes):
    lanes = lanes % LANES
    return values if lanes == 0 else pltpu.roll(values, lanes, 1)


def first_block(counts_ref, shard):
    return lax.fori_loop(0, shard, lambda at, total: total + counts_ref[at] // LANES, jnp.int32(0))


def by_quarter(parts):
    lane = lane_of(parts[0].shape[0])
    low = jnp.where(lane < QUARTER, parts[0], parts[1])
    high = jnp.where(lane < 3 * QUARTER, parts[2], parts[3])
    return jnp.where(lane < HALF, low, high)


def pack_shard(place_ref, counts_ref, probe_ref, out_ref, rows):
    copy = place_ref[0]
    shift = lax.rem(first_block(counts_ref, place_ref[1]), BLOCKS)
    rows[...] = jnp.zeros_like(rows)
    for block in range(probe_ref.shape[1] // LANES):
        rows[pl.ds(shift + block, 1), :] = probe_ref[0:1, block * LANES : (block + 1) * LANES].astype(jnp.float32)

    def window(head):
        block, lane = WIDE[head]
        wide = rows[pl.ds(block, SPAN, stride=BLOCKS), :]
        pairs = jnp.where(lane_of(PAIRS) < HALF, turn(wide[:PAIRS], -lane), turn(wide[PAIRS:], HALF - lane))
        block, lane = SLIM[head]
        slim = rows[pl.ds(block, SPAN, stride=BLOCKS), :]
        quads = by_quarter(
            [turn(slim[at * QUADS : (at + 1) * QUADS], at * QUARTER - lane) for at in range(4)]
        )
        return jnp.concatenate([pairs, quads], axis=0).astype(jnp.bfloat16)

    for which in range(2):

        @pl.when(copy == which)
        def _():
            even, odd = window(2 * which), window(2 * which + 1)

            def store(at, carry):
                first = at // ROW * 2 * ROW + lax.rem(at, ROW)
                out_ref[first] = even
                out_ref[first + ROW] = odd
                return carry

            lax.fori_loop(0, out_ref.shape[0] // 2, store, 0, unroll=4)


def split_heads(place_ref, tokens_ref, query_ref, key_ref, value_ref, cot_ref, keep_ref, x_ref, copy_ref):
    copy, parity, core = place_ref[0], place_ref[2], place_ref[3]
    length, features = tokens_ref.shape
    half = length // 2
    packed = 2 * HEADS * HEAD
    tokens = tokens_ref[pl.ds(pl.multiple_of(core * half, half), half), :]
    x_ref[:, packed : packed + features] = tokens
    copy_ref[:, :features] = tokens
    arrays = (query_ref, key_ref, value_ref, cot_ref)

    def put(head, target_ref, start):
        for side in range(2):
            for at, ref in enumerate(arrays):
                to = start + (side * HEADS + at) * HEAD
                target_ref[:, to : to + HEAD] = ref[side * half : (side + 1) * half, head * HEAD : (head + 1) * HEAD]

    for mine in range(HEADS):

        @pl.when(2 * copy + parity == mine)
        def _():
            for at, ref in enumerate(arrays):
                keep_ref[:, at * HEAD : (at + 1) * HEAD] = ref[:, mine * HEAD : (mine + 1) * HEAD]
            put(mine ^ 1, x_ref, 0)
            put(mine ^ 3, x_ref, packed + features)
            put(mine ^ 2, copy_ref, features)


def attention_part(heads):
    length = heads.shape[0]
    query, key_head, value_head, cot_head = (heads[:, at * HEAD : (at + 1) * HEAD] for at in range(HEADS))
    inv_root = 1.0 / math.sqrt(HEAD)
    causal = lax.broadcasted_iota(jnp.int32, (length, length), 0) >= lax.broadcasted_iota(
        jnp.int32, (length, length), 1
    )
    scores = inv_root * times_transposed(query, key_head)
    scores = jnp.where(causal, scores, jnp.float32(-1e30))
    expo_terms = jnp.exp(scores - jnp.max(scores, axis=1, keepdims=True))
    attn = expo_terms / jnp.sum(expo_terms, axis=1, keepdims=True)
    back = times_transposed(cot_head, value_head)
    return key_head, attn, back, back - jnp.sum(attn * back, axis=1, keepdims=True)


def times_transposed(left, right):
    return lax.dot_general(left, right, (((1,), (1,)), ((), ())), preferred_element_type=jnp.float32)


def gather_sequences(features, place_ref, whole, halves, out_refs):
    core = place_ref[3]
    tokens_ref, turned_ref, key_ref, attn_ref, back_ref, centred_ref = out_refs
    length = attn_ref.shape[1]
    half = length // 2
    packed = 2 * HEADS * HEAD
    at = 0
    heads_of = []
    for one_ref, heads_ref in whole:
        tokens_ref[at * length : (at + 1) * length, :] = one_ref[...]
        heads_of.append(heads_ref[...])
        at += 1
    for mine_ref, mine_at, heads_at, other_ref, other_row in halves:
        tokens_ref[pl.ds(pl.multiple_of(at * length + core * half, half), half), :] = mine_ref[
            :, mine_at : mine_at + features
        ]
        tokens_ref[pl.ds(pl.multiple_of(at * length + (1 - core) * half, half), half), :] = other_ref[
            other_row : other_row + half, :
        ]
        heads_of.append(
            jnp.concatenate(
                [
                    mine_ref[:, heads_at : heads_at + packed // 2],
                    mine_ref[:, heads_at + packed // 2 : heads_at + packed],
                ],
                axis=0,
            )
        )
        at += 1
    for at, heads in enumerate(heads_of):
        rows = slice(at * length, (at + 1) * length)
        turned_ref[:, rows] = tokens_ref[rows, :].T
        key_ref[at], attn_ref[at], back_ref[at], centred_ref[at] = attention_part(heads)


def gather_three(place_ref, tokens_ref, keep_ref, x_ref, copy_ref, swapped_ref, *out_refs):
    features = tokens_ref.shape[1]
    packed = 2 * HEADS * HEAD
    gather_sequences(
        features,
        place_ref,
        [(tokens_ref, keep_ref)],
        [
            (x_ref, packed, 0, swapped_ref, 0),
            (copy_ref, 0, features, swapped_ref, x_ref.shape[0]),
        ],
        out_refs,
    )


def gather_last(place_ref, relay_ref, swapped_ref, *out_refs):
    features = swapped_ref.shape[1]
    gather_sequences(features, place_ref, [], [(relay_ref, 0, features, swapped_ref, 0)], out_refs)


def middle_part(place_ref, counts_ref, pieces_ref, *refs):
    three, last = refs[:6], refs[6:12]
    out_ref, wide, slim, probe, tangent, spread = refs[12:]
    copy, parity = place_ref[0], place_ref[2]
    length = three[3].shape[1]
    features = probe.shape[0]
    shards = pieces_ref.shape[0]
    inv_root = 1.0 / math.sqrt(HEAD)
    pair_lane, quad_lane = lane_of(PAIRS), lane_of(QUADS)
    top_row = lax.broadcasted_iota(jnp.int32, (8, LANES), 0) == 0
    wide_block = (2 * copy + parity + 1) // 2
    slim_block = 2 * copy

    def place(shard, start):
        first = start // BLOCKS
        shift = start - first * BLOCKS
        piece = pieces_ref[shard].astype(jnp.float32)
        pairs, quads = piece[:PAIRS], piece[PAIRS:]
        wide_values = [jnp.where(pair_lane < HALF, pairs, 0.0), jnp.where(pair_lane < HALF, 0.0, pairs)]
        slim_values = [jnp.where(quad_lane // QUARTER == at, quads, 0.0) for at in range(4)]
        for slab, block, values in ((wide, wide_block, wide_values), (slim, slim_block, slim_values)):
            values = jnp.concatenate(values, axis=0)
            before = slab[pl.ds(first, 8), :]
            slab[pl.ds(first, 8), :] = jnp.where(top_row & (block < shift), before, values[:8])
            slab[pl.ds(first + 8, USED - 8), :] = values[8:USED]
        return start + counts_ref[shard] // LANES

    lax.fori_loop(0, shards, place, jnp.int32(0), unroll=4)
    probe[:, :LANES] = wide[:features, :].astype(jnp.bfloat16)
    probe[:, LANES:] = slim[:features, :].astype(jnp.bfloat16)

    row = 0
    for tokens_ref, *_ in (three, last):
        count = tokens_ref.shape[0]
        product = jnp.dot(tokens_ref[...], probe[...], preferred_element_type=jnp.float32)
        wide_sum, slim_sum = product[:, :LANES], product[:, LANES:]
        wide_sum = wide_sum + turn(wide_sum, HALF)
        slim_sum = slim_sum + turn(slim_sum, HALF)
        slim_sum = slim_sum + turn(slim_sum, QUARTER)
        lane = lane_of(count)
        ordered = jnp.where(
            parity == 0,
            jnp.where(lane < HALF, wide_sum, slim_sum),
            jnp.where(lane < QUARTER, slim_sum, turn(wide_sum, QUARTER)),
        )
        tangent[row : row + count, :] = ordered[:, :HEAD].astype(jnp.bfloat16)
        row += count

    row = 0
    for _, _, key_ref, attn_ref, back_ref, centred_ref in (three, last):
        for at in range(key_ref.shape[0]):
            rows = slice(row, row + length)
            key_head, attn, back = key_ref[at], attn_ref[at], back_ref[at]
            score_tangent = inv_root * times_transposed(tangent[rows, :], key_head)
            mean_tangent = jnp.sum(attn * score_tangent, axis=1, keepdims=True)
            weight_tangent = attn * (score_tangent - mean_tangent)
            delta_tangent = jnp.sum(weight_tangent * back, axis=1, keepdims=True)
            grad_tangent = (weight_tangent * centred_ref[at] - attn * delta_tangent).astype(jnp.bfloat16)
            scaled = inv_root * jnp.dot(grad_tangent, key_head, preferred_element_type=jnp.float32)
            scaled = scaled.astype(jnp.bfloat16)

            def lay(wide_part, slim_part):
                for side in range(2):
                    spread[rows, side * HALF : (side + 1) * HALF] = wide_part
                for side in range(4):
                    spread[rows, LANES + side * QUARTER : LANES + (side + 1) * QUARTER] = slim_part

            @pl.when(parity == 0)
            def _():
                lay(scaled[:, :HALF], scaled[:, HALF:])

            @pl.when(parity == 1)
            def _():
                lay(scaled[:, QUARTER:], scaled[:, :QUARTER])

            row += length

    split = three[0].shape[0]
    term = jnp.dot(three[1][...], spread[:split, :], preferred_element_type=jnp.float32)
    term += jnp.dot(last[1][...], spread[split:, :], preferred_element_type=jnp.float32)
    wide[:features, :] = term[:, :LANES]
    slim[:features, :] = term[:, LANES:]

    def cut_out(shard, start):
        first = start // BLOCKS
        pairs = jnp.where(pair_lane < HALF, wide[pl.ds(first, PAIRS), :], wide[pl.ds(first + PAIRS, PAIRS), :])
        quads = by_quarter([slim[pl.ds(first + at * QUADS, QUADS), :] for at in range(4)])
        out_ref[shard] = jnp.concatenate([pairs, quads], axis=0).astype(jnp.bfloat16)
        return start + counts_ref[shard] // LANES

    lax.fori_loop(0, shards, cut_out, jnp.int32(0), unroll=4)


def add_groups(terms_ref, out_ref):
    for parity in range(2):

        def add(at, total):
            return total + terms_ref[at // ROW * 2 * ROW + lax.rem(at, ROW) + parity * ROW].astype(jnp.float32)

        out_ref[parity * WINDOW : (parity + 1) * WINDOW, :] = lax.fori_loop(
            0, terms_ref.shape[0] // 2, add, jnp.zeros((WINDOW, LANES), jnp.float32), unroll=4
        )


def update_shard(place_ref, counts_ref, sums_ref, probe_ref, hess_ref, out_ref, rows):
    shard = place_ref[1]
    shift = lax.rem(first_block(counts_ref, shard), BLOCKS)
    blocks = probe_ref.shape[0]

    def wide_part(head):
        pairs = sums_ref[head // 2, head % 2 * WINDOW : head % 2 * WINDOW + PAIRS, :]
        lane = WIDE[head][1]
        return jnp.concatenate([turn(pairs, lane - at * HALF) for at in range(2)], axis=0)

    def slim_part(head):
        quads = sums_ref[head // 2, head % 2 * WINDOW + PAIRS : (head % 2 + 1) * WINDOW, :]
        lane = SLIM[head][1]
        return jnp.concatenate([turn(quads, lane - at * QUARTER) for at in range(4)], axis=0)

    lane = lane_of(SPAN)
    rows[pl.ds(0, SPAN, stride=BLOCKS), :] = jnp.where(
        lane < HALF, wide_part(0), jnp.where(lane < 3 * QUARTER, slim_part(0), slim_part(1))
    )
    rows[pl.ds(1, SPAN, stride=BLOCKS), :] = jnp.where(lane < HALF, wide_part(1), wide_part(2))
    rows[pl.ds(2, SPAN, stride=BLOCKS), :] = jnp.where(
        lane < HALF, jnp.where(lane < QUARTER, slim_part(2), slim_part(3)), wide_part(3)
    )
    inner = lax.broadcasted_iota(jnp.int32, (blocks, LANES), 0)
    product = jnp.where(inner < counts_ref[shard] // LANES, rows[pl.ds(shift, blocks), :], 0.0)
    out_ref[...] = decay_rate * hess_ref[...] + (1.0 - decay_rate) * probe_ref[...].astype(jnp.float32) * product


def call(kernel, outs, operands, scalars, scratch=()):
    shapes = [jax.ShapeDtypeStruct(shape, dtype) for shape, dtype in outs]
    result = pl.pallas_call(
        kernel,
        out_shape=shapes,
        in_specs=[SMEM] * scalars + [VMEM] * (len(operands) - scalars),
        out_specs=[VMEM] * len(shapes),
        scratch_shapes=list(scratch),
        compiler_params=params(),
        name=kernel.__name__,
    )(*operands)
    return result if len(shapes) > 1 else result[0]


def body(tokens, queries, key_rows, value_rows, cotangent, probe_shards, hess_old, shard_counts):
    length, features = tokens.shape
    half = length // 2
    packed = 2 * HEADS * HEAD
    shards = shard_counts.shape[0]
    blocks = probe_shards.shape[1] // LANES
    bf16, f32 = jnp.bfloat16, jnp.float32
    slab = pltpu.VMEM((features + SPAN, LANES), f32)
    rows = pltpu.VMEM((BLOCKS * SPAN + 8, LANES), f32)
    at = lax.axis_index("dp")
    place = jnp.stack(
        [lax.axis_index("replica"), at, at // ROW % 2, lax.axis_index("tensor") % 2]
    ).astype(jnp.int32)

    def swap_copies(array):
        return lax.ppermute(array, "replica", [(0, 1), (1, 0)])

    def swap_cores(array):
        return lax.ppermute(array, "tensor", [(one, one ^ 1) for one in range(lax.axis_size("tensor"))])

    keep, to_x, to_copy = call(
        split_heads,
        [
            ((length, HEADS * HEAD), bf16),
            ((half, packed + features + packed), bf16),
            ((half, features + packed), bf16),
        ],
        (place, tokens, queries, key_rows, value_rows, cotangent),
        1,
    )
    from_x = lax.ppermute(to_x, "dp", [(one, one ^ ROW) for one in range(shards)])
    from_copy = swap_copies(to_copy)

    windows = call(
        pack_shard, [((shards, WINDOW, LANES), bf16)], (place, shard_counts, probe_shards), 2, (rows,)
    )
    pieces = lax.all_to_all(windows, "dp", 0, 0)

    relayed = swap_copies(from_x[:, packed:])
    swapped = swap_cores(
        jnp.concatenate([from_x[:, packed : packed + features], from_copy[:, :features]], axis=0)
    )
    swapped_last = swap_cores(relayed[:, :features])

    def gathered(count):
        square = ((count, length, length), f32)
        return [
            ((count * length, features), bf16),
            ((features, count * length), bf16),
            ((count, length, HEAD), bf16),
            square,
            square,
            square,
        ]

    three = call(gather_three, gathered(3), (place, tokens, keep, from_x, from_copy, swapped), 1)
    last = call(gather_last, gathered(1), (place, relayed, swapped_last), 1)

    term_windows = call(
        middle_part,
        [((shards, WINDOW, LANES), bf16)],
        (place, shard_counts, pieces, *three, *last),
        2,
        (
            slab,
            slab,
            pltpu.VMEM((features, 2 * LANES), bf16),
            pltpu.VMEM((4 * length, HEAD), bf16),
            pltpu.VMEM((4 * length, 2 * LANES), bf16),
        ),
    )
    terms = lax.all_to_all(term_windows, "dp", 0, 0)
    summed = call(add_groups, [((2 * WINDOW, LANES), f32)], (terms,), 0)
    sums = lax.all_gather(summed, "replica", axis=0)
    updated = call(
        update_shard,
        [((blocks, LANES), f32)],
        (place, shard_counts, sums, probe_shards.reshape(blocks, LANES), hess_old.reshape(blocks, LANES)),
        2,
        (rows,),
    )
    return updated.reshape(1, blocks * LANES)


def solution(mesh):
    placed = (
        P(("dp", "replica"), None),
        P(("dp", "replica"), "tensor"),
        P(("dp", "replica"), "tensor"),
        P(("dp", "replica"), "tensor"),
        P(("dp", "replica"), "tensor"),
        P("tensor", "dp"),
        P("tensor", "dp"),
        P(),
    )
    return jax.shard_map(
        body, mesh=mesh, in_specs=placed, out_specs=P("tensor", "dp"), check_vma=False
    )
```

time: 454 us -> 115 us (0.25)
  the two profiles are of different devices: /device:TPU:4 before, /device:TPU:260 now
where the time goes in v2:
time: 115 us; the launch traced here: 114 us
  starting transfers between devices  40.1 us (35%)
  waiting for transfers between devices  33.7 us (29%)
  Pallas kernels  27.9 us (24%)
  local copies, waits for them, and re-layouts  5.14 us (4%)
  blocking collectives  5.07 us (4%)
  other arithmetic  2.31 us (2%)
    pallas_call x7, Pallas kernels, call(): pl.pallas_call(kernel, out_shape=shapes, in_specs=[SMEM] * scalars + [VME...  27.9 us
    all_to_all x1, waiting for transfers between devices, body(): terms = lax.all_to_all(term_windows, 'dp', 0, 0)  23.9 us
    all_to_all x1, starting transfers between devices, body(): pieces = lax.all_to_all(windows, 'dp', 0, 0)  12.9 us
    all_to_all x1, starting transfers between devices, body(): terms = lax.all_to_all(term_windows, 'dp', 0, 0)  12.8 us
    ppermute x2, waiting for transfers between devices, swap_copies(): return lax.ppermute(array, 'replica', [(0, 1), (1, 0)])  9.76 us
    ppermute x2, starting transfers between devices, swap_copies(): return lax.ppermute(array, 'replica', [(0, 1), (1, 0)])  7.11 us
    all_gather x1, blocking collectives, body(): sums = lax.all_gather(summed, 'replica', axis=0)  5.07 us
    unnamed x19, local copies, waits for them, and re-layouts  5.02 us
  transfers between devices with their start and end apart: 7, of which 2 were waited for; matrix products, arithmetic and copies ran while one was open for 2% of the time, Pallas kernels for 9%

profile of v2, /device:TPU:260, one launch (start us, length us, event | category | flops | bytes accessed | tf_op | source)
XLA Modules:
  0.0 114.4 jit_solution(1526600303397546564)
XLA Ops:
  0.0 0.6 pad_add_fusion.place_ref
  0.6 2.6 %split_heads.1 = (bf16[128,384]{1,0:T(8,128)(2,1)}, bf16[64,4608]{1,0:T(8,128)(2,1)}, bf16[64,3840]{1,0:T(8,128)(2,1)}) custom-call(s32[4]{0:T(128)} %pad_add_fusion.place_ref, bf16[128,3072]{1,0:T(8,128)(2,1)} %tokens_ref.3, bf16[128,384]{1,0:T(8,128)(2,1)} %query_ref.1, bf16[128,384]{1,0:T(8,128)(2,1)} %key_ref.1, bf16[128,384]{1,0:T(8,128)(2,1)} %value_ref.1, ...), custom_call_target="tpu_custom_call" | custom-call | tf_op jit(solution)/shard_map/split_heads/pallas_call | solution.py:325
  3.2 3.4 %collective-permute-start = (bf16[64,4608]{1,0:T(8,128)(2,1)}, bf16[64,4608]{1,0:T(8,128)(2,1)S(1)}, u32[]{:S(2)}, u32[]{:S(2)}) collective-permute-start(bf16[64,4608]{1,0:T(8,128)(2,1)} %get-tuple-element.21), channel_id=1, source_target_pairs={{0,128},{16,144},{32,160},{48,176},{64,192},{80,208},{96,224},{112... | collective-permute-start | bytes 1769480 | tf_op jit(solution)/shard_map/ppermute | solution.py:367
  6.6 5.2 %collective-permute-start.1 = (bf16[64,3840]{1,0:T(8,128)(2,1)}, bf16[64,3840]{1,0:T(8,128)(2,1)S(1)}, u32[]{:S(2)}, u32[]{:S(2)}) collective-permute-start(bf16[64,3840]{1,0:T(8,128)(2,1)} %get-tuple-element.22), channel_id=1, source_target_pairs={{0,1},{1,0},{2,3},{3,2},{4,5},{5,4},{6,7},{7,6},{8,9},{9,8},{10,11... | collective-permute-start | bytes 1474568 | tf_op jit(solution)/shard_map/ppermute | solution.py:352
  11.8 2.3 %pack_shard.1 = bf16[64,48,128]{2,1,0:T(8,128)(2,1)} custom-call(s32[4]{0:T(128)} %pad_add_fusion.place_ref, s32[64]{0:T(128)} %counts_ref.5, bf16[1,20736]{1,0:T(2,128)(2,1)} %probe_ref.1), custom_call_target="tpu_custom_call" | custom-call | tf_op jit(solution)/shard_map/pack_shard/pallas_call | solution.py:325
  14.1 12.9 %all-to-all-start = ((bf16[64,48,128]{2,1,0:T(8,128)(2,1)}), bf16[64,48,128]{2,1,0:T(8,128)(2,1)S(1)}, u32[]{:S(2)}, u32[]{:S(2)}) async-start(bf16[64,48,128]{2,1,0:T(8,128)(2,1)} %pack_shard.1), calls=%async_computation | async-start | bytes 1572864 | tf_op jit(solution)/shard_map/all_to_all | solution.py:373
  27.0 0.0 collective-permute-done.1.copy_ref
  27.0 0.0 copy-start.3
  27.1 0.0 collective-permute-done.x_ref
  27.1 0.0 copy-start
  27.2 1.9 %collective-permute-start.3 = (bf16[64,3840]{1,0:T(8,128)(2,1)S(1)}, bf16[64,3840]{1,0:T(8,128)(2,1)S(1)}, u32[]{:S(2)}, u32[]{:S(2)}) collective-permute-start(bf16[64,3840]{1,0:T(8,128)(2,1)S(1)} %slice.18), channel_id=1, source_target_pairs={{0,1},{1,0},{2,3},{3,2},{4,5},{5,4},{6,7},{7,6},{8,9},{9,8},{10,11... | collective-permute-start | bytes 1474568 | tf_op jit(solution)/shard_map/ppermute | solution.py:352
  29.1 0.1 pad_maximum_fusion
  29.2 0.0 copy-done.3
  29.2 0.0 copy-done
  29.2 1.9 %collective-permute-start.2 = (bf16[128,3072]{1,0:T(8,128)(2,1)S(1)}, bf16[128,3072]{1,0:T(8,128)(2,1)S(1)}, u32[]{:S(2)}, u32[]{:S(2)}) collective-permute-start(bf16[128,3072]{1,0:T(8,128)(2,1)S(1)} %pad_maximum_fusion), channel_id=1, source_target_pairs={{0,2},{2,0},{4,6},{6,4},{8,10},{10,8},{12,14},{14,12},{1,3},{3,1},... | collective-permute-start | bytes 2359304 | tf_op jit(solution)/shard_map/ppermute | solution.py:355
  31.1 9.8 %collective-permute-done.3.relay_ref = bf16[64,3840]{1,0:T(8,128)(2,1)S(1)} collective-permute-done((bf16[64,3840]{1,0:T(8,128)(2,1)S(1)}, bf16[64,3840]{1,0:T(8,128)(2,1)S(1)}, u32[]{:S(2)}, u32[]{:S(2)}) %collective-permute-start.3) | collective-permute-done | bytes 491552 | tf_op jit(solution)/shard_map/ppermute | solution.py:352
  40.9 0.0 copy-start.4
  40.9 1.9 %collective-permute-start.4 = (bf16[64,3072]{1,0:T(8,128)(2,1)S(1)}, bf16[64,3072]{1,0:T(8,128)(2,1)S(1)}, u32[]{:S(2)}, u32[]{:S(2)}) collective-permute-start(bf16[64,3072]{1,0:T(8,128)(2,1)S(1)} %slice.19), channel_id=1, source_target_pairs={{0,2},{2,0},{4,6},{6,4},{8,10},{10,8},{12,14},{14,12},{1,3},{3,1},... | collective-permute-start | bytes 1179656 | tf_op jit(solution)/shard_map/ppermute | solution.py:355
  42.9 0.0 collective-permute-done.2.swapped_ref
  42.9 0.0 copy-start.5
  42.9 0.9 copy-done.5
  43.7 4.9 %gather_three.1 = (bf16[384,3072]{1,0:T(8,128)(2,1)}, bf16[3072,384]{1,0:T(8,128)(2,1)}, bf16[3,128,96]{2,1,0:T(8,128)(2,1)}, f32[3,128,128]{2,1,0:T(8,128)}, f3...) custom-call(s32[4]{0:T(128)} %pad_add_fusion.place_ref, bf16[128,3072]{1,0:T(8,128)(2,1)} %tokens_ref.3, ...), custom_call_target="tpu_custom_call" | custom-call | tf_op jit(solution)/shard_map/gather_three/pallas_call | solution.py:325
  48.6 0.0 copy-done.4
  48.6 0.0 collective-permute-done.4.swapped_ref
  48.7 0.0 copy-start.6
  48.7 0.7 copy-done.6
  49.4 2.7 %gather_last.1 = (bf16[128,3072]{1,0:T(8,128)(2,1)}, bf16[3072,128]{1,0:T(8,128)(2,1)}, bf16[1,128,96]{2,1,0:T(8,128)(2,1)}, f32[1,128,128]{2,1,0:T(8,128)}, f32...) custom-call(s32[4]{0:T(128)} %pad_add_fusion.place_ref, bf16[64,3840]{1,0:T(8,128)(2,1)} %copy-done.4, bf16[64,3072]{1,0:T(8,128)(2,1)} %copy-done.6), custom_call_target="tpu_custom_call" | custom-call | tf_op jit(solution)/shard_map/gather_last/pallas_call | solution.py:325
  52.1 0.0 all-to-all-done.pieces_ref
  52.1 0.0 copy-start.1
  52.1 0.9 copy-done.1
  52.9 11.3 %middle_part.1 = bf16[64,48,128]{2,1,0:T(8,128)(2,1)} custom-call(s32[4]{0:T(128)} %pad_add_fusion.place_ref, s32[64]{0:T(128)} %counts_ref.5, bf16[64,48,128]{2,1,0:T(8,128)(2,1)} %copy-done.1, bf16[384,3072]{1,0:T(8,128)(2,1)} %get-tuple-element.23.refs_0_, bf16[3072,384]{1,0:T(8,128)(2,1)} %get-tuple-element.24.refs_1_, ...), custom_call_target="tpu_custom_call" | custom-call | tf_op jit(solution)/shard_map/middle_part/pallas_call | solution.py:325
  64.2 0.0 copy-start.7
  64.2 0.0 copy-start.8
  64.3 12.8 %all-to-all-start.1 = ((bf16[64,48,128]{2,1,0:T(8,128)(2,1)}), bf16[64,48,128]{2,1,0:T(8,128)(2,1)S(1)}, u32[]{:S(2)}, u32[]{:S(2)}) async-start(bf16[64,48,128]{2,1,0:T(8,128)(2,1)} %middle_part.1), calls=%async_computation.1 | async-start | bytes 1572864 | tf_op jit(solution)/shard_map/all_to_all | solution.py:408
  77.1 0.0 copy-done.7
  77.1 0.8 reduce
  78.0 0.0 copy-done.8
  78.0 0.8 reduce.1
  78.8 23.9 %all-to-all-done.1.terms_ref = bf16[64,48,128]{2,1,0:T(8,128)(2,1)S(1)} async-done(((bf16[64,48,128]{2,1,0:T(8,128)(2,1)}), bf16[64,48,128]{2,1,0:T(8,128)(2,1)S(1)}, u32[]{:S(2)}, u32[]{:S(2)}) %all-to-all-start.1) | async-done | bytes 786464 | tf_op jit(solution)/shard_map/all_to_all | solution.py:408
  102.7 0.0 copy-start.2
  102.7 0.9 copy-done.2
  103.6 2.2 %add_groups.1 = f32[96,128]{1,0:T(8,128)} custom-call(bf16[64,48,128]{2,1,0:T(8,128)(2,1)} %copy-done.2), custom_call_target="tpu_custom_call" | custom-call | tf_op jit(solution)/shard_map/add_groups/pallas_call | solution.py:325
  105.8 5.1 %all-gather = f32[192,128]{1,0:T(8,128)} all-gather(f32[96,128]{1,0:T(8,128)} %add_groups.1), channel_id=2, replica_groups=mesh['dp'=64,'tensor'=8,'replica'=2] {'replica'}, dimensions={0}, use_global_device_ids=true | all-gather | bytes 147456 | tf_op jit(solution)/shard_map/all_gather | solution.py:410
  110.9 1.9 %update_shard.1 = f32[162,128]{1,0:T(8,128)} custom-call(s32[4]{0:T(128)} %pad_add_fusion.place_ref, s32[64]{0:T(128)} %counts_ref.5, f32[2,96,128]{2,1,0:T(8,128)} %bitcast.12, bf16[162,128]{1,0:T(8,128)(2,1)} %bitcast.15, f32[162,128]{1,0:T(8,128)} %bitcast.13), custom_call_target="tpu_custom_call" | custom-call | tf_op jit(solution)/shard_map/update_shard/pallas_call | solution.py:325
  112.8 1.6 %copy.11 = f32[1,1,162,128]{3,1,2,0:T(1,128)} copy(f32[1,1,162,128]{3,2,1,0:T(8,128)} %bitcast.14) | data formatting | bytes 165888
  (4 shorter events, 0.1 us)
Async XLA Ops:
  3.2 23.9 %collective-permute-start = (bf16[64,4608]{1,0:T(8,128)(2,1)}, bf16[64,4608]{1,0:T(8,128)(2,1)S(1)}, u32[]{:S(2)}, u32[]{:S(2)}) collective-permute-start(bf16[64,4608]{1,0:T(8,128)(2,1)} %get-tuple-element.21), channel_id=1, source_target_pairs={{0,128},{16,144},{32,160},{48,176},{64,192},{80,208},{96,224},{112... | collective-permute-start | bytes 1769480 | tf_op jit(solution)/shard_map/ppermute | solution.py:367
  6.6 20.5 %collective-permute-start.1 = (bf16[64,3840]{1,0:T(8,128)(2,1)}, bf16[64,3840]{1,0:T(8,128)(2,1)S(1)}, u32[]{:S(2)}, u32[]{:S(2)}) collective-permute-start(bf16[64,3840]{1,0:T(8,128)(2,1)} %get-tuple-element.22), channel_id=1, source_target_pairs={{0,1},{1,0},{2,3},{3,2},{4,5},{5,4},{6,7},{7,6},{8,9},{9,8},{10,11... | collective-permute-start | bytes 1474568 | tf_op jit(solution)/shard_map/ppermute | solution.py:352
  14.1 37.9 %all-to-all-start = ((bf16[64,48,128]{2,1,0:T(8,128)(2,1)}), bf16[64,48,128]{2,1,0:T(8,128)(2,1)S(1)}, u32[]{:S(2)}, u32[]{:S(2)}) async-start(bf16[64,48,128]{2,1,0:T(8,128)(2,1)} %pack_shard.1), calls=%async_computation | async-start | bytes 1572864 | tf_op jit(solution)/shard_map/all_to_all | solution.py:373
  27.0 2.1 %copy-start.3 = (bf16[64,3840]{1,0:T(8,128)(2,1)}, bf16[64,3840]{1,0:T(8,128)(2,1)S(1)}, u32[]{:S(2)}) copy-start(bf16[64,3840]{1,0:T(8,128)(2,1)S(1)} %collective-permute-done.1.copy_ref) | copy-start | bytes 1474564
  27.1 2.1 %copy-start = (bf16[64,4608]{1,0:T(8,128)(2,1)}, bf16[64,4608]{1,0:T(8,128)(2,1)S(1)}, u32[]{:S(2)}) copy-start(bf16[64,4608]{1,0:T(8,128)(2,1)S(1)} %collective-permute-done.x_ref) | copy-start | bytes 1769476
  27.2 13.7 %collective-permute-start.3 = (bf16[64,3840]{1,0:T(8,128)(2,1)S(1)}, bf16[64,3840]{1,0:T(8,128)(2,1)S(1)}, u32[]{:S(2)}, u32[]{:S(2)}) collective-permute-start(bf16[64,3840]{1,0:T(8,128)(2,1)S(1)} %slice.18), channel_id=1, source_target_pairs={{0,1},{1,0},{2,3},{3,2},{4,5},{5,4},{6,7},{7,6},{8,9},{9,8},{10,11... | collective-permute-start | bytes 1474568 | tf_op jit(solution)/shard_map/ppermute | solution.py:352
  29.2 13.7 %collective-permute-start.2 = (bf16[128,3072]{1,0:T(8,128)(2,1)S(1)}, bf16[128,3072]{1,0:T(8,128)(2,1)S(1)}, u32[]{:S(2)}, u32[]{:S(2)}) collective-permute-start(bf16[128,3072]{1,0:T(8,128)(2,1)S(1)} %pad_maximum_fusion), channel_id=1, source_target_pairs={{0,2},{2,0},{4,6},{6,4},{8,10},{10,8},{12,14},{14,12},{1,3},{3,1},... | collective-permute-start | bytes 2359304 | tf_op jit(solution)/shard_map/ppermute | solution.py:355
  40.9 7.7 %copy-start.4 = (bf16[64,3840]{1,0:T(8,128)(2,1)}, bf16[64,3840]{1,0:T(8,128)(2,1)S(1)}, u32[]{:S(2)}) copy-start(bf16[64,3840]{1,0:T(8,128)(2,1)S(1)} %collective-permute-done.3.relay_ref) | copy-start | bytes 1474564
  40.9 7.7 %collective-permute-start.4 = (bf16[64,3072]{1,0:T(8,128)(2,1)S(1)}, bf16[64,3072]{1,0:T(8,128)(2,1)S(1)}, u32[]{:S(2)}, u32[]{:S(2)}) collective-permute-start(bf16[64,3072]{1,0:T(8,128)(2,1)S(1)} %slice.19), channel_id=1, source_target_pairs={{0,2},{2,0},{4,6},{6,4},{8,10},{10,8},{12,14},{14,12},{1,3},{3,1},... | collective-permute-start | bytes 1179656 | tf_op jit(solution)/shard_map/ppermute | solution.py:355
  42.9 0.9 copy-start.5
  48.7 0.8 copy-start.6
  52.1 0.9 copy-start.1
  64.2 12.9 %copy-start.7 = (bf16[1,20736]{1,0:T(2,128)(2,1)S(1)}, bf16[1,20736]{1,0:T(2,128)(2,1)}, u32[]{:S(2)}) copy-start(bf16[1,20736]{1,0:T(2,128)(2,1)} %probe_ref.1) | copy-start | bytes 124420
  64.2 13.7 %copy-start.8 = (f32[1,20736]{1,0:T(1,128)S(1)}, f32[1,20736]{1,0:T(1,128)}, u32[]{:S(2)}) copy-start(f32[1,20736]{1,0:T(1,128)} %param.14) | copy-start | bytes 248836
  64.3 38.5 %all-to-all-start.1 = ((bf16[64,48,128]{2,1,0:T(8,128)(2,1)}), bf16[64,48,128]{2,1,0:T(8,128)(2,1)S(1)}, u32[]{:S(2)}, u32[]{:S(2)}) async-start(bf16[64,48,128]{2,1,0:T(8,128)(2,1)} %middle_part.1), calls=%async_computation.1 | async-start | bytes 1572864 | tf_op jit(solution)/shard_map/all_to_all | solution.py:408
  102.7 0.9 copy-start.2

commit v3 on v2

v3 whole, which is shorter than its diff:
```python
import math

import jax
import jax.numpy as jnp
from jax import lax
from jax.experimental import pallas as pl
from jax.experimental.pallas import tpu as pltpu
from jax.sharding import PartitionSpec as P

HEAD = 96
LANES = 128
decay_rate = 0.99

ROW = 8

HEADS = 4

BLOCKS = 3
WIDE = ((0, 0), (1, 0), (1, 64), (2, 64))
SLIM = ((0, 64), (0, 96), (2, 0), (2, 32))
SPAN = 64
PAIRS = SPAN // 2
QUADS = SPAN // 4
WINDOW = PAIRS + QUADS
USED = 56
HALF = LANES // 2
QUARTER = LANES // 4

VMEM = pl.BlockSpec(memory_space=pltpu.VMEM)
SMEM = pl.BlockSpec(memory_space=pltpu.SMEM)
HBM = pl.BlockSpec(memory_space=pltpu.HBM)


def lane_of(rows):
    return lax.broadcasted_iota(jnp.int32, (rows, LANES), 1)


def turn(values, lanes):
    lanes = lanes % LANES
    return values if lanes == 0 else pltpu.roll(values, lanes, 1)


def first_block(counts_ref, shard):
    return lax.fori_loop(0, shard, lambda at, total: total + counts_ref[at] // LANES, jnp.int32(0))


def by_quarter(parts):
    lane = lane_of(parts[0].shape[0])
    low = jnp.where(lane < QUARTER, parts[0], parts[1])
    high = jnp.where(lane < 3 * QUARTER, parts[2], parts[3])
    return jnp.where(lane < HALF, low, high)


def pack_shard(place_ref, counts_hbm, probe_hbm, out_ref, rows, counts_ref, probe_ref, sems):
    copy = place_ref[0]
    loads = [
        pltpu.make_async_copy(counts_hbm, counts_ref, sems.at[0]),
        pltpu.make_async_copy(probe_hbm, probe_ref, sems.at[1]),
    ]
    for load in loads:
        load.start()
    rows[...] = jnp.zeros_like(rows)
    for load in loads:
        load.wait()
    shift = lax.rem(first_block(counts_ref, place_ref[1]), BLOCKS)
    for block in range(probe_ref.shape[1] // LANES):
        rows[pl.ds(shift + block, 1), :] = probe_ref[0:1, block * LANES : (block + 1) * LANES].astype(jnp.float32)

    def window(head):
        block, lane = WIDE[head]
        wide = rows[pl.ds(block, SPAN, stride=BLOCKS), :]
        pairs = jnp.where(lane_of(PAIRS) < HALF, turn(wide[:PAIRS], -lane), turn(wide[PAIRS:], HALF - lane))
        block, lane = SLIM[head]
        slim = rows[pl.ds(block, SPAN, stride=BLOCKS), :]
        quads = by_quarter(
            [turn(slim[at * QUADS : (at + 1) * QUADS], at * QUARTER - lane) for at in range(4)]
        )
        return jnp.concatenate([pairs, quads], axis=0).astype(jnp.bfloat16)

    for which in range(2):

        @pl.when(copy == which)
        def _():
            even, odd = window(2 * which), window(2 * which + 1)

            def store(at, carry):
                first = at // ROW * 2 * ROW + lax.rem(at, ROW)
                out_ref[first] = even
                out_ref[first + ROW] = odd
                return carry

            lax.fori_loop(0, out_ref.shape[0] // 2, store, 0, unroll=4)


def split_heads(
    place_ref, tokens_hbm, query_hbm, key_hbm, value_hbm, cot_hbm, keep_ref, x_ref, copy_ref, held, sems
):
    copy, parity, core = place_ref[0], place_ref[2], place_ref[3]
    length, features = tokens_hbm.shape
    half = length // 2
    packed = 2 * HEADS * HEAD
    arrays = [held.at[at] for at in range(HEADS)]
    loads = [
        pltpu.make_async_copy(source, target, sems.at[at])
        for at, (source, target) in enumerate(zip((query_hbm, key_hbm, value_hbm, cot_hbm), arrays))
    ]
    tokens = tokens_hbm.at[pl.ds(pl.multiple_of(core * half, half), half), :]
    loads.append(pltpu.make_async_copy(tokens, x_ref.at[:, pl.ds(packed, features)], sems.at[4]))
    loads.append(pltpu.make_async_copy(tokens, copy_ref.at[:, pl.ds(0, features)], sems.at[5]))
    for load in loads:
        load.start()
    for load in loads[:HEADS]:
        load.wait()

    def put(head, target_ref, start):
        for side in range(2):
            for at, ref in enumerate(arrays):
                to = start + (side * HEADS + at) * HEAD
                target_ref[:, to : to + HEAD] = ref[side * half : (side + 1) * half, head * HEAD : (head + 1) * HEAD]

    for mine in range(HEADS):

        @pl.when(2 * copy + parity == mine)
        def _():
            for at, ref in enumerate(arrays):
                keep_ref[:, at * HEAD : (at + 1) * HEAD] = ref[:, mine * HEAD : (mine + 1) * HEAD]
            put(mine ^ 1, x_ref, 0)
            put(mine ^ 3, x_ref, packed + features)
            put(mine ^ 2, copy_ref, features)

    for load in loads[HEADS:]:
        load.wait()


def attention_part(heads):
    length = heads.shape[0]
    query, key_head, value_head, cot_head = (heads[:, at * HEAD : (at + 1) * HEAD] for at in range(HEADS))
    inv_root = 1.0 / math.sqrt(HEAD)
    causal = lax.broadcasted_iota(jnp.int32, (length, length), 0) >= lax.broadcasted_iota(
        jnp.int32, (length, length), 1
    )
    scores = inv_root * times_transposed(query, key_head)
    scores = jnp.where(causal, scores, jnp.float32(-1e30))
    expo_terms = jnp.exp(scores - jnp.max(scores, axis=1, keepdims=True))
    attn = expo_terms / jnp.sum(expo_terms, axis=1, keepdims=True)
    back = times_transposed(cot_head, value_head)
    padded_key = jnp.concatenate([key_head, jnp.zeros((length, LANES - HEAD), key_head.dtype)], axis=1)
    return padded_key, attn, back, back - jnp.sum(attn * back, axis=1, keepdims=True)


def times_transposed(left, right):
    return lax.dot_general(left, right, (((1,), (1,)), ((), ())), preferred_element_type=jnp.float32)


def join_halves(core, mine_ref, mine_at, heads_at, other_ref, other_row, tokens_ref, row):
    half, features = mine_ref.shape[0], tokens_ref.shape[1]
    side = HEADS * HEAD
    tokens_ref[pl.ds(pl.multiple_of(row + core * half, half), half), :] = mine_ref[:, mine_at : mine_at + features]
    tokens_ref[pl.ds(pl.multiple_of(row + (1 - core) * half, half), half), :] = other_ref[
        other_row : other_row + half, :
    ]
    return jnp.concatenate(
        [mine_ref[:, heads_at : heads_at + side], mine_ref[:, heads_at + side : heads_at + 2 * side]], axis=0
    )


def prepare(
    place_ref,
    tokens_hbm,
    probe_hbm,
    hess_hbm,
    keep_ref,
    x_ref,
    copy_ref,
    swapped_ref,
    tokens_out,
    turned_out,
    key_ref,
    attn_ref,
    back_ref,
    centred_ref,
    factor_ref,
    base_ref,
    tokens_ref,
    turned_ref,
    probe_ref,
    hess_ref,
    sems,
):
    core = place_ref[3]
    length, features = tokens_hbm.shape
    packed = 2 * HEADS * HEAD
    loads = [
        pltpu.make_async_copy(tokens_hbm, tokens_ref.at[pl.ds(0, length), :], sems.at[0]),
        pltpu.make_async_copy(probe_hbm, probe_ref, sems.at[1]),
        pltpu.make_async_copy(hess_hbm, hess_ref, sems.at[2]),
    ]
    for load in loads:
        load.start()
    heads_of = [
        keep_ref[...],
        join_halves(core, x_ref, packed, 0, swapped_ref, 0, tokens_ref, length),
        join_halves(core, copy_ref, 0, features, swapped_ref, x_ref.shape[0], tokens_ref, 2 * length),
    ]
    loads[0].wait()
    stores = [
        pltpu.make_async_copy(tokens_ref, tokens_out, sems.at[3]),
        pltpu.make_async_copy(turned_ref, turned_out, sems.at[4]),
    ]
    stores[0].start()
    turned_ref[...] = tokens_ref[...].T
    stores[1].start()
    for at, heads in enumerate(heads_of):
        key_ref[at], attn_ref[at], back_ref[at], centred_ref[at] = attention_part(heads)
    for load in loads[1:]:
        load.wait()
    for block in range(probe_ref.shape[1] // LANES):
        lanes = slice(block * LANES, (block + 1) * LANES)
        factor_ref[block : block + 1, :] = (1.0 - decay_rate) * probe_ref[0:1, lanes].astype(jnp.float32)
        base_ref[block : block + 1, :] = decay_rate * hess_ref[0:1, lanes]
    for store in stores:
        store.wait()


def middle_part(
    place_ref,
    counts_ref,
    tokens_hbm,
    turned_hbm,
    pieces_ref,
    relay_ref,
    swapped_ref,
    key_ref,
    attn_ref,
    back_ref,
    centred_ref,
    out_ref,
    wide,
    slim,
    probe,
    tangent,
    spread,
    tokens,
    turned,
    last_tokens,
    last_turned,
    sems,
):
    loads = [
        pltpu.make_async_copy(tokens_hbm, tokens, sems.at[0]),
        pltpu.make_async_copy(turned_hbm, turned, sems.at[1]),
    ]
    for load in loads:
        load.start()
    copy, parity, core = place_ref[0], place_ref[2], place_ref[3]
    length = attn_ref.shape[1]
    features = probe.shape[0]
    shards = pieces_ref.shape[0]
    inv_root = 1.0 / math.sqrt(HEAD)
    pair_lane, quad_lane = lane_of(PAIRS), lane_of(QUADS)
    top_row = lax.broadcasted_iota(jnp.int32, (8, LANES), 0) == 0
    wide_block = (2 * copy + parity + 1) // 2
    slim_block = 2 * copy

    def place(shard, start):
        first = start // BLOCKS
        shift = start - first * BLOCKS
        piece = pieces_ref[shard].astype(jnp.float32)
        pairs, quads = piece[:PAIRS], piece[PAIRS:]
        wide_values = [jnp.where(pair_lane < HALF, pairs, 0.0), jnp.where(pair_lane < HALF, 0.0, pairs)]
        slim_values = [jnp.where(quad_lane // QUARTER == at, quads, 0.0) for at in range(4)]
        for slab, block, values in ((wide, wide_block, wide_values), (slim, slim_block, slim_values)):
            values = jnp.concatenate(values, axis=0)
            ours = jnp.logical_not(top_row & (block < shift))
            pltpu.store(slab.at[pl.ds(first, 8), :], values[:8], mask=ours)
            slab[pl.ds(first + 8, USED - 8), :] = values[8:USED]
        return start + counts_ref[shard] // LANES

    last_heads = join_halves(core, relay_ref, 0, features, swapped_ref, 0, last_tokens, 0)
    last_turned[...] = last_tokens[...].T
    parts = [(key_ref[at], attn_ref[at], back_ref[at], centred_ref[at]) for at in range(key_ref.shape[0])]
    parts.append(attention_part(last_heads))
    lax.fori_loop(0, shards, place, jnp.int32(0), unroll=4)
    for load in loads:
        load.wait()
    probe[:, :LANES] = wide[:features, :].astype(jnp.bfloat16)
    probe[:, LANES:] = slim[:features, :].astype(jnp.bfloat16)

    row = 0
    for tokens_ref in (tokens, last_tokens):
        count = tokens_ref.shape[0]
        product = jnp.dot(tokens_ref[...], probe[...], preferred_element_type=jnp.float32)
        wide_sum, slim_sum = product[:, :LANES], product[:, LANES:]
        wide_sum = wide_sum + turn(wide_sum, HALF)
        slim_sum = slim_sum + turn(slim_sum, HALF)
        slim_sum = slim_sum + turn(slim_sum, QUARTER)
        lane = lane_of(count)
        ordered = jnp.where(
            parity == 0,
            jnp.where(lane < HALF, wide_sum, slim_sum),
            jnp.where(lane < QUARTER, slim_sum, turn(wide_sum, QUARTER)),
        )
        tangent[row : row + count, :] = ordered.astype(jnp.bfloat16)
        row += count

    for at, (key_head, attn, back, centred) in enumerate(parts):
        rows = slice(at * length, (at + 1) * length)
        score_tangent = inv_root * times_transposed(tangent[rows, :], key_head)
        mean_tangent = jnp.sum(attn * score_tangent, axis=1, keepdims=True)
        weight_tangent = attn * (score_tangent - mean_tangent)
        delta_tangent = jnp.sum(weight_tangent * back, axis=1, keepdims=True)
        grad_tangent = (weight_tangent * centred - attn * delta_tangent).astype(jnp.bfloat16)
        scaled = inv_root * jnp.dot(grad_tangent, key_head, preferred_element_type=jnp.float32)
        turns = [turn(scaled, at * QUARTER) for at in range(4)]
        wide_part = jnp.where(
            parity == 0,
            jnp.where(lane_of(length) < HALF, scaled, turns[2]),
            jnp.where(lane_of(length) < HALF, turns[3], turns[1]),
        )
        slim_part = jnp.where(
            parity == 0, by_quarter([turns[2], turns[3], scaled, turns[1]]), by_quarter(turns)
        )
        spread[rows, :LANES] = wide_part.astype(jnp.bfloat16)
        spread[rows, LANES:] = slim_part.astype(jnp.bfloat16)

    split = tokens.shape[0]
    term = jnp.dot(turned[...], spread[:split, :], preferred_element_type=jnp.float32)
    term += jnp.dot(last_turned[...], spread[split:, :], preferred_element_type=jnp.float32)
    wide[:features, :] = term[:, :LANES]
    slim[:features, :] = term[:, LANES:]

    def cut_out(shard, start):
        first = start // BLOCKS
        pairs = jnp.where(pair_lane < HALF, wide[pl.ds(first, PAIRS), :], wide[pl.ds(first + PAIRS, PAIRS), :])
        quads = by_quarter([slim[pl.ds(first + at * QUADS, QUADS), :] for at in range(4)])
        out_ref[shard] = jnp.concatenate([pairs, quads], axis=0).astype(jnp.bfloat16)
        return start + counts_ref[shard] // LANES

    lax.fori_loop(0, shards, cut_out, jnp.int32(0), unroll=4)


def add_groups(terms_ref, out_ref):
    for parity in range(2):

        def add(at, total):
            return total + terms_ref[at // ROW * 2 * ROW + lax.rem(at, ROW) + parity * ROW].astype(jnp.float32)

        out_ref[parity * WINDOW : (parity + 1) * WINDOW, :] = lax.fori_loop(
            0, terms_ref.shape[0] // 2, add, jnp.zeros((WINDOW, LANES), jnp.float32), unroll=4
        )


def update_shard(place_ref, counts_ref, sums_ref, factor_ref, base_ref, out_ref, rows):
    shard = place_ref[1]
    shift = lax.rem(first_block(counts_ref, shard), BLOCKS)
    blocks = factor_ref.shape[0]

    def wide_part(head):
        pairs = sums_ref[head // 2, head % 2 * WINDOW : head % 2 * WINDOW + PAIRS, :]
        lane = WIDE[head][1]
        return jnp.concatenate([turn(pairs, lane - at * HALF) for at in range(2)], axis=0)

    def slim_part(head):
        quads = sums_ref[head // 2, head % 2 * WINDOW + PAIRS : (head % 2 + 1) * WINDOW, :]
        lane = SLIM[head][1]
        return jnp.concatenate([turn(quads, lane - at * QUARTER) for at in range(4)], axis=0)

    lane = lane_of(SPAN)
    rows[pl.ds(0, SPAN, stride=BLOCKS), :] = jnp.where(
        lane < HALF, wide_part(0), jnp.where(lane < 3 * QUARTER, slim_part(0), slim_part(1))
    )
    rows[pl.ds(1, SPAN, stride=BLOCKS), :] = jnp.where(lane < HALF, wide_part(1), wide_part(2))
    rows[pl.ds(2, SPAN, stride=BLOCKS), :] = jnp.where(
        lane < HALF, jnp.where(lane < QUARTER, slim_part(2), slim_part(3)), wide_part(3)
    )
    inner = lax.broadcasted_iota(jnp.int32, (blocks, LANES), 0)
    product = jnp.where(inner < counts_ref[shard] // LANES, rows[pl.ds(shift, blocks), :], 0.0)
    updated = base_ref[...] + factor_ref[...] * product
    for block in range(blocks):
        out_ref[0:1, block * LANES : (block + 1) * LANES] = updated[block : block + 1, :]


def call(kernel, outs, specs, operands, mebibytes, scratch=(), in_hbm=0):
    shapes = [
        (pltpu.HBM if at < in_hbm else jax.ShapeDtypeStruct)(shape, dtype) for at, (shape, dtype) in enumerate(outs)
    ]
    specs = specs + [VMEM] * (len(operands) - len(specs))
    operands = [
        pltpu.with_memory_space_constraint(operand, pltpu.HBM) if spec is HBM else operand
        for spec, operand in zip(specs, operands)
    ]
    result = pl.pallas_call(
        kernel,
        out_shape=shapes,
        in_specs=specs,
        out_specs=[HBM] * in_hbm + [VMEM] * (len(shapes) - in_hbm),
        scratch_shapes=list(scratch),
        compiler_params=pltpu.CompilerParams(vmem_limit_bytes=mebibytes * 1024 * 1024),
        name=kernel.__name__,
    )(*operands)
    return result if len(shapes) > 1 else result[0]


def body(tokens, queries, key_rows, value_rows, cotangent, probe_shards, hess_old, shard_counts):
    length, features = tokens.shape
    half = length // 2
    packed = 2 * HEADS * HEAD
    shards = shard_counts.shape[0]
    blocks = probe_shards.shape[1] // LANES
    bf16, f32 = jnp.bfloat16, jnp.float32
    slab = pltpu.VMEM((features + SPAN, LANES), f32)
    rows = pltpu.VMEM((BLOCKS * SPAN + 8, LANES), f32)
    at = lax.axis_index("dp")
    place = jnp.stack(
        [lax.axis_index("replica"), at, at // ROW % 2, lax.axis_index("tensor") % 2]
    ).astype(jnp.int32)

    def swap_copies(array):
        return lax.ppermute(array, "replica", [(0, 1), (1, 0)])

    def swap_cores(array):
        return lax.ppermute(array, "tensor", [(one, one ^ 1) for one in range(lax.axis_size("tensor"))])

    keep, to_x, to_copy = call(
        split_heads,
        [
            ((length, HEADS * HEAD), bf16),
            ((half, packed + features + packed), bf16),
            ((half, features + packed), bf16),
        ],
        [SMEM] + [HBM] * 5,
        (place, tokens, queries, key_rows, value_rows, cotangent),
        8,
        (pltpu.VMEM((HEADS, *queries.shape), bf16), pltpu.SemaphoreType.DMA((6,))),
    )
    from_x = lax.ppermute(to_x, "dp", [(one, one ^ ROW) for one in range(shards)])
    from_copy = swap_copies(to_copy)

    windows = call(
        pack_shard,
        [((shards, WINDOW, LANES), bf16)],
        [SMEM, HBM, HBM],
        (place, shard_counts, probe_shards),
        8,
        (
            rows,
            pltpu.SMEM(shard_counts.shape, jnp.int32),
            pltpu.VMEM(probe_shards.shape, bf16),
            pltpu.SemaphoreType.DMA((2,)),
        ),
    )
    pieces = lax.all_to_all(windows, "dp", 0, 0)

    relayed = swap_copies(from_x[:, packed:])
    swapped = swap_cores(
        jnp.concatenate([from_x[:, packed : packed + features], from_copy[:, :features]], axis=0)
    )
    swapped_last = swap_cores(relayed[:, :features])

    square = ((3, length, length), f32)
    update_part = ((blocks, LANES), f32)
    three_tokens = pltpu.VMEM((3 * length, features), bf16)
    three_turned = pltpu.VMEM((features, 3 * length), bf16)
    all_tokens, all_turned, *parts, factor, base = call(
        prepare,
        [
            ((3 * length, features), bf16),
            ((features, 3 * length), bf16),
            ((3, length, LANES), bf16),
            square,
            square,
            square,
            update_part,
            update_part,
        ],
        [SMEM, HBM, HBM, HBM],
        (place, tokens, probe_shards, hess_old, keep, from_x, from_copy, swapped),
        16,
        (
            three_tokens,
            three_turned,
            pltpu.VMEM(probe_shards.shape, bf16),
            pltpu.VMEM(hess_old.shape, f32),
            pltpu.SemaphoreType.DMA((5,)),
        ),
        in_hbm=2,
    )
    term_windows = call(
        middle_part,
        [((shards, WINDOW, LANES), bf16)],
        [SMEM, SMEM, HBM, HBM],
        (place, shard_counts, all_tokens, all_turned, pieces, relayed, swapped_last, *parts),
        24,
        (
            slab,
            slab,
            pltpu.VMEM((features, 2 * LANES), bf16),
            pltpu.VMEM((4 * length, LANES), bf16),
            pltpu.VMEM((4 * length, 2 * LANES), bf16),
            three_tokens,
            three_turned,
            pltpu.VMEM((length, features), bf16),
            pltpu.VMEM((features, length), bf16),
            pltpu.SemaphoreType.DMA((2,)),
        ),
    )
    terms = lax.all_to_all(term_windows, "dp", 0, 0)
    summed = call(add_groups, [((2 * WINDOW, LANES), f32)], [], (terms,), 8)
    sums = lax.all_gather(summed, "replica", axis=0)
    return call(
        update_shard,
        [((1, blocks * LANES), f32)],
        [SMEM, SMEM],
        (place, shard_counts, sums, factor, base),
        8,
        (rows,),
    )


def solution(mesh):
    placed = (
        P(("dp", "replica"), None),
        P(("dp", "replica"), "tensor"),
        P(("dp", "replica"), "tensor"),
        P(("dp", "replica"), "tensor"),
        P(("dp", "replica"), "tensor"),
        P("tensor", "dp"),
        P("tensor", "dp"),
        P(),
    )
    return jax.shard_map(
        body, mesh=mesh, in_specs=placed, out_specs=P("tensor", "dp"), check_vma=False
    )
```

time: 115 us -> 101 us (0.88)
  blocking collectives: 5.07 us -> 39.7 us
  waiting for transfers between devices: 33.7 us -> 13.1 us
  starting transfers between devices: 40.1 us -> 27.2 us
  Pallas kernels: 27.9 us -> 19.3 us
  local copies, waits for them, and re-layouts: 5.14 us -> 1.39 us
  other arithmetic: 2.31 us -> 0.13 us
    all_to_all x0 -> x1, blocking collectives: none -> 34.9 us  [body(): terms = lax.all_to_all(term_windows, 'dp', 0, 0)]
    all_to_all x1 -> x0, waiting for transfers between devices: 23.9 us -> none  [body(): terms = lax.all_to_all(term_windows, 'dp', 0, 0)]
    all_to_all x1 -> x0, starting transfers between devices: 12.8 us -> none  [body(): terms = lax.all_to_all(term_windows, 'dp', 0, 0)]
    pallas_call x7 -> x6, Pallas kernels: 27.9 us -> 19.3 us  [call(): pl.pallas_call(kernel, out_shape=shapes, in_specs=specs, out_specs=[HBM]...]
    unnamed x19 -> x10, local copies, waits for them, and re-layouts: 5.02 us -> 1.28 us
    all_to_all x1, waiting for transfers between devices: 0.01 us -> 3.34 us  [body(): pieces = lax.all_to_all(windows, 'dp', 0, 0)]
    unnamed x2 -> x0, other arithmetic: 1.7 us -> none
  transfers between devices with their start and end apart: 7 -> 6, of which waited for: 2 -> 2; matrix products, arithmetic and copies ran while one was open for 2% -> 0% of each run, Pallas kernels for 9% -> 7%
where the time goes in v3:
time: 101 us
  blocking collectives  39.7 us (39%)
  starting transfers between devices  27.2 us (27%)
  Pallas kernels  19.3 us (19%)
  waiting for transfers between devices  13.1 us (13%)
  local copies, waits for them, and re-layouts  1.39 us (1%)
    all_to_all x1, blocking collectives, body(): terms = lax.all_to_all(term_windows, 'dp', 0, 0)  34.9 us
    pallas_call x6, Pallas kernels, call(): pl.pallas_call(kernel, out_shape=shapes, in_specs=specs, out_specs=[HBM]...  19.3 us
    all_to_all x1, starting transfers between devices, body(): pieces = lax.all_to_all(windows, 'dp', 0, 0)  12.9 us
    ppermute x2, waiting for transfers between devices, swap_copies(): return lax.ppermute(array, 'replica', [(0, 1), (1, 0)])  9.77 us
    ppermute x2, starting transfers between devices, swap_copies(): return lax.ppermute(array, 'replica', [(0, 1), (1, 0)])  7.11 us
    all_gather x1, blocking collectives, body(): sums = lax.all_gather(summed, 'replica', axis=0)  4.77 us
    ppermute x2, starting transfers between devices, swap_cores(): lax.ppermute(array, 'tensor', [(one, one ^ 1) for one in range(lax.axis_s...  3.84 us
    ppermute x1, starting transfers between devices, body(): lax.ppermute(to_x, 'dp', [(one, one ^ ROW) for one in range(shards)])  3.4 us
  transfers between devices with their start and end apart: 6, of which 2 were waited for; matrix products, arithmetic and copies ran while one was open for 0% of the time, Pallas kernels for 7%

profile of v3, /device:TPU:260, one launch (start us, length us, event | category | flops | bytes accessed | tf_op | source)
XLA Modules:
  0.0 101.0 jit_solution(5158980710179371667)
XLA Ops:
  0.0 0.1 pad_add_fusion.place_ref
  0.1 1.9 %split_heads.1 = (bf16[128,384]{1,0:T(8,128)(2,1)S(1)}, bf16[64,4608]{1,0:T(8,128)(2,1)S(1)}, bf16[64,3840]{1,0:T(8,128)(2,1)S(1)}) custom-call(s32[4]{0:T(128)S(1)} %pad_add_fusion.place_ref, bf16[128,3072]{1,0:T(8,128)(2,1)} %tokens_hbm.3, bf16[128,384]{1,0:T(8,128)(2,1)} %query_hbm.1, bf16[128,384]{1,0:T(8,128)(2,1)} %key_hbm.1, ...), custom_call_target="tpu_custom_call" | custom-call | tf_op jit(solution)/shard_map/split_heads/pallas_call | solution.py:392
  2.0 3.4 %collective-permute-start = (bf16[64,4608]{1,0:T(8,128)(2,1)S(1)}, bf16[64,4608]{1,0:T(8,128)(2,1)S(1)}, u32[]{:S(2)}, u32[]{:S(2)}) collective-permute-start(bf16[64,4608]{1,0:T(8,128)(2,1)S(1)} %get-tuple-element.17), channel_id=1, source_target_pairs={{0,128},{16,144},{32,160},{48,176},{64,192},{80,208},{96,224},{112... | collective-permute-start | bytes 1769480 | tf_op jit(solution)/shard_map/ppermute | solution.py:436
  5.4 5.2 %collective-permute-start.1 = (bf16[64,3840]{1,0:T(8,128)(2,1)S(1)}, bf16[64,3840]{1,0:T(8,128)(2,1)S(1)}, u32[]{:S(2)}, u32[]{:S(2)}) collective-permute-start(bf16[64,3840]{1,0:T(8,128)(2,1)S(1)} %get-tuple-element.18), channel_id=1, source_target_pairs={{0,1},{1,0},{2,3},{3,2},{4,5},{5,4},{6,7},{7,6},{8,9},{9,8},{10,11... | collective-permute-start | bytes 1474568 | tf_op jit(solution)/shard_map/ppermute | solution.py:419
  10.6 2.7 %pack_shard.1 = bf16[64,48,128]{2,1,0:T(8,128)(2,1)} custom-call(s32[4]{0:T(128)S(1)} %pad_add_fusion.place_ref, s32[64]{0:T(128)} %counts_ref.3, bf16[1,20736]{1,0:T(2,128)(2,1)} %probe_hbm.3), custom_call_target="tpu_custom_call" | custom-call | tf_op jit(solution)/shard_map/pack_shard/pallas_call | solution.py:392
  13.3 12.9 %all-to-all-start = ((bf16[64,48,128]{2,1,0:T(8,128)(2,1)}), bf16[64,48,128]{2,1,0:T(8,128)(2,1)S(1)}, u32[]{:S(2)}, u32[]{:S(2)}) async-start(bf16[64,48,128]{2,1,0:T(8,128)(2,1)} %pack_shard.1), calls=%async_computation | async-start | bytes 1572864 | tf_op jit(solution)/shard_map/all_to_all | solution.py:452
  26.2 0.0 collective-permute-done.1.copy_ref
  26.3 0.0 collective-permute-done.x_ref
  26.3 1.9 %collective-permute-start.3 = (bf16[64,3840]{1,0:T(8,128)(2,1)S(1)}, bf16[64,3840]{1,0:T(8,128)(2,1)S(1)}, u32[]{:S(2)}, u32[]{:S(2)}) collective-permute-start(bf16[64,3840]{1,0:T(8,128)(2,1)S(1)} %slice.18), channel_id=1, source_target_pairs={{0,1},{1,0},{2,3},{3,2},{4,5},{5,4},{6,7},{7,6},{8,9},{9,8},{10,11... | collective-permute-start | bytes 1474568 | tf_op jit(solution)/shard_map/ppermute | solution.py:419
  28.3 0.1 pad_maximum_fusion
  28.3 1.9 %collective-permute-start.2 = (bf16[128,3072]{1,0:T(8,128)(2,1)S(1)}, bf16[128,3072]{1,0:T(8,128)(2,1)S(1)}, u32[]{:S(2)}, u32[]{:S(2)}) collective-permute-start(bf16[128,3072]{1,0:T(8,128)(2,1)S(1)} %pad_maximum_fusion), channel_id=1, source_target_pairs={{0,2},{2,0},{4,6},{6,4},{8,10},{10,8},{12,14},{14,12},{1,3},{3,1},... | collective-permute-start | bytes 2359304 | tf_op jit(solution)/shard_map/ppermute | solution.py:422
  30.3 9.8 %collective-permute-done.3.relay_ref = bf16[64,3840]{1,0:T(8,128)(2,1)S(1)} collective-permute-done((bf16[64,3840]{1,0:T(8,128)(2,1)S(1)}, bf16[64,3840]{1,0:T(8,128)(2,1)S(1)}, u32[]{:S(2)}, u32[]{:S(2)}) %collective-permute-start.3) | collective-permute-done | bytes 491552 | tf_op jit(solution)/shard_map/ppermute | solution.py:419
  40.1 0.0 copy-start.4
  40.1 1.9 %collective-permute-start.4 = (bf16[64,3072]{1,0:T(8,128)(2,1)S(1)}, bf16[64,3072]{1,0:T(8,128)(2,1)S(1)}, u32[]{:S(2)}, u32[]{:S(2)}) collective-permute-start(bf16[64,3072]{1,0:T(8,128)(2,1)S(1)} %slice.19), channel_id=1, source_target_pairs={{0,2},{2,0},{4,6},{6,4},{8,10},{10,8},{12,14},{14,12},{1,3},{3,1},... | collective-permute-start | bytes 1179656 | tf_op jit(solution)/shard_map/ppermute | solution.py:422
  42.0 0.0 collective-permute-done.2.swapped_ref
  42.0 3.9 %prepare.1 = (bf16[384,3072]{1,0:T(8,128)(2,1)}, bf16[3072,384]{1,0:T(8,128)(2,1)}, bf16[3,128,128]{2,1,0:T(8,128)(2,1)S(1)}, f32[3,128,128]{2,1,0:T(8,128)S(1)}...) custom-call(s32[4]{0:T(128)S(1)} %pad_add_fusion.place_ref, ...), custom_call_target="tpu_custom_call" | custom-call | tf_op jit(solution)/shard_map/prepare/pallas_call | solution.py:392
  45.9 0.0 copy-start
  46.0 0.6 copy-done
  46.6 0.0 copy-start.2
  46.6 0.6 copy-done.2
  47.2 0.0 collective-permute-done.4.swapped_ref
  47.2 3.3 %all-to-all-done.pieces_ref = bf16[64,48,128]{2,1,0:T(8,128)(2,1)S(1)} async-done(((bf16[64,48,128]{2,1,0:T(8,128)(2,1)}), bf16[64,48,128]{2,1,0:T(8,128)(2,1)S(1)}, u32[]{:S(2)}, u32[]{:S(2)}) %all-to-all-start) | async-done | bytes 786464 | tf_op jit(solution)/shard_map/all_to_all | solution.py:452
  50.6 0.0 copy-done.4
  50.6 8.7 %middle_part.1 = bf16[64,48,128]{2,1,0:T(8,128)(2,1)S(1)} custom-call(s32[4]{0:T(128)S(1)} %pad_add_fusion.place_ref, s32[64]{0:T(128)S(1)} %copy-done.4, bf16[384,3072]{1,0:T(8,128)(2,1)} %get-tuple-element.19.tokens_hbm, bf16[3072,384]{1,0:T(8,128)(2,1)} %get-tuple-element.20.turned_hbm, bf16[64,48,128]{2,1,0:T(8,128)(2,1)S(1)} %all-to-all-done.pieces_ref, ...), custom_call_target="tpu_custom_call" | custom-call | tf_op jit(solution)/shard_map/middle_part/pallas_call | solution.py:392
  59.3 0.0 copy-start.1
  59.3 0.0 copy-start.3
  59.3 34.9 %all_to_all.10.terms_ref = bf16[64,48,128]{2,1,0:T(8,128)(2,1)S(1)} all-to-all(bf16[64,48,128]{2,1,0:T(8,128)(2,1)S(1)} %middle_part.1), channel_id=1, replica_groups=mesh['dp'=64,'tensor'=8,'replica'=2] {'dp'}, dimensions={0} | all-to-all | bytes 1572864 | tf_op jit(solution)/shard_map/all_to_all | solution.py:507
  94.2 0.4 add_groups.1
  94.7 4.8 %all-gather = f32[192,128]{1,0:T(8,128)S(1)} all-gather(f32[96,128]{1,0:T(8,128)S(1)} %add_groups.1), channel_id=2, replica_groups=mesh['dp'=64,'tensor'=8,'replica'=2] {'replica'}, dimensions={0}, use_global_device_ids=true | all-gather | bytes 147456 | tf_op jit(solution)/shard_map/all_gather | solution.py:509
  99.4 0.0 copy-done.1
  99.4 0.0 copy-done.3
  99.4 1.5 %update_shard.1 = f32[1,20736]{1,0:T(1,128)} custom-call(s32[4]{0:T(128)S(1)} %pad_add_fusion.place_ref, s32[64]{0:T(128)S(1)} %copy-done.4, f32[2,96,128]{2,1,0:T(8,128)S(1)} %bitcast.5, f32[162,128]{1,0:T(8,128)S(1)} %copy-done.1, f32[162,128]{1,0:T(8,128)S(1)} %copy-done.3), custom_call_target="tpu_custom_call" | custom-call | tf_op jit(solution)/shard_map/update_shard/pallas_call | solution.py:392
  (4 shorter events, 0.1 us)
Async XLA Ops:
  2.0 24.2 %collective-permute-start = (bf16[64,4608]{1,0:T(8,128)(2,1)S(1)}, bf16[64,4608]{1,0:T(8,128)(2,1)S(1)}, u32[]{:S(2)}, u32[]{:S(2)}) collective-permute-start(bf16[64,4608]{1,0:T(8,128)(2,1)S(1)} %get-tuple-element.17), channel_id=1, source_target_pairs={{0,128},{16,144},{32,160},{48,176},{64,192},{80,208},{96,224},{112... | collective-permute-start | bytes 1769480 | tf_op jit(solution)/shard_map/ppermute | solution.py:436
  5.4 20.8 %collective-permute-start.1 = (bf16[64,3840]{1,0:T(8,128)(2,1)S(1)}, bf16[64,3840]{1,0:T(8,128)(2,1)S(1)}, u32[]{:S(2)}, u32[]{:S(2)}) collective-permute-start(bf16[64,3840]{1,0:T(8,128)(2,1)S(1)} %get-tuple-element.18), channel_id=1, source_target_pairs={{0,1},{1,0},{2,3},{3,2},{4,5},{5,4},{6,7},{7,6},{8,9},{9,8},{10,11... | collective-permute-start | bytes 1474568 | tf_op jit(solution)/shard_map/ppermute | solution.py:419
  13.3 37.2 %all-to-all-start = ((bf16[64,48,128]{2,1,0:T(8,128)(2,1)}), bf16[64,48,128]{2,1,0:T(8,128)(2,1)S(1)}, u32[]{:S(2)}, u32[]{:S(2)}) async-start(bf16[64,48,128]{2,1,0:T(8,128)(2,1)} %pack_shard.1), calls=%async_computation | async-start | bytes 1572864 | tf_op jit(solution)/shard_map/all_to_all | solution.py:452
  26.3 13.7 %collective-permute-start.3 = (bf16[64,3840]{1,0:T(8,128)(2,1)S(1)}, bf16[64,3840]{1,0:T(8,128)(2,1)S(1)}, u32[]{:S(2)}, u32[]{:S(2)}) collective-permute-start(bf16[64,3840]{1,0:T(8,128)(2,1)S(1)} %slice.18), channel_id=1, source_target_pairs={{0,1},{1,0},{2,3},{3,2},{4,5},{5,4},{6,7},{7,6},{8,9},{9,8},{10,11... | collective-permute-start | bytes 1474568 | tf_op jit(solution)/shard_map/ppermute | solution.py:419
  28.3 13.7 %collective-permute-start.2 = (bf16[128,3072]{1,0:T(8,128)(2,1)S(1)}, bf16[128,3072]{1,0:T(8,128)(2,1)S(1)}, u32[]{:S(2)}, u32[]{:S(2)}) collective-permute-start(bf16[128,3072]{1,0:T(8,128)(2,1)S(1)} %pad_maximum_fusion), channel_id=1, source_target_pairs={{0,2},{2,0},{4,6},{6,4},{8,10},{10,8},{12,14},{14,12},{1,3},{3,1},... | collective-permute-start | bytes 2359304 | tf_op jit(solution)/shard_map/ppermute | solution.py:422
  40.1 10.5 %copy-start.4 = (s32[64]{0:T(128)S(1)}, s32[64]{0:T(128)}, u32[]{:S(2)}) copy-start(s32[64]{0:T(128)} %counts_ref.3) | copy-start | bytes 772
  40.1 7.1 %collective-permute-start.4 = (bf16[64,3072]{1,0:T(8,128)(2,1)S(1)}, bf16[64,3072]{1,0:T(8,128)(2,1)S(1)}, u32[]{:S(2)}, u32[]{:S(2)}) collective-permute-start(bf16[64,3072]{1,0:T(8,128)(2,1)S(1)} %slice.19), channel_id=1, source_target_pairs={{0,2},{2,0},{4,6},{6,4},{8,10},{10,8},{12,14},{14,12},{1,3},{3,1},... | collective-permute-start | bytes 1179656 | tf_op jit(solution)/shard_map/ppermute | solution.py:422
  45.9 0.6 copy-start
  46.6 0.6 copy-start.2
  59.3 40.1 %copy-start.1 = (f32[162,128]{1,0:T(8,128)S(1)}, f32[162,128]{1,0:T(8,128)}, u32[]{:S(2)}) copy-start(f32[162,128]{1,0:T(8,128)} %copy-done) | copy-start | bytes 248836
  59.3 40.1 %copy-start.3 = (f32[162,128]{1,0:T(8,128)S(1)}, f32[162,128]{1,0:T(8,128)}, u32[]{:S(2)}) copy-start(f32[162,128]{1,0:T(8,128)} %copy-done.2) | copy-start | bytes 248836

commit v4 on v3

--- a/solution.py
+++ b/solution.py
@@ -51,17 +51,50 @@
     return jnp.where(lane < HALF, low, high)
 
 
-def pack_shard(place_ref, counts_hbm, probe_hbm, out_ref, rows, counts_ref, probe_ref, sems):
-    copy = place_ref[0]
-    loads = [
+def pack(
+    place_ref,
+    counts_hbm,
+    probe_hbm,
+    tokens_hbm,
+    query_hbm,
+    key_hbm,
+    value_hbm,
+    cot_hbm,
+    windows_hbm,
+    keep_ref,
+    x_ref,
+    copy_ref,
+    rows,
+    counts_ref,
+    probe_ref,
+    windows,
+    held,
+    sems,
+):
+    copy, parity, core = place_ref[0], place_ref[2], place_ref[3]
+    length, features = tokens_hbm.shape
+    half = length // 2
+    packed = 2 * HEADS * HEAD
+    shard_loads = [
         pltpu.make_async_copy(counts_hbm, counts_ref, sems.at[0]),
         pltpu.make_async_copy(probe_hbm, probe_ref, sems.at[1]),
     ]
-    for load in loads:
+    arrays = [held.at[at] for at in range(HEADS)]
+    head_loads = [
+        pltpu.make_async_copy(source, target, sems.at[2 + at])
+        for at, (source, target) in enumerate(zip((query_hbm, key_hbm, value_hbm, cot_hbm), arrays))
+    ]
+    tokens = tokens_hbm.at[pl.ds(pl.multiple_of(core * half, half), half), :]
+    token_loads = [
+        pltpu.make_async_copy(tokens, x_ref.at[:, pl.ds(packed, features)], sems.at[6]),
+        pltpu.make_async_copy(tokens, copy_ref.at[:, pl.ds(0, features)], sems.at[7]),
+    ]
+    for load in shard_loads + head_loads + token_loads:
         load.start()
     rows[...] = jnp.zeros_like(rows)
-    for load in loads:
+    for load in shard_loads:
         load.wait()
+
     shift = lax.rem(first_block(counts_ref, place_ref[1]), BLOCKS)
     for block in range(probe_ref.shape[1] // LANES):
         rows[pl.ds(shift + block, 1), :] = probe_ref[0:1, block * LANES : (block + 1) * LANES].astype(jnp.float32)
@@ -85,31 +118,15 @@
 
             def store(at, carry):
                 first = at // ROW * 2 * ROW + lax.rem(at, ROW)
-                out_ref[first] = even
-                out_ref[first + ROW] = odd
+                windows[first] = even
+                windows[first + ROW] = odd
                 return carry
 
-            lax.fori_loop(0, out_ref.shape[0] // 2, store, 0, unroll=4)
-
-
-def split_heads(
-    place_ref, tokens_hbm, query_hbm, key_hbm, value_hbm, cot_hbm, keep_ref, x_ref, copy_ref, held, sems
-):
-    copy, parity, core = place_ref[0], place_ref[2], place_ref[3]
-    length, features = tokens_hbm.shape
-    half = length // 2
-    packed = 2 * HEADS * HEAD
-    arrays = [held.at[at] for at in range(HEADS)]
-    loads = [
-        pltpu.make_async_copy(source, target, sems.at[at])
-        for at, (source, target) in enumerate(zip((query_hbm, key_hbm, value_hbm, cot_hbm), arrays))
-    ]
-    tokens = tokens_hbm.at[pl.ds(pl.multiple_of(core * half, half), half), :]
-    loads.append(pltpu.make_async_copy(tokens, x_ref.at[:, pl.ds(packed, features)], sems.at[4]))
-    loads.append(pltpu.make_async_copy(tokens, copy_ref.at[:, pl.ds(0, features)], sems.at[5]))
-    for load in loads:
-        load.start()
-    for load in loads[:HEADS]:
+            lax.fori_loop(0, windows.shape[0] // 2, store, 0, unroll=4)
+
+    leave = pltpu.make_async_copy(windows, windows_hbm, sems.at[8])
+    leave.start()
+    for load in head_loads:
         load.wait()
 
     def put(head, target_ref, start):
@@ -128,8 +145,9 @@
             put(mine ^ 3, x_ref, packed + features)
             put(mine ^ 2, copy_ref, features)
 
-    for load in loads[HEADS:]:
+    for load in token_loads:
         load.wait()
+    leave.wait()
 
 
 def attention_part(heads):
@@ -238,20 +256,15 @@
     wide,
     slim,
     probe,
-    tangent,
     spread,
     tokens,
     turned,
-    last_tokens,
-    last_turned,
     sems,
 ):
-    loads = [
-        pltpu.make_async_copy(tokens_hbm, tokens, sems.at[0]),
-        pltpu.make_async_copy(turned_hbm, turned, sems.at[1]),
-    ]
-    for load in loads:
-        load.start()
+    last = tokens_hbm.shape[0]
+    load_tokens = pltpu.make_async_copy(tokens_hbm, tokens.at[pl.ds(0, last), :], sems.at[0])
+    load_turned = pltpu.make_async_copy(turned_hbm, turned.at[:, pl.ds(0, last)], sems.at[1])
+    load_tokens.start()
     copy, parity, core = place_ref[0], place_ref[2], place_ref[3]
     length = attn_ref.shape[1]
     features = probe.shape[0]
@@ -276,56 +289,55 @@
             slab[pl.ds(first + 8, USED - 8), :] = values[8:USED]
         return start + counts_ref[shard] // LANES
 
-    last_heads = join_halves(core, relay_ref, 0, features, swapped_ref, 0, last_tokens, 0)
-    last_turned[...] = last_tokens[...].T
+    last_heads = join_halves(core, relay_ref, 0, features, swapped_ref, 0, tokens, last)
+    turned[:, last:] = tokens[last:, :].T
     parts = [(key_ref[at], attn_ref[at], back_ref[at], centred_ref[at]) for at in range(key_ref.shape[0])]
     parts.append(attention_part(last_heads))
-    lax.fori_loop(0, shards, place, jnp.int32(0), unroll=4)
-    for load in loads:
-        load.wait()
+    lax.fori_loop(0, shards, place, jnp.int32(0), unroll=16)
+    load_tokens.wait()
+    load_turned.start()
     probe[:, :LANES] = wide[:features, :].astype(jnp.bfloat16)
     probe[:, LANES:] = slim[:features, :].astype(jnp.bfloat16)
 
-    row = 0
-    for tokens_ref in (tokens, last_tokens):
-        count = tokens_ref.shape[0]
-        product = jnp.dot(tokens_ref[...], probe[...], preferred_element_type=jnp.float32)
-        wide_sum, slim_sum = product[:, :LANES], product[:, LANES:]
-        wide_sum = wide_sum + turn(wide_sum, HALF)
-        slim_sum = slim_sum + turn(slim_sum, HALF)
-        slim_sum = slim_sum + turn(slim_sum, QUARTER)
-        lane = lane_of(count)
-        ordered = jnp.where(
-            parity == 0,
-            jnp.where(lane < HALF, wide_sum, slim_sum),
-            jnp.where(lane < QUARTER, slim_sum, turn(wide_sum, QUARTER)),
-        )
-        tangent[row : row + count, :] = ordered.astype(jnp.bfloat16)
-        row += count
-
-    for at, (key_head, attn, back, centred) in enumerate(parts):
-        rows = slice(at * length, (at + 1) * length)
-        score_tangent = inv_root * times_transposed(tangent[rows, :], key_head)
-        mean_tangent = jnp.sum(attn * score_tangent, axis=1, keepdims=True)
-        weight_tangent = attn * (score_tangent - mean_tangent)
-        delta_tangent = jnp.sum(weight_tangent * back, axis=1, keepdims=True)
-        grad_tangent = (weight_tangent * centred - attn * delta_tangent).astype(jnp.bfloat16)
-        scaled = inv_root * jnp.dot(grad_tangent, key_head, preferred_element_type=jnp.float32)
+    product = jnp.dot(tokens[...], probe[...], preferred_element_type=jnp.float32)
+    wide_sum, slim_sum = product[:, :LANES], product[:, LANES:]
+    wide_sum = wide_sum + turn(wide_sum, HALF)
+    slim_sum = slim_sum + turn(slim_sum, HALF)
+    slim_sum = slim_sum + turn(slim_sum, QUARTER)
+    lane = lane_of(product.shape[0])
+    tangent = jnp.where(
+        parity == 0,
+        jnp.where(lane < HALF, wide_sum, slim_sum),
+        jnp.where(lane < QUARTER, slim_sum, turn(wide_sum, QUARTER)),
+    ).astype(jnp.bfloat16)
+
+    keys, attns, backs, centreds = zip(*parts)
+    cuts = [slice(at * length, (at + 1) * length) for at in range(len(parts))]
+    score_tangents = [inv_root * times_transposed(tangent[cut], key_head) for cut, key_head in zip(cuts, keys)]
+    means = [jnp.sum(attn * score, axis=1, keepdims=True) for attn, score in zip(attns, score_tangents)]
+    weights = [attn * (score - mean) for attn, score, mean in zip(attns, score_tangents, means)]
+    deltas = [jnp.sum(weight * back, axis=1, keepdims=True) for weight, back in zip(weights, backs)]
+    grads = [
+        (weight * centred - attn * delta).astype(jnp.bfloat16)
+        for weight, centred, attn, delta in zip(weights, centreds, attns, deltas)
+    ]
+    lane = lane_of(length)
+    for cut, grad, key_head in zip(cuts, grads, keys):
+        scaled = inv_root * jnp.dot(grad, key_head, preferred_element_type=jnp.float32)
         turns = [turn(scaled, at * QUARTER) for at in range(4)]
         wide_part = jnp.where(
             parity == 0,
-            jnp.where(lane_of(length) < HALF, scaled, turns[2]),
-            jnp.where(lane_of(length) < HALF, turns[3], turns[1]),
+            jnp.where(lane < HALF, scaled, turns[2]),
+            jnp.where(lane < HALF, turns[3], turns[1]),
         )
         slim_part = jnp.where(
             parity == 0, by_quarter([turns[2], turns[3], scaled, turns[1]]), by_quarter(turns)
         )
-        spread[rows, :LANES] = wide_part.astype(jnp.bfloat16)
-        spread[rows, LANES:] = slim_part.astype(jnp.bfloat16)
-
-    split = tokens.shape[0]
-    term = jnp.dot(turned[...], spread[:split, :], preferred_element_type=jnp.float32)
-    term += jnp.dot(last_turned[...], spread[split:, :], preferred_element_type=jnp.float32)
+        spread[cut, :LANES] = wide_part.astype(jnp.bfloat16)
+        spread[cut, LANES:] = slim_part.astype(jnp.bfloat16)
+
+    load_turned.wait()
+    term = jnp.dot(turned[...], spread[...], preferred_element_type=jnp.float32)
     wide[:features, :] = term[:, :LANES]
     slim[:features, :] = term[:, LANES:]
 
@@ -336,7 +348,7 @@
         out_ref[shard] = jnp.concatenate([pairs, quads], axis=0).astype(jnp.bfloat16)
         return start + counts_ref[shard] // LANES
 
-    lax.fori_loop(0, shards, cut_out, jnp.int32(0), unroll=4)
+    lax.fori_loop(0, shards, cut_out, jnp.int32(0), unroll=16)
 
 
 def add_groups(terms_ref, out_ref):
@@ -421,34 +433,30 @@
     def swap_cores(array):
         return lax.ppermute(array, "tensor", [(one, one ^ 1) for one in range(lax.axis_size("tensor"))])
 
-    keep, to_x, to_copy = call(
-        split_heads,
+    windows, keep, to_x, to_copy = call(
+        pack,
         [
+            ((shards, WINDOW, LANES), bf16),
             ((length, HEADS * HEAD), bf16),
             ((half, packed + features + packed), bf16),
             ((half, features + packed), bf16),
         ],
-        [SMEM] + [HBM] * 5,
-        (place, tokens, queries, key_rows, value_rows, cotangent),
-        8,
-        (pltpu.VMEM((HEADS, *queries.shape), bf16), pltpu.SemaphoreType.DMA((6,))),
-    )
-    from_x = lax.ppermute(to_x, "dp", [(one, one ^ ROW) for one in range(shards)])
-    from_copy = swap_copies(to_copy)
-
-    windows = call(
-        pack_shard,
-        [((shards, WINDOW, LANES), bf16)],
-        [SMEM, HBM, HBM],
-        (place, shard_counts, probe_shards),
-        8,
+        [SMEM] + [HBM] * 7,
+        (place, shard_counts, probe_shards, tokens, queries, key_rows, value_rows, cotangent),
+        12,
         (
             rows,
             pltpu.SMEM(shard_counts.shape, jnp.int32),
             pltpu.VMEM(probe_shards.shape, bf16),
-            pltpu.SemaphoreType.DMA((2,)),
+            pltpu.VMEM((shards, WINDOW, LANES), bf16),
+            pltpu.VMEM((HEADS, *queries.shape), bf16),
+            pltpu.SemaphoreType.DMA((9,)),
         ),
-    )
+        in_hbm=1,
+    )
+    from_x = lax.ppermute(to_x, "dp", [(one, one ^ ROW) for one in range(shards)])
+    from_copy = swap_copies(to_copy)
+
     pieces = lax.all_to_all(windows, "dp", 0, 0)
 
     relayed = swap_copies(from_x[:, packed:])
@@ -459,8 +467,6 @@
 
     square = ((3, length, length), f32)
     update_part = ((blocks, LANES), f32)
-    three_tokens = pltpu.VMEM((3 * length, features), bf16)
-    three_turned = pltpu.VMEM((features, 3 * length), bf16)
     all_tokens, all_turned, *parts, factor, base = call(
         prepare,
         [
@@ -477,8 +483,8 @@
         (place, tokens, probe_shards, hess_old, keep, from_x, from_copy, swapped),
         16,
         (
-            three_tokens,
-            three_turned,
+            pltpu.VMEM((3 * length, features), bf16),
+            pltpu.VMEM((features, 3 * length), bf16),
             pltpu.VMEM(probe_shards.shape, bf16),
             pltpu.VMEM(hess_old.shape, f32),
             pltpu.SemaphoreType.DMA((5,)),
@@ -495,12 +501,9 @@
             slab,
             slab,
             pltpu.VMEM((features, 2 * LANES), bf16),
-            pltpu.VMEM((4 * length, LANES), bf16),
             pltpu.VMEM((4 * length, 2 * LANES), bf16),
-            three_tokens,
-            three_turned,
-            pltpu.VMEM((length, features), bf16),
-            pltpu.VMEM((features, length), bf16),
+            pltpu.VMEM((4 * length, features), bf16),
+            pltpu.VMEM((features, 4 * length), bf16),
             pltpu.SemaphoreType.DMA((2,)),
         ),
     )

time: 101 us -> 98.2 us (0.972)
  the two profiles are of different devices: /device:TPU:260 before, /device:TPU:4 now
where the time goes in v4:
time: 98.2 us; the launch traced here: 97.8 us
  blocking collectives  39.7 us (40%)
  starting transfers between devices  28.9 us (29%)
  Pallas kernels  16 us (16%)
  waiting for transfers between devices  11.4 us (12%)
  local copies, waits for them, and re-layouts  1.39 us (1%)
    all_to_all x1, blocking collectives, body(): terms = lax.all_to_all(term_windows, 'dp', 0, 0)  34.9 us
    pallas_call x5, Pallas kernels, call(): pl.pallas_call(kernel, out_shape=shapes, in_specs=specs, out_specs=[HBM]...  16 us
    all_to_all x1, starting transfers between devices, body(): pieces = lax.all_to_all(windows, 'dp', 0, 0)  12.9 us
    ppermute x2, starting transfers between devices, swap_copies(): return lax.ppermute(array, 'replica', [(0, 1), (1, 0)])  8.81 us
    ppermute x2, waiting for transfers between devices, swap_copies(): return lax.ppermute(array, 'replica', [(0, 1), (1, 0)])  8.08 us
    all_gather x1, blocking collectives, body(): sums = lax.all_gather(summed, 'replica', axis=0)  4.77 us
    ppermute x2, starting transfers between devices, swap_cores(): lax.ppermute(array, 'tensor', [(one, one ^ 1) for one in range(lax.axis_s...  3.84 us
    ppermute x1, starting transfers between devices, body(): lax.ppermute(to_x, 'dp', [(one, one ^ ROW) for one in range(shards)])  3.43 us
  transfers between devices with their start and end apart: 6, of which 2 were waited for; matrix products, arithmetic and copies ran while one was open for 0% of the time, Pallas kernels for 4%

profile of v4, /device:TPU:4, one launch (start us, length us, event | category | flops | bytes accessed | tf_op | source)
XLA Modules:
  0.0 97.8 jit_solution(3736526365746839757)
XLA Ops:
  0.0 0.1 pad_add_fusion.place_ref
  0.1 2.8 %pack.1 = (bf16[64,48,128]{2,1,0:T(8,128)(2,1)}, bf16[128,384]{1,0:T(8,128)(2,1)S(1)}, bf16[64,4608]{1,0:T(8,128)(2,1)S(1)}, bf16[64,3840]{1,0:T(8,128)(2,1)S(1)}) custom-call(s32[4]{0:T(128)S(1)} %pad_add_fusion.place_ref, s32[64]{0:T(128)} %counts_ref.3, bf16[1,20736]{1,0:T(2,128)(2,1)} %probe_hbm.3, bf16[128,3072]{1,0:T(8,128)(2,1)} %tokens_hbm.3, ...), custom_call_target="tpu_custom_call" | custom-call | tf_op jit(solution)/shard_map/pack/pallas_call | solution.py:404
  2.9 3.4 %collective-permute-start = (bf16[64,4608]{1,0:T(8,128)(2,1)S(1)}, bf16[64,4608]{1,0:T(8,128)(2,1)S(1)}, u32[]{:S(2)}, u32[]{:S(2)}) collective-permute-start(bf16[64,4608]{1,0:T(8,128)(2,1)S(1)} %get-tuple-element.18), channel_id=1, source_target_pairs={{0,128},{16,144},{32,160},{48,176},{64,192},{80,208},{96,224},{112... | collective-permute-start | bytes 1769480 | tf_op jit(solution)/shard_map/ppermute | solution.py:457
  6.3 5.2 %collective-permute-start.1 = (bf16[64,3840]{1,0:T(8,128)(2,1)S(1)}, bf16[64,3840]{1,0:T(8,128)(2,1)S(1)}, u32[]{:S(2)}, u32[]{:S(2)}) collective-permute-start(bf16[64,3840]{1,0:T(8,128)(2,1)S(1)} %get-tuple-element.19), channel_id=1, source_target_pairs={{0,1},{1,0},{2,3},{3,2},{4,5},{5,4},{6,7},{7,6},{8,9},{9,8},{10,11... | collective-permute-start | bytes 1474568 | tf_op jit(solution)/shard_map/ppermute | solution.py:431
  11.5 12.9 %all-to-all-start = ((bf16[64,48,128]{2,1,0:T(8,128)(2,1)}), bf16[64,48,128]{2,1,0:T(8,128)(2,1)S(1)}, u32[]{:S(2)}, u32[]{:S(2)}) async-start(bf16[64,48,128]{2,1,0:T(8,128)(2,1)} %get-tuple-element.22), calls=%async_computation | async-start | bytes 1572864 | tf_op jit(solution)/shard_map/all_to_all | solution.py:460
  24.4 0.0 collective-permute-done.1.copy_ref
  24.4 0.0 collective-permute-done.x_ref
  24.5 3.6 %collective-permute-start.3 = (bf16[64,3840]{1,0:T(8,128)(2,1)S(1)}, bf16[64,3840]{1,0:T(8,128)(2,1)S(1)}, u32[]{:S(2)}, u32[]{:S(2)}) collective-permute-start(bf16[64,3840]{1,0:T(8,128)(2,1)S(1)} %slice.18), channel_id=1, source_target_pairs={{0,1},{1,0},{2,3},{3,2},{4,5},{5,4},{6,7},{7,6},{8,9},{9,8},{10,11... | collective-permute-start | bytes 1474568 | tf_op jit(solution)/shard_map/ppermute | solution.py:431
  28.1 0.1 pad_maximum_fusion
  28.2 1.9 %collective-permute-start.2 = (bf16[128,3072]{1,0:T(8,128)(2,1)S(1)}, bf16[128,3072]{1,0:T(8,128)(2,1)S(1)}, u32[]{:S(2)}, u32[]{:S(2)}) collective-permute-start(bf16[128,3072]{1,0:T(8,128)(2,1)S(1)} %pad_maximum_fusion), channel_id=1, source_target_pairs={{0,2},{2,0},{4,6},{6,4},{8,10},{10,8},{12,14},{14,12},{1,3},{3,1},... | collective-permute-start | bytes 2359304 | tf_op jit(solution)/shard_map/ppermute | solution.py:434
  30.1 8.1 %collective-permute-done.3.relay_ref = bf16[64,3840]{1,0:T(8,128)(2,1)S(1)} collective-permute-done((bf16[64,3840]{1,0:T(8,128)(2,1)S(1)}, bf16[64,3840]{1,0:T(8,128)(2,1)S(1)}, u32[]{:S(2)}, u32[]{:S(2)}) %collective-permute-start.3) | collective-permute-done | bytes 491552 | tf_op jit(solution)/shard_map/ppermute | solution.py:431
  38.2 0.0 copy-start.4
  38.2 1.9 %collective-permute-start.4 = (bf16[64,3072]{1,0:T(8,128)(2,1)S(1)}, bf16[64,3072]{1,0:T(8,128)(2,1)S(1)}, u32[]{:S(2)}, u32[]{:S(2)}) collective-permute-start(bf16[64,3072]{1,0:T(8,128)(2,1)S(1)} %slice.19), channel_id=1, source_target_pairs={{0,2},{2,0},{4,6},{6,4},{8,10},{10,8},{12,14},{14,12},{1,3},{3,1},... | collective-permute-start | bytes 1179656 | tf_op jit(solution)/shard_map/ppermute | solution.py:434
  40.2 0.0 collective-permute-done.2.swapped_ref
  40.2 3.9 %prepare.1 = (bf16[384,3072]{1,0:T(8,128)(2,1)}, bf16[3072,384]{1,0:T(8,128)(2,1)}, bf16[3,128,128]{2,1,0:T(8,128)(2,1)S(1)}, f32[3,128,128]{2,1,0:T(8,128)S(1)}...) custom-call(s32[4]{0:T(128)S(1)} %pad_add_fusion.place_ref, ...), custom_call_target="tpu_custom_call" | custom-call | tf_op jit(solution)/shard_map/prepare/pallas_call | solution.py:404
  44.1 0.0 copy-start
  44.1 0.6 copy-done
  44.7 0.0 copy-start.2
  44.7 0.6 copy-done.2
  45.4 0.0 collective-permute-done.4.swapped_ref
  45.4 3.3 %all-to-all-done.pieces_ref = bf16[64,48,128]{2,1,0:T(8,128)(2,1)S(1)} async-done(((bf16[64,48,128]{2,1,0:T(8,128)(2,1)}), bf16[64,48,128]{2,1,0:T(8,128)(2,1)S(1)}, u32[]{:S(2)}, u32[]{:S(2)}) %all-to-all-start) | async-done | bytes 786464 | tf_op jit(solution)/shard_map/all_to_all | solution.py:460
  48.7 0.0 copy-done.4
  48.7 7.4 %middle_part.1 = bf16[64,48,128]{2,1,0:T(8,128)(2,1)S(1)} custom-call(s32[4]{0:T(128)S(1)} %pad_add_fusion.place_ref, s32[64]{0:T(128)S(1)} %copy-done.4, bf16[384,3072]{1,0:T(8,128)(2,1)} %get-tuple-element.20.tokens_hbm, bf16[3072,384]{1,0:T(8,128)(2,1)} %get-tuple-element.21.turned_hbm, bf16[64,48,128]{2,1,0:T(8,128)(2,1)S(1)} %all-to-all-done.pieces_ref, ...), custom_call_target="tpu_custom_call" | custom-call | tf_op jit(solution)/shard_map/middle_part/pallas_call | solution.py:404
  56.1 0.0 copy-start.1
  56.1 0.0 copy-start.3
  56.1 34.9 %all_to_all.10.terms_ref = bf16[64,48,128]{2,1,0:T(8,128)(2,1)S(1)} all-to-all(bf16[64,48,128]{2,1,0:T(8,128)(2,1)S(1)} %middle_part.1), channel_id=1, replica_groups=mesh['dp'=64,'tensor'=8,'replica'=2] {'dp'}, dimensions={0} | all-to-all | bytes 1572864 | tf_op jit(solution)/shard_map/all_to_all | solution.py:510
  91.1 0.4 add_groups.1
  91.5 4.8 %all-gather = f32[192,128]{1,0:T(8,128)S(1)} all-gather(f32[96,128]{1,0:T(8,128)S(1)} %add_groups.1), channel_id=2, replica_groups=mesh['dp'=64,'tensor'=8,'replica'=2] {'replica'}, dimensions={0}, use_global_device_ids=true | all-gather | bytes 147456 | tf_op jit(solution)/shard_map/all_gather | solution.py:512
  96.3 0.0 copy-done.1
  96.3 0.0 copy-done.3
  96.3 1.5 %update_shard.1 = f32[1,20736]{1,0:T(1,128)} custom-call(s32[4]{0:T(128)S(1)} %pad_add_fusion.place_ref, s32[64]{0:T(128)S(1)} %copy-done.4, f32[2,96,128]{2,1,0:T(8,128)S(1)} %bitcast.5, f32[162,128]{1,0:T(8,128)S(1)} %copy-done.1, f32[162,128]{1,0:T(8,128)S(1)} %copy-done.3), custom_call_target="tpu_custom_call" | custom-call | tf_op jit(solution)/shard_map/update_shard/pallas_call | solution.py:404
  (4 shorter events, 0.1 us)
Async XLA Ops:
  2.9 21.6 %collective-permute-start = (bf16[64,4608]{1,0:T(8,128)(2,1)S(1)}, bf16[64,4608]{1,0:T(8,128)(2,1)S(1)}, u32[]{:S(2)}, u32[]{:S(2)}) collective-permute-start(bf16[64,4608]{1,0:T(8,128)(2,1)S(1)} %get-tuple-element.18), channel_id=1, source_target_pairs={{0,128},{16,144},{32,160},{48,176},{64,192},{80,208},{96,224},{112... | collective-permute-start | bytes 1769480 | tf_op jit(solution)/shard_map/ppermute | solution.py:457
  6.3 18.1 %collective-permute-start.1 = (bf16[64,3840]{1,0:T(8,128)(2,1)S(1)}, bf16[64,3840]{1,0:T(8,128)(2,1)S(1)}, u32[]{:S(2)}, u32[]{:S(2)}) collective-permute-start(bf16[64,3840]{1,0:T(8,128)(2,1)S(1)} %get-tuple-element.19), channel_id=1, source_target_pairs={{0,1},{1,0},{2,3},{3,2},{4,5},{5,4},{6,7},{7,6},{8,9},{9,8},{10,11... | collective-permute-start | bytes 1474568 | tf_op jit(solution)/shard_map/ppermute | solution.py:431
  11.5 37.2 %all-to-all-start = ((bf16[64,48,128]{2,1,0:T(8,128)(2,1)}), bf16[64,48,128]{2,1,0:T(8,128)(2,1)S(1)}, u32[]{:S(2)}, u32[]{:S(2)}) async-start(bf16[64,48,128]{2,1,0:T(8,128)(2,1)} %get-tuple-element.22), calls=%async_computation | async-start | bytes 1572864 | tf_op jit(solution)/shard_map/all_to_all | solution.py:460
  24.5 13.7 %collective-permute-start.3 = (bf16[64,3840]{1,0:T(8,128)(2,1)S(1)}, bf16[64,3840]{1,0:T(8,128)(2,1)S(1)}, u32[]{:S(2)}, u32[]{:S(2)}) collective-permute-start(bf16[64,3840]{1,0:T(8,128)(2,1)S(1)} %slice.18), channel_id=1, source_target_pairs={{0,1},{1,0},{2,3},{3,2},{4,5},{5,4},{6,7},{7,6},{8,9},{9,8},{10,11... | collective-permute-start | bytes 1474568 | tf_op jit(solution)/shard_map/ppermute | solution.py:431
  28.2 12.0 %collective-permute-start.2 = (bf16[128,3072]{1,0:T(8,128)(2,1)S(1)}, bf16[128,3072]{1,0:T(8,128)(2,1)S(1)}, u32[]{:S(2)}, u32[]{:S(2)}) collective-permute-start(bf16[128,3072]{1,0:T(8,128)(2,1)S(1)} %pad_maximum_fusion), channel_id=1, source_target_pairs={{0,2},{2,0},{4,6},{6,4},{8,10},{10,8},{12,14},{14,12},{1,3},{3,1},... | collective-permute-start | bytes 2359304 | tf_op jit(solution)/shard_map/ppermute | solution.py:434
  38.2 10.5 %copy-start.4 = (s32[64]{0:T(128)S(1)}, s32[64]{0:T(128)}, u32[]{:S(2)}) copy-start(s32[64]{0:T(128)} %counts_ref.3) | copy-start | bytes 772
  38.2 7.1 %collective-permute-start.4 = (bf16[64,3072]{1,0:T(8,128)(2,1)S(1)}, bf16[64,3072]{1,0:T(8,128)(2,1)S(1)}, u32[]{:S(2)}, u32[]{:S(2)}) collective-permute-start(bf16[64,3072]{1,0:T(8,128)(2,1)S(1)} %slice.19), channel_id=1, source_target_pairs={{0,2},{2,0},{4,6},{6,4},{8,10},{10,8},{12,14},{14,12},{1,3},{3,1},... | collective-permute-start | bytes 1179656 | tf_op jit(solution)/shard_map/ppermute | solution.py:434
  44.1 0.6 copy-start
  44.7 0.6 copy-start.2
  56.1 40.2 %copy-start.1 = (f32[162,128]{1,0:T(8,128)S(1)}, f32[162,128]{1,0:T(8,128)}, u32[]{:S(2)}) copy-start(f32[162,128]{1,0:T(8,128)} %copy-done) | copy-start | bytes 248836
  56.1 40.1 %copy-start.3 = (f32[162,128]{1,0:T(8,128)S(1)}, f32[162,128]{1,0:T(8,128)}, u32[]{:S(2)}) copy-start(f32[162,128]{1,0:T(8,128)} %copy-done.2) | copy-start | bytes 248836

commit v5 on v4

--- a/solution.py
+++ b/solution.py
@@ -293,13 +293,20 @@
     turned[:, last:] = tokens[last:, :].T
     parts = [(key_ref[at], attn_ref[at], back_ref[at], centred_ref[at]) for at in range(key_ref.shape[0])]
     parts.append(attention_part(last_heads))
-    lax.fori_loop(0, shards, place, jnp.int32(0), unroll=16)
+    lax.fori_loop(0, shards, place, jnp.int32(0), unroll=8)
     load_tokens.wait()
     load_turned.start()
     probe[:, :LANES] = wide[:features, :].astype(jnp.bfloat16)
     probe[:, LANES:] = slim[:features, :].astype(jnp.bfloat16)
 
-    product = jnp.dot(tokens[...], probe[...], preferred_element_type=jnp.float32)
+    side = tokens.shape[0] // 2
+    product = jnp.concatenate(
+        [
+            jnp.dot(tokens[at * side : (at + 1) * side, :], probe[...], preferred_element_type=jnp.float32)
+            for at in range(2)
+        ],
+        axis=0,
+    )
     wide_sum, slim_sum = product[:, :LANES], product[:, LANES:]
     wide_sum = wide_sum + turn(wide_sum, HALF)
     slim_sum = slim_sum + turn(slim_sum, HALF)

time: 98.2 us -> 96.6 us (0.984)
  the two profiles are of different devices: /device:TPU:4 before, /device:TPU:260 now
where the time goes in v5:
time: 96.6 us; the launch traced here: 96.2 us
  blocking collectives  39.7 us (41%)
  starting transfers between devices  27.2 us (28%)
  Pallas kernels  14.4 us (15%)
  waiting for transfers between devices  13.1 us (14%)
  local copies, waits for them, and re-layouts  1.39 us (1%)
    all_to_all x1, blocking collectives, body(): terms = lax.all_to_all(term_windows, 'dp', 0, 0)  34.9 us
    pallas_call x5, Pallas kernels, call(): pl.pallas_call(kernel, out_shape=shapes, in_specs=specs, out_specs=[HBM]...  14.4 us
    all_to_all x1, starting transfers between devices, body(): pieces = lax.all_to_all(windows, 'dp', 0, 0)  12.9 us
    ppermute x2, waiting for transfers between devices, swap_copies(): return lax.ppermute(array, 'replica', [(0, 1), (1, 0)])  9.78 us
    ppermute x2, starting transfers between devices, swap_copies(): return lax.ppermute(array, 'replica', [(0, 1), (1, 0)])  7.11 us
    all_gather x1, blocking collectives, body(): sums = lax.all_gather(summed, 'replica', axis=0)  4.77 us
    ppermute x2, starting transfers between devices, swap_cores(): lax.ppermute(array, 'tensor', [(one, one ^ 1) for one in range(lax.axis_s...  3.84 us
    ppermute x1, starting transfers between devices, body(): lax.ppermute(to_x, 'dp', [(one, one ^ ROW) for one in range(shards)])  3.43 us
  transfers between devices with their start and end apart: 6, of which 2 were waited for; matrix products, arithmetic and copies ran while one was open for 0% of the time, Pallas kernels for 4%

profile of v5, /device:TPU:260, one launch (start us, length us, event | category | flops | bytes accessed | tf_op | source)
XLA Modules:
  0.0 96.2 jit_solution(2070408624118763546)
XLA Ops:
  0.0 0.1 pad_add_fusion.place_ref
  0.1 2.8 %pack.1 = (bf16[64,48,128]{2,1,0:T(8,128)(2,1)}, bf16[128,384]{1,0:T(8,128)(2,1)S(1)}, bf16[64,4608]{1,0:T(8,128)(2,1)S(1)}, bf16[64,3840]{1,0:T(8,128)(2,1)S(1)}) custom-call(s32[4]{0:T(128)S(1)} %pad_add_fusion.place_ref, s32[64]{0:T(128)} %counts_ref.3, bf16[1,20736]{1,0:T(2,128)(2,1)} %probe_hbm.3, bf16[128,3072]{1,0:T(8,128)(2,1)} %tokens_hbm.3, ...), custom_call_target="tpu_custom_call" | custom-call | tf_op jit(solution)/shard_map/pack/pallas_call | solution.py:411
  2.9 3.4 %collective-permute-start = (bf16[64,4608]{1,0:T(8,128)(2,1)S(1)}, bf16[64,4608]{1,0:T(8,128)(2,1)S(1)}, u32[]{:S(2)}, u32[]{:S(2)}) collective-permute-start(bf16[64,4608]{1,0:T(8,128)(2,1)S(1)} %get-tuple-element.18), channel_id=1, source_target_pairs={{0,128},{16,144},{32,160},{48,176},{64,192},{80,208},{96,224},{112... | collective-permute-start | bytes 1769480 | tf_op jit(solution)/shard_map/ppermute | solution.py:464
  6.3 5.2 %collective-permute-start.1 = (bf16[64,3840]{1,0:T(8,128)(2,1)S(1)}, bf16[64,3840]{1,0:T(8,128)(2,1)S(1)}, u32[]{:S(2)}, u32[]{:S(2)}) collective-permute-start(bf16[64,3840]{1,0:T(8,128)(2,1)S(1)} %get-tuple-element.19), channel_id=1, source_target_pairs={{0,1},{1,0},{2,3},{3,2},{4,5},{5,4},{6,7},{7,6},{8,9},{9,8},{10,11... | collective-permute-start | bytes 1474568 | tf_op jit(solution)/shard_map/ppermute | solution.py:438
  11.5 12.9 %all-to-all-start = ((bf16[64,48,128]{2,1,0:T(8,128)(2,1)}), bf16[64,48,128]{2,1,0:T(8,128)(2,1)S(1)}, u32[]{:S(2)}, u32[]{:S(2)}) async-start(bf16[64,48,128]{2,1,0:T(8,128)(2,1)} %get-tuple-element.22), calls=%async_computation | async-start | bytes 1572864 | tf_op jit(solution)/shard_map/all_to_all | solution.py:467
  24.4 0.0 collective-permute-done.1.copy_ref
  24.4 0.0 collective-permute-done.x_ref
  24.5 1.9 %collective-permute-start.3 = (bf16[64,3840]{1,0:T(8,128)(2,1)S(1)}, bf16[64,3840]{1,0:T(8,128)(2,1)S(1)}, u32[]{:S(2)}, u32[]{:S(2)}) collective-permute-start(bf16[64,3840]{1,0:T(8,128)(2,1)S(1)} %slice.18), channel_id=1, source_target_pairs={{0,1},{1,0},{2,3},{3,2},{4,5},{5,4},{6,7},{7,6},{8,9},{9,8},{10,11... | collective-permute-start | bytes 1474568 | tf_op jit(solution)/shard_map/ppermute | solution.py:438
  26.4 0.1 pad_maximum_fusion
  26.5 1.9 %collective-permute-start.2 = (bf16[128,3072]{1,0:T(8,128)(2,1)S(1)}, bf16[128,3072]{1,0:T(8,128)(2,1)S(1)}, u32[]{:S(2)}, u32[]{:S(2)}) collective-permute-start(bf16[128,3072]{1,0:T(8,128)(2,1)S(1)} %pad_maximum_fusion), channel_id=1, source_target_pairs={{0,2},{2,0},{4,6},{6,4},{8,10},{10,8},{12,14},{14,12},{1,3},{3,1},... | collective-permute-start | bytes 2359304 | tf_op jit(solution)/shard_map/ppermute | solution.py:441
  28.4 9.8 %collective-permute-done.3.relay_ref = bf16[64,3840]{1,0:T(8,128)(2,1)S(1)} collective-permute-done((bf16[64,3840]{1,0:T(8,128)(2,1)S(1)}, bf16[64,3840]{1,0:T(8,128)(2,1)S(1)}, u32[]{:S(2)}, u32[]{:S(2)}) %collective-permute-start.3) | collective-permute-done | bytes 491552 | tf_op jit(solution)/shard_map/ppermute | solution.py:438
  38.2 0.0 copy-start.4
  38.2 1.9 %collective-permute-start.4 = (bf16[64,3072]{1,0:T(8,128)(2,1)S(1)}, bf16[64,3072]{1,0:T(8,128)(2,1)S(1)}, u32[]{:S(2)}, u32[]{:S(2)}) collective-permute-start(bf16[64,3072]{1,0:T(8,128)(2,1)S(1)} %slice.19), channel_id=1, source_target_pairs={{0,2},{2,0},{4,6},{6,4},{8,10},{10,8},{12,14},{14,12},{1,3},{3,1},... | collective-permute-start | bytes 1179656 | tf_op jit(solution)/shard_map/ppermute | solution.py:441
  40.2 0.0 collective-permute-done.2.swapped_ref
  40.2 3.9 %prepare.1 = (bf16[384,3072]{1,0:T(8,128)(2,1)}, bf16[3072,384]{1,0:T(8,128)(2,1)}, bf16[3,128,128]{2,1,0:T(8,128)(2,1)S(1)}, f32[3,128,128]{2,1,0:T(8,128)S(1)}...) custom-call(s32[4]{0:T(128)S(1)} %pad_add_fusion.place_ref, ...), custom_call_target="tpu_custom_call" | custom-call | tf_op jit(solution)/shard_map/prepare/pallas_call | solution.py:411
  44.1 0.0 copy-start
  44.1 0.6 copy-done
  44.7 0.0 copy-start.2
  44.8 0.6 copy-done.2
  45.4 0.0 collective-permute-done.4.swapped_ref
  45.4 3.3 %all-to-all-done.pieces_ref = bf16[64,48,128]{2,1,0:T(8,128)(2,1)S(1)} async-done(((bf16[64,48,128]{2,1,0:T(8,128)(2,1)}), bf16[64,48,128]{2,1,0:T(8,128)(2,1)S(1)}, u32[]{:S(2)}, u32[]{:S(2)}) %all-to-all-start) | async-done | bytes 786464 | tf_op jit(solution)/shard_map/all_to_all | solution.py:467
  48.7 0.0 copy-done.4
  48.7 5.7 %middle_part.1 = bf16[64,48,128]{2,1,0:T(8,128)(2,1)S(1)} custom-call(s32[4]{0:T(128)S(1)} %pad_add_fusion.place_ref, s32[64]{0:T(128)S(1)} %copy-done.4, bf16[384,3072]{1,0:T(8,128)(2,1)} %get-tuple-element.20.tokens_hbm, bf16[3072,384]{1,0:T(8,128)(2,1)} %get-tuple-element.21.turned_hbm, bf16[64,48,128]{2,1,0:T(8,128)(2,1)S(1)} %all-to-all-done.pieces_ref, ...), custom_call_target="tpu_custom_call" | custom-call | tf_op jit(solution)/shard_map/middle_part/pallas_call | solution.py:411
  54.5 0.0 copy-start.1
  54.5 0.0 copy-start.3
  54.5 34.9 %all_to_all.10.terms_ref = bf16[64,48,128]{2,1,0:T(8,128)(2,1)S(1)} all-to-all(bf16[64,48,128]{2,1,0:T(8,128)(2,1)S(1)} %middle_part.1), channel_id=1, replica_groups=mesh['dp'=64,'tensor'=8,'replica'=2] {'dp'}, dimensions={0} | all-to-all | bytes 1572864 | tf_op jit(solution)/shard_map/all_to_all | solution.py:517
  89.4 0.4 add_groups.1
  89.9 4.8 %all-gather = f32[192,128]{1,0:T(8,128)S(1)} all-gather(f32[96,128]{1,0:T(8,128)S(1)} %add_groups.1), channel_id=2, replica_groups=mesh['dp'=64,'tensor'=8,'replica'=2] {'replica'}, dimensions={0}, use_global_device_ids=true | all-gather | bytes 147456 | tf_op jit(solution)/shard_map/all_gather | solution.py:519
  94.6 0.0 copy-done.1
  94.6 0.0 copy-done.3
  94.6 1.5 %update_shard.1 = f32[1,20736]{1,0:T(1,128)} custom-call(s32[4]{0:T(128)S(1)} %pad_add_fusion.place_ref, s32[64]{0:T(128)S(1)} %copy-done.4, f32[2,96,128]{2,1,0:T(8,128)S(1)} %bitcast.5, f32[162,128]{1,0:T(8,128)S(1)} %copy-done.1, f32[162,128]{1,0:T(8,128)S(1)} %copy-done.3), custom_call_target="tpu_custom_call" | custom-call | tf_op jit(solution)/shard_map/update_shard/pallas_call | solution.py:411
  (4 shorter events, 0.1 us)
Async XLA Ops:
  2.9 21.6 %collective-permute-start = (bf16[64,4608]{1,0:T(8,128)(2,1)S(1)}, bf16[64,4608]{1,0:T(8,128)(2,1)S(1)}, u32[]{:S(2)}, u32[]{:S(2)}) collective-permute-start(bf16[64,4608]{1,0:T(8,128)(2,1)S(1)} %get-tuple-element.18), channel_id=1, source_target_pairs={{0,128},{16,144},{32,160},{48,176},{64,192},{80,208},{96,224},{112... | collective-permute-start | bytes 1769480 | tf_op jit(solution)/shard_map/ppermute | solution.py:464
  6.3 18.1 %collective-permute-start.1 = (bf16[64,3840]{1,0:T(8,128)(2,1)S(1)}, bf16[64,3840]{1,0:T(8,128)(2,1)S(1)}, u32[]{:S(2)}, u32[]{:S(2)}) collective-permute-start(bf16[64,3840]{1,0:T(8,128)(2,1)S(1)} %get-tuple-element.19), channel_id=1, source_target_pairs={{0,1},{1,0},{2,3},{3,2},{4,5},{5,4},{6,7},{7,6},{8,9},{9,8},{10,11... | collective-permute-start | bytes 1474568 | tf_op jit(solution)/shard_map/ppermute | solution.py:438
  11.5 37.2 %all-to-all-start = ((bf16[64,48,128]{2,1,0:T(8,128)(2,1)}), bf16[64,48,128]{2,1,0:T(8,128)(2,1)S(1)}, u32[]{:S(2)}, u32[]{:S(2)}) async-start(bf16[64,48,128]{2,1,0:T(8,128)(2,1)} %get-tuple-element.22), calls=%async_computation | async-start | bytes 1572864 | tf_op jit(solution)/shard_map/all_to_all | solution.py:467
  24.5 13.7 %collective-permute-start.3 = (bf16[64,3840]{1,0:T(8,128)(2,1)S(1)}, bf16[64,3840]{1,0:T(8,128)(2,1)S(1)}, u32[]{:S(2)}, u32[]{:S(2)}) collective-permute-start(bf16[64,3840]{1,0:T(8,128)(2,1)S(1)} %slice.18), channel_id=1, source_target_pairs={{0,1},{1,0},{2,3},{3,2},{4,5},{5,4},{6,7},{7,6},{8,9},{9,8},{10,11... | collective-permute-start | bytes 1474568 | tf_op jit(solution)/shard_map/ppermute | solution.py:438
  26.5 13.7 %collective-permute-start.2 = (bf16[128,3072]{1,0:T(8,128)(2,1)S(1)}, bf16[128,3072]{1,0:T(8,128)(2,1)S(1)}, u32[]{:S(2)}, u32[]{:S(2)}) collective-permute-start(bf16[128,3072]{1,0:T(8,128)(2,1)S(1)} %pad_maximum_fusion), channel_id=1, source_target_pairs={{0,2},{2,0},{4,6},{6,4},{8,10},{10,8},{12,14},{14,12},{1,3},{3,1},... | collective-permute-start | bytes 2359304 | tf_op jit(solution)/shard_map/ppermute | solution.py:441
  38.2 10.5 %copy-start.4 = (s32[64]{0:T(128)S(1)}, s32[64]{0:T(128)}, u32[]{:S(2)}) copy-start(s32[64]{0:T(128)} %counts_ref.3) | copy-start | bytes 772
  38.2 7.1 %collective-permute-start.4 = (bf16[64,3072]{1,0:T(8,128)(2,1)S(1)}, bf16[64,3072]{1,0:T(8,128)(2,1)S(1)}, u32[]{:S(2)}, u32[]{:S(2)}) collective-permute-start(bf16[64,3072]{1,0:T(8,128)(2,1)S(1)} %slice.19), channel_id=1, source_target_pairs={{0,2},{2,0},{4,6},{6,4},{8,10},{10,8},{12,14},{14,12},{1,3},{3,1},... | collective-permute-start | bytes 1179656 | tf_op jit(solution)/shard_map/ppermute | solution.py:441
  44.1 0.6 copy-start
  44.7 0.6 copy-start.2
  54.5 40.2 %copy-start.1 = (f32[162,128]{1,0:T(8,128)S(1)}, f32[162,128]{1,0:T(8,128)}, u32[]{:S(2)}) copy-start(f32[162,128]{1,0:T(8,128)} %copy-done) | copy-start | bytes 248836
  54.5 40.2 %copy-start.3 = (f32[162,128]{1,0:T(8,128)S(1)}, f32[162,128]{1,0:T(8,128)}, u32[]{:S(2)}) copy-start(f32[162,128]{1,0:T(8,128)} %copy-done.2) | copy-start | bytes 248836

commit v6 on v5

--- a/solution.py
+++ b/solution.py
@@ -193,14 +193,16 @@
     swapped_ref,
     tokens_out,
     turned_out,
+    factor_out,
+    base_out,
     key_ref,
     attn_ref,
     back_ref,
     centred_ref,
+    tokens_ref,
+    turned_ref,
     factor_ref,
     base_ref,
-    tokens_ref,
-    turned_ref,
     probe_ref,
     hess_ref,
     sems,
@@ -224,18 +226,22 @@
     stores = [
         pltpu.make_async_copy(tokens_ref, tokens_out, sems.at[3]),
         pltpu.make_async_copy(turned_ref, turned_out, sems.at[4]),
+        pltpu.make_async_copy(factor_ref, factor_out, sems.at[5]),
+        pltpu.make_async_copy(base_ref, base_out, sems.at[6]),
     ]
     stores[0].start()
     turned_ref[...] = tokens_ref[...].T
     stores[1].start()
-    for at, heads in enumerate(heads_of):
-        key_ref[at], attn_ref[at], back_ref[at], centred_ref[at] = attention_part(heads)
     for load in loads[1:]:
         load.wait()
     for block in range(probe_ref.shape[1] // LANES):
         lanes = slice(block * LANES, (block + 1) * LANES)
         factor_ref[block : block + 1, :] = (1.0 - decay_rate) * probe_ref[0:1, lanes].astype(jnp.float32)
         base_ref[block : block + 1, :] = decay_rate * hess_ref[0:1, lanes]
+    for store in stores[2:]:
+        store.start()
+    for at, heads in enumerate(heads_of):
+        key_ref[at], attn_ref[at], back_ref[at], centred_ref[at] = attention_part(heads)
     for store in stores:
         store.wait()
 
@@ -470,21 +476,19 @@
     swapped = swap_cores(
         jnp.concatenate([from_x[:, packed : packed + features], from_copy[:, :features]], axis=0)
     )
-    swapped_last = swap_cores(relayed[:, :features])
-
     square = ((3, length, length), f32)
     update_part = ((blocks, LANES), f32)
-    all_tokens, all_turned, *parts, factor, base = call(
+    all_tokens, all_turned, factor, base, *parts = call(
         prepare,
         [
             ((3 * length, features), bf16),
             ((features, 3 * length), bf16),
+            update_part,
+            update_part,
             ((3, length, LANES), bf16),
             square,
             square,
             square,
-            update_part,
-            update_part,
         ],
         [SMEM, HBM, HBM, HBM],
         (place, tokens, probe_shards, hess_old, keep, from_x, from_copy, swapped),
@@ -492,12 +496,15 @@
         (
             pltpu.VMEM((3 * length, features), bf16),
             pltpu.VMEM((features, 3 * length), bf16),
+            pltpu.VMEM((blocks, LANES), f32),
+            pltpu.VMEM((blocks, LANES), f32),
             pltpu.VMEM(probe_shards.shape, bf16),
             pltpu.VMEM(hess_old.shape, f32),
-            pltpu.SemaphoreType.DMA((5,)),
+            pltpu.SemaphoreType.DMA((7,)),
         ),
-        in_hbm=2,
-    )
+        in_hbm=4,
+    )
+    swapped_last = swap_cores(relayed[:, :features])
     term_windows = call(
         middle_part,
         [((shards, WINDOW, LANES), bf16)],

time: 96.6 us -> 95.3 us (0.987)
  blocking collectives: 39.7 us -> 38.4 us
  waiting for transfers between devices: 13.1 us -> 14.4 us
  local copies, waits for them, and re-layouts: 1.39 us -> 0.13 us
    all_to_all x1, waiting for transfers between devices: 3.33 us -> 4.62 us  [body(): pieces = lax.all_to_all(windows, 'dp', 0, 0)]
    all_to_all x1, blocking collectives: 34.9 us -> 33.6 us  [body(): terms = lax.all_to_all(term_windows, 'dp', 0, 0)]
    unnamed x10 -> x6, local copies, waits for them, and re-layouts: 1.28 us -> 0.01 us
where the time goes in v6:
time: 95.3 us; the launch traced here: 94.9 us
  blocking collectives  38.4 us (40%)
  starting transfers between devices  27.2 us (29%)
  Pallas kernels  14.4 us (15%)
  waiting for transfers between devices  14.4 us (15%)
    all_to_all x1, blocking collectives, body(): terms = lax.all_to_all(term_windows, 'dp', 0, 0)  33.6 us
    pallas_call x5, Pallas kernels, call(): pl.pallas_call(kernel, out_shape=shapes, in_specs=specs, out_specs=[HBM]...  14.4 us
    all_to_all x1, starting transfers between devices, body(): pieces = lax.all_to_all(windows, 'dp', 0, 0)  12.9 us
    ppermute x2, waiting for transfers between devices, swap_copies(): return lax.ppermute(array, 'replica', [(0, 1), (1, 0)])  9.78 us
    ppermute x2, starting transfers between devices, swap_copies(): return lax.ppermute(array, 'replica', [(0, 1), (1, 0)])  7.1 us
    all_gather x1, blocking collectives, body(): sums = lax.all_gather(summed, 'replica', axis=0)  4.77 us
    all_to_all x1, waiting for transfers between devices, body(): pieces = lax.all_to_all(windows, 'dp', 0, 0)  4.62 us
    ppermute x2, starting transfers between devices, swap_cores(): lax.ppermute(array, 'tensor', [(one, one ^ 1) for one in range(lax.axis_s...  3.84 us
  transfers between devices with their start and end apart: 6, of which 2 were waited for; matrix products, arithmetic and copies ran while one was open for 0% of the time, Pallas kernels for 4%

profile of v6, /device:TPU:260, one launch (start us, length us, event | category | flops | bytes accessed | tf_op | source)
XLA Modules:
  0.0 94.9 jit_solution(3917385337412995830)
XLA Ops:
  0.0 0.1 pad_add_fusion.place_ref
  0.1 2.8 %pack.1 = (bf16[64,48,128]{2,1,0:T(8,128)(2,1)}, bf16[128,384]{1,0:T(8,128)(2,1)S(1)}, bf16[64,4608]{1,0:T(8,128)(2,1)S(1)}, bf16[64,3840]{1,0:T(8,128)(2,1)S(1)}) custom-call(s32[4]{0:T(128)S(1)} %pad_add_fusion.place_ref, s32[64]{0:T(128)} %counts_ref.3, bf16[1,20736]{1,0:T(2,128)(2,1)} %probe_hbm.3, bf16[128,3072]{1,0:T(8,128)(2,1)} %tokens_hbm.3, ...), custom_call_target="tpu_custom_call" | custom-call | tf_op jit(solution)/shard_map/pack/pallas_call | solution.py:417
  2.9 3.4 %collective-permute-start = (bf16[64,4608]{1,0:T(8,128)(2,1)S(1)}, bf16[64,4608]{1,0:T(8,128)(2,1)S(1)}, u32[]{:S(2)}, u32[]{:S(2)}) collective-permute-start(bf16[64,4608]{1,0:T(8,128)(2,1)S(1)} %get-tuple-element.18), channel_id=1, source_target_pairs={{0,128},{16,144},{32,160},{48,176},{64,192},{80,208},{96,224},{112... | collective-permute-start | bytes 1769480 | tf_op jit(solution)/shard_map/ppermute | solution.py:470
  6.3 5.2 %collective-permute-start.1 = (bf16[64,3840]{1,0:T(8,128)(2,1)S(1)}, bf16[64,3840]{1,0:T(8,128)(2,1)S(1)}, u32[]{:S(2)}, u32[]{:S(2)}) collective-permute-start(bf16[64,3840]{1,0:T(8,128)(2,1)S(1)} %get-tuple-element.19), channel_id=1, source_target_pairs={{0,1},{1,0},{2,3},{3,2},{4,5},{5,4},{6,7},{7,6},{8,9},{9,8},{10,11... | collective-permute-start | bytes 1474568 | tf_op jit(solution)/shard_map/ppermute | solution.py:444
  11.5 12.9 %all-to-all-start = ((bf16[64,48,128]{2,1,0:T(8,128)(2,1)}), bf16[64,48,128]{2,1,0:T(8,128)(2,1)S(1)}, u32[]{:S(2)}, u32[]{:S(2)}) async-start(bf16[64,48,128]{2,1,0:T(8,128)(2,1)} %get-tuple-element.22), calls=%async_computation | async-start | bytes 1572864 | tf_op jit(solution)/shard_map/all_to_all | solution.py:473
  24.4 0.0 collective-permute-done.1.copy_ref
  24.4 0.0 collective-permute-done.x_ref
  24.5 1.9 %collective-permute-start.3 = (bf16[64,3840]{1,0:T(8,128)(2,1)S(1)}, bf16[64,3840]{1,0:T(8,128)(2,1)S(1)}, u32[]{:S(2)}, u32[]{:S(2)}) collective-permute-start(bf16[64,3840]{1,0:T(8,128)(2,1)S(1)} %slice.18), channel_id=1, source_target_pairs={{0,1},{1,0},{2,3},{3,2},{4,5},{5,4},{6,7},{7,6},{8,9},{9,8},{10,11... | collective-permute-start | bytes 1474568 | tf_op jit(solution)/shard_map/ppermute | solution.py:444
  26.4 0.1 pad_maximum_fusion
  26.5 1.9 %collective-permute-start.2 = (bf16[128,3072]{1,0:T(8,128)(2,1)S(1)}, bf16[128,3072]{1,0:T(8,128)(2,1)S(1)}, u32[]{:S(2)}, u32[]{:S(2)}) collective-permute-start(bf16[128,3072]{1,0:T(8,128)(2,1)S(1)} %pad_maximum_fusion), channel_id=1, source_target_pairs={{0,2},{2,0},{4,6},{6,4},{8,10},{10,8},{12,14},{14,12},{1,3},{3,1},... | collective-permute-start | bytes 2359304 | tf_op jit(solution)/shard_map/ppermute | solution.py:447
  28.4 9.8 %collective-permute-done.3.relay_ref = bf16[64,3840]{1,0:T(8,128)(2,1)S(1)} collective-permute-done((bf16[64,3840]{1,0:T(8,128)(2,1)S(1)}, bf16[64,3840]{1,0:T(8,128)(2,1)S(1)}, u32[]{:S(2)}, u32[]{:S(2)}) %collective-permute-start.3) | collective-permute-done | bytes 491552 | tf_op jit(solution)/shard_map/ppermute | solution.py:444
  38.2 0.0 copy-start.2
  38.2 1.9 %collective-permute-start.4 = (bf16[64,3072]{1,0:T(8,128)(2,1)S(1)}, bf16[64,3072]{1,0:T(8,128)(2,1)S(1)}, u32[]{:S(2)}, u32[]{:S(2)}) collective-permute-start(bf16[64,3072]{1,0:T(8,128)(2,1)S(1)} %slice.19), channel_id=1, source_target_pairs={{0,2},{2,0},{4,6},{6,4},{8,10},{10,8},{12,14},{14,12},{1,3},{3,1},... | collective-permute-start | bytes 1179656 | tf_op jit(solution)/shard_map/ppermute | solution.py:447
  40.2 0.0 collective-permute-done.2.swapped_ref
  40.2 3.9 %prepare.1 = (bf16[384,3072]{1,0:T(8,128)(2,1)}, bf16[3072,384]{1,0:T(8,128)(2,1)}, f32[162,128]{1,0:T(8,128)}, f32[162,128]{1,0:T(8,128)}, bf16[3,128,128]{2,1,...) custom-call(s32[4]{0:T(128)S(1)} %pad_add_fusion.place_ref, ...), custom_call_target="tpu_custom_call" | custom-call | tf_op jit(solution)/shard_map/prepare/pallas_call | solution.py:417
  44.1 0.0 collective-permute-done.4.swapped_ref
  44.1 4.6 %all-to-all-done.pieces_ref = bf16[64,48,128]{2,1,0:T(8,128)(2,1)S(1)} async-done(((bf16[64,48,128]{2,1,0:T(8,128)(2,1)}), bf16[64,48,128]{2,1,0:T(8,128)(2,1)S(1)}, u32[]{:S(2)}, u32[]{:S(2)}) %all-to-all-start) | async-done | bytes 786464 | tf_op jit(solution)/shard_map/all_to_all | solution.py:473
  48.7 0.0 copy-done.2
  48.7 5.7 %middle_part.1 = bf16[64,48,128]{2,1,0:T(8,128)(2,1)S(1)} custom-call(s32[4]{0:T(128)S(1)} %pad_add_fusion.place_ref, s32[64]{0:T(128)S(1)} %copy-done.2, bf16[384,3072]{1,0:T(8,128)(2,1)} %get-tuple-element.20.tokens_hbm, bf16[3072,384]{1,0:T(8,128)(2,1)} %get-tuple-element.21.turned_hbm, bf16[64,48,128]{2,1,0:T(8,128)(2,1)S(1)} %all-to-all-done.pieces_ref, ...), custom_call_target="tpu_custom_call" | custom-call | tf_op jit(solution)/shard_map/middle_part/pallas_call | solution.py:417
  54.5 0.0 copy-start
  54.5 0.0 copy-start.1
  54.5 33.6 %all_to_all.10.terms_ref = bf16[64,48,128]{2,1,0:T(8,128)(2,1)S(1)} all-to-all(bf16[64,48,128]{2,1,0:T(8,128)(2,1)S(1)} %middle_part.1), channel_id=1, replica_groups=mesh['dp'=64,'tensor'=8,'replica'=2] {'dp'}, dimensions={0} | all-to-all | bytes 1572864 | tf_op jit(solution)/shard_map/all_to_all | solution.py:524
  88.1 0.4 add_groups.1
  88.6 4.8 %all-gather = f32[192,128]{1,0:T(8,128)S(1)} all-gather(f32[96,128]{1,0:T(8,128)S(1)} %add_groups.1), channel_id=2, replica_groups=mesh['dp'=64,'tensor'=8,'replica'=2] {'replica'}, dimensions={0}, use_global_device_ids=true | all-gather | bytes 147456 | tf_op jit(solution)/shard_map/all_gather | solution.py:526
  93.3 0.0 copy-done
  93.3 0.0 copy-done.1
  93.3 1.5 %update_shard.1 = f32[1,20736]{1,0:T(1,128)} custom-call(s32[4]{0:T(128)S(1)} %pad_add_fusion.place_ref, s32[64]{0:T(128)S(1)} %copy-done.2, f32[2,96,128]{2,1,0:T(8,128)S(1)} %bitcast.5, f32[162,128]{1,0:T(8,128)S(1)} %copy-done, f32[162,128]{1,0:T(8,128)S(1)} %copy-done.1), custom_call_target="tpu_custom_call" | custom-call | tf_op jit(solution)/shard_map/update_shard/pallas_call | solution.py:417
  (4 shorter events, 0.1 us)
Async XLA Ops:
  2.9 21.6 %collective-permute-start = (bf16[64,4608]{1,0:T(8,128)(2,1)S(1)}, bf16[64,4608]{1,0:T(8,128)(2,1)S(1)}, u32[]{:S(2)}, u32[]{:S(2)}) collective-permute-start(bf16[64,4608]{1,0:T(8,128)(2,1)S(1)} %get-tuple-element.18), channel_id=1, source_target_pairs={{0,128},{16,144},{32,160},{48,176},{64,192},{80,208},{96,224},{112... | collective-permute-start | bytes 1769480 | tf_op jit(solution)/shard_map/ppermute | solution.py:470
  6.3 18.1 %collective-permute-start.1 = (bf16[64,3840]{1,0:T(8,128)(2,1)S(1)}, bf16[64,3840]{1,0:T(8,128)(2,1)S(1)}, u32[]{:S(2)}, u32[]{:S(2)}) collective-permute-start(bf16[64,3840]{1,0:T(8,128)(2,1)S(1)} %get-tuple-element.19), channel_id=1, source_target_pairs={{0,1},{1,0},{2,3},{3,2},{4,5},{5,4},{6,7},{7,6},{8,9},{9,8},{10,11... | collective-permute-start | bytes 1474568 | tf_op jit(solution)/shard_map/ppermute | solution.py:444
  11.5 37.2 %all-to-all-start = ((bf16[64,48,128]{2,1,0:T(8,128)(2,1)}), bf16[64,48,128]{2,1,0:T(8,128)(2,1)S(1)}, u32[]{:S(2)}, u32[]{:S(2)}) async-start(bf16[64,48,128]{2,1,0:T(8,128)(2,1)} %get-tuple-element.22), calls=%async_computation | async-start | bytes 1572864 | tf_op jit(solution)/shard_map/all_to_all | solution.py:473
  24.5 13.7 %collective-permute-start.3 = (bf16[64,3840]{1,0:T(8,128)(2,1)S(1)}, bf16[64,3840]{1,0:T(8,128)(2,1)S(1)}, u32[]{:S(2)}, u32[]{:S(2)}) collective-permute-start(bf16[64,3840]{1,0:T(8,128)(2,1)S(1)} %slice.18), channel_id=1, source_target_pairs={{0,1},{1,0},{2,3},{3,2},{4,5},{5,4},{6,7},{7,6},{8,9},{9,8},{10,11... | collective-permute-start | bytes 1474568 | tf_op jit(solution)/shard_map/ppermute | solution.py:444
  26.5 13.7 %collective-permute-start.2 = (bf16[128,3072]{1,0:T(8,128)(2,1)S(1)}, bf16[128,3072]{1,0:T(8,128)(2,1)S(1)}, u32[]{:S(2)}, u32[]{:S(2)}) collective-permute-start(bf16[128,3072]{1,0:T(8,128)(2,1)S(1)} %pad_maximum_fusion), channel_id=1, source_target_pairs={{0,2},{2,0},{4,6},{6,4},{8,10},{10,8},{12,14},{14,12},{1,3},{3,1},... | collective-permute-start | bytes 2359304 | tf_op jit(solution)/shard_map/ppermute | solution.py:447
  38.2 10.5 %copy-start.2 = (s32[64]{0:T(128)S(1)}, s32[64]{0:T(128)}, u32[]{:S(2)}) copy-start(s32[64]{0:T(128)} %counts_ref.3) | copy-start | bytes 772
  38.2 5.8 %collective-permute-start.4 = (bf16[64,3072]{1,0:T(8,128)(2,1)S(1)}, bf16[64,3072]{1,0:T(8,128)(2,1)S(1)}, u32[]{:S(2)}, u32[]{:S(2)}) collective-permute-start(bf16[64,3072]{1,0:T(8,128)(2,1)S(1)} %slice.19), channel_id=1, source_target_pairs={{0,2},{2,0},{4,6},{6,4},{8,10},{10,8},{12,14},{14,12},{1,3},{3,1},... | collective-permute-start | bytes 1179656 | tf_op jit(solution)/shard_map/ppermute | solution.py:447
  54.5 38.9 %copy-start = (f32[162,128]{1,0:T(8,128)S(1)}, f32[162,128]{1,0:T(8,128)}, u32[]{:S(2)}) copy-start(f32[162,128]{1,0:T(8,128)} %get-tuple-element.27.factor_ref) | copy-start | bytes 248836
  54.5 38.9 %copy-start.1 = (f32[162,128]{1,0:T(8,128)S(1)}, f32[162,128]{1,0:T(8,128)}, u32[]{:S(2)}) copy-start(f32[162,128]{1,0:T(8,128)} %get-tuple-element.28.base_ref) | copy-start | bytes 248836

commit v7 on v6

--- a/solution.py
+++ b/solution.py
@@ -222,6 +222,7 @@
         join_halves(core, x_ref, packed, 0, swapped_ref, 0, tokens_ref, length),
         join_halves(core, copy_ref, 0, features, swapped_ref, x_ref.shape[0], tokens_ref, 2 * length),
     ]
+    key_ref[0], attn_ref[0], back_ref[0], centred_ref[0] = attention_part(heads_of[0])
     loads[0].wait()
     stores = [
         pltpu.make_async_copy(tokens_ref, tokens_out, sems.at[3]),
@@ -240,7 +241,7 @@
         base_ref[block : block + 1, :] = decay_rate * hess_ref[0:1, lanes]
     for store in stores[2:]:
         store.start()
-    for at, heads in enumerate(heads_of):
+    for at, heads in list(enumerate(heads_of))[1:]:
         key_ref[at], attn_ref[at], back_ref[at], centred_ref[at] = attention_part(heads)
     for store in stores:
         store.wait()

time: 95.3 us -> 95.3 us (level)
  no operation moved by 1% of the time
where the time goes in v7:
time: 95.3 us; the launch traced here: 94.9 us
  blocking collectives  38.4 us (40%)
  starting transfers between devices  27.2 us (29%)
  Pallas kernels  14.4 us (15%)
  waiting for transfers between devices  14.4 us (15%)
    all_to_all x1, blocking collectives, body(): terms = lax.all_to_all(term_windows, 'dp', 0, 0)  33.7 us
    pallas_call x5, Pallas kernels, call(): pl.pallas_call(kernel, out_shape=shapes, in_specs=specs, out_specs=[HBM]...  14.4 us
    all_to_all x1, starting transfers between devices, body(): pieces = lax.all_to_all(windows, 'dp', 0, 0)  12.9 us
    ppermute x2, waiting for transfers between devices, swap_copies(): return lax.ppermute(array, 'replica', [(0, 1), (1, 0)])  9.78 us
    ppermute x2, starting transfers between devices, swap_copies(): return lax.ppermute(array, 'replica', [(0, 1), (1, 0)])  7.1 us
    all_gather x1, blocking collectives, body(): sums = lax.all_gather(summed, 'replica', axis=0)  4.77 us
    all_to_all x1, waiting for transfers between devices, body(): pieces = lax.all_to_all(windows, 'dp', 0, 0)  4.61 us
    ppermute x2, starting transfers between devices, swap_cores(): lax.ppermute(array, 'tensor', [(one, one ^ 1) for one in range(lax.axis_s...  3.84 us
  transfers between devices with their start and end apart: 6, of which 2 were waited for; matrix products, arithmetic and copies ran while one was open for 0% of the time, Pallas kernels for 4%

profile of v7, /device:TPU:260, one launch (start us, length us, event | category | flops | bytes accessed | tf_op | source)
XLA Modules:
  0.0 94.9 jit_solution(4330279839197913499)
XLA Ops:
  0.0 0.1 pad_add_fusion.place_ref
  0.1 2.8 %pack.1 = (bf16[64,48,128]{2,1,0:T(8,128)(2,1)}, bf16[128,384]{1,0:T(8,128)(2,1)S(1)}, bf16[64,4608]{1,0:T(8,128)(2,1)S(1)}, bf16[64,3840]{1,0:T(8,128)(2,1)S(1)}) custom-call(s32[4]{0:T(128)S(1)} %pad_add_fusion.place_ref, s32[64]{0:T(128)} %counts_ref.3, bf16[1,20736]{1,0:T(2,128)(2,1)} %probe_hbm.3, bf16[128,3072]{1,0:T(8,128)(2,1)} %tokens_hbm.3, ...), custom_call_target="tpu_custom_call" | custom-call | tf_op jit(solution)/shard_map/pack/pallas_call | solution.py:418
  2.9 3.4 %collective-permute-start = (bf16[64,4608]{1,0:T(8,128)(2,1)S(1)}, bf16[64,4608]{1,0:T(8,128)(2,1)S(1)}, u32[]{:S(2)}, u32[]{:S(2)}) collective-permute-start(bf16[64,4608]{1,0:T(8,128)(2,1)S(1)} %get-tuple-element.18), channel_id=1, source_target_pairs={{0,128},{16,144},{32,160},{48,176},{64,192},{80,208},{96,224},{112... | collective-permute-start | bytes 1769480 | tf_op jit(solution)/shard_map/ppermute | solution.py:471
  6.3 5.2 %collective-permute-start.1 = (bf16[64,3840]{1,0:T(8,128)(2,1)S(1)}, bf16[64,3840]{1,0:T(8,128)(2,1)S(1)}, u32[]{:S(2)}, u32[]{:S(2)}) collective-permute-start(bf16[64,3840]{1,0:T(8,128)(2,1)S(1)} %get-tuple-element.19), channel_id=1, source_target_pairs={{0,1},{1,0},{2,3},{3,2},{4,5},{5,4},{6,7},{7,6},{8,9},{9,8},{10,11... | collective-permute-start | bytes 1474568 | tf_op jit(solution)/shard_map/ppermute | solution.py:445
  11.5 12.9 %all-to-all-start = ((bf16[64,48,128]{2,1,0:T(8,128)(2,1)}), bf16[64,48,128]{2,1,0:T(8,128)(2,1)S(1)}, u32[]{:S(2)}, u32[]{:S(2)}) async-start(bf16[64,48,128]{2,1,0:T(8,128)(2,1)} %get-tuple-element.22), calls=%async_computation | async-start | bytes 1572864 | tf_op jit(solution)/shard_map/all_to_all | solution.py:474
  24.4 0.0 collective-permute-done.1.copy_ref
  24.4 0.0 collective-permute-done.x_ref
  24.5 1.9 %collective-permute-start.3 = (bf16[64,3840]{1,0:T(8,128)(2,1)S(1)}, bf16[64,3840]{1,0:T(8,128)(2,1)S(1)}, u32[]{:S(2)}, u32[]{:S(2)}) collective-permute-start(bf16[64,3840]{1,0:T(8,128)(2,1)S(1)} %slice.18), channel_id=1, source_target_pairs={{0,1},{1,0},{2,3},{3,2},{4,5},{5,4},{6,7},{7,6},{8,9},{9,8},{10,11... | collective-permute-start | bytes 1474568 | tf_op jit(solution)/shard_map/ppermute | solution.py:445
  26.4 0.1 pad_maximum_fusion
  26.5 1.9 %collective-permute-start.2 = (bf16[128,3072]{1,0:T(8,128)(2,1)S(1)}, bf16[128,3072]{1,0:T(8,128)(2,1)S(1)}, u32[]{:S(2)}, u32[]{:S(2)}) collective-permute-start(bf16[128,3072]{1,0:T(8,128)(2,1)S(1)} %pad_maximum_fusion), channel_id=1, source_target_pairs={{0,2},{2,0},{4,6},{6,4},{8,10},{10,8},{12,14},{14,12},{1,3},{3,1},... | collective-permute-start | bytes 2359304 | tf_op jit(solution)/shard_map/ppermute | solution.py:448
  28.4 9.8 %collective-permute-done.3.relay_ref = bf16[64,3840]{1,0:T(8,128)(2,1)S(1)} collective-permute-done((bf16[64,3840]{1,0:T(8,128)(2,1)S(1)}, bf16[64,3840]{1,0:T(8,128)(2,1)S(1)}, u32[]{:S(2)}, u32[]{:S(2)}) %collective-permute-start.3) | collective-permute-done | bytes 491552 | tf_op jit(solution)/shard_map/ppermute | solution.py:445
  38.2 0.0 copy-start.2
  38.2 1.9 %collective-permute-start.4 = (bf16[64,3072]{1,0:T(8,128)(2,1)S(1)}, bf16[64,3072]{1,0:T(8,128)(2,1)S(1)}, u32[]{:S(2)}, u32[]{:S(2)}) collective-permute-start(bf16[64,3072]{1,0:T(8,128)(2,1)S(1)} %slice.19), channel_id=1, source_target_pairs={{0,2},{2,0},{4,6},{6,4},{8,10},{10,8},{12,14},{14,12},{1,3},{3,1},... | collective-permute-start | bytes 1179656 | tf_op jit(solution)/shard_map/ppermute | solution.py:448
  40.2 0.0 collective-permute-done.2.swapped_ref
  40.2 3.9 %prepare.1 = (bf16[384,3072]{1,0:T(8,128)(2,1)}, bf16[3072,384]{1,0:T(8,128)(2,1)}, f32[162,128]{1,0:T(8,128)}, f32[162,128]{1,0:T(8,128)}, bf16[3,128,128]{2,1,...) custom-call(s32[4]{0:T(128)S(1)} %pad_add_fusion.place_ref, ...), custom_call_target="tpu_custom_call" | custom-call | tf_op jit(solution)/shard_map/prepare/pallas_call | solution.py:418
  44.1 0.0 collective-permute-done.4.swapped_ref
  44.1 4.6 %all-to-all-done.pieces_ref = bf16[64,48,128]{2,1,0:T(8,128)(2,1)S(1)} async-done(((bf16[64,48,128]{2,1,0:T(8,128)(2,1)}), bf16[64,48,128]{2,1,0:T(8,128)(2,1)S(1)}, u32[]{:S(2)}, u32[]{:S(2)}) %all-to-all-start) | async-done | bytes 786464 | tf_op jit(solution)/shard_map/all_to_all | solution.py:474
  48.7 0.0 copy-done.2
  48.7 5.7 %middle_part.1 = bf16[64,48,128]{2,1,0:T(8,128)(2,1)S(1)} custom-call(s32[4]{0:T(128)S(1)} %pad_add_fusion.place_ref, s32[64]{0:T(128)S(1)} %copy-done.2, bf16[384,3072]{1,0:T(8,128)(2,1)} %get-tuple-element.20.tokens_hbm, bf16[3072,384]{1,0:T(8,128)(2,1)} %get-tuple-element.21.turned_hbm, bf16[64,48,128]{2,1,0:T(8,128)(2,1)S(1)} %all-to-all-done.pieces_ref, ...), custom_call_target="tpu_custom_call" | custom-call | tf_op jit(solution)/shard_map/middle_part/pallas_call | solution.py:418
  54.5 0.0 copy-start
  54.5 0.0 copy-start.1
  54.5 33.7 %all_to_all.10.terms_ref = bf16[64,48,128]{2,1,0:T(8,128)(2,1)S(1)} all-to-all(bf16[64,48,128]{2,1,0:T(8,128)(2,1)S(1)} %middle_part.1), channel_id=1, replica_groups=mesh['dp'=64,'tensor'=8,'replica'=2] {'dp'}, dimensions={0} | all-to-all | bytes 1572864 | tf_op jit(solution)/shard_map/all_to_all | solution.py:525
  88.1 0.4 add_groups.1
  88.6 4.8 %all-gather = f32[192,128]{1,0:T(8,128)S(1)} all-gather(f32[96,128]{1,0:T(8,128)S(1)} %add_groups.1), channel_id=2, replica_groups=mesh['dp'=64,'tensor'=8,'replica'=2] {'replica'}, dimensions={0}, use_global_device_ids=true | all-gather | bytes 147456 | tf_op jit(solution)/shard_map/all_gather | solution.py:527
  93.4 0.0 copy-done
  93.4 0.0 copy-done.1
  93.4 1.5 %update_shard.1 = f32[1,20736]{1,0:T(1,128)} custom-call(s32[4]{0:T(128)S(1)} %pad_add_fusion.place_ref, s32[64]{0:T(128)S(1)} %copy-done.2, f32[2,96,128]{2,1,0:T(8,128)S(1)} %bitcast.5, f32[162,128]{1,0:T(8,128)S(1)} %copy-done, f32[162,128]{1,0:T(8,128)S(1)} %copy-done.1), custom_call_target="tpu_custom_call" | custom-call | tf_op jit(solution)/shard_map/update_shard/pallas_call | solution.py:418
  (4 shorter events, 0.1 us)
Async XLA Ops:
  2.9 21.6 %collective-permute-start = (bf16[64,4608]{1,0:T(8,128)(2,1)S(1)}, bf16[64,4608]{1,0:T(8,128)(2,1)S(1)}, u32[]{:S(2)}, u32[]{:S(2)}) collective-permute-start(bf16[64,4608]{1,0:T(8,128)(2,1)S(1)} %get-tuple-element.18), channel_id=1, source_target_pairs={{0,128},{16,144},{32,160},{48,176},{64,192},{80,208},{96,224},{112... | collective-permute-start | bytes 1769480 | tf_op jit(solution)/shard_map/ppermute | solution.py:471
  6.3 18.1 %collective-permute-start.1 = (bf16[64,3840]{1,0:T(8,128)(2,1)S(1)}, bf16[64,3840]{1,0:T(8,128)(2,1)S(1)}, u32[]{:S(2)}, u32[]{:S(2)}) collective-permute-start(bf16[64,3840]{1,0:T(8,128)(2,1)S(1)} %get-tuple-element.19), channel_id=1, source_target_pairs={{0,1},{1,0},{2,3},{3,2},{4,5},{5,4},{6,7},{7,6},{8,9},{9,8},{10,11... | collective-permute-start | bytes 1474568 | tf_op jit(solution)/shard_map/ppermute | solution.py:445
  11.5 37.2 %all-to-all-start = ((bf16[64,48,128]{2,1,0:T(8,128)(2,1)}), bf16[64,48,128]{2,1,0:T(8,128)(2,1)S(1)}, u32[]{:S(2)}, u32[]{:S(2)}) async-start(bf16[64,48,128]{2,1,0:T(8,128)(2,1)} %get-tuple-element.22), calls=%async_computation | async-start | bytes 1572864 | tf_op jit(solution)/shard_map/all_to_all | solution.py:474
  24.5 13.7 %collective-permute-start.3 = (bf16[64,3840]{1,0:T(8,128)(2,1)S(1)}, bf16[64,3840]{1,0:T(8,128)(2,1)S(1)}, u32[]{:S(2)}, u32[]{:S(2)}) collective-permute-start(bf16[64,3840]{1,0:T(8,128)(2,1)S(1)} %slice.18), channel_id=1, source_target_pairs={{0,1},{1,0},{2,3},{3,2},{4,5},{5,4},{6,7},{7,6},{8,9},{9,8},{10,11... | collective-permute-start | bytes 1474568 | tf_op jit(solution)/shard_map/ppermute | solution.py:445
  26.5 13.7 %collective-permute-start.2 = (bf16[128,3072]{1,0:T(8,128)(2,1)S(1)}, bf16[128,3072]{1,0:T(8,128)(2,1)S(1)}, u32[]{:S(2)}, u32[]{:S(2)}) collective-permute-start(bf16[128,3072]{1,0:T(8,128)(2,1)S(1)} %pad_maximum_fusion), channel_id=1, source_target_pairs={{0,2},{2,0},{4,6},{6,4},{8,10},{10,8},{12,14},{14,12},{1,3},{3,1},... | collective-permute-start | bytes 2359304 | tf_op jit(solution)/shard_map/ppermute | solution.py:448
  38.2 10.5 %copy-start.2 = (s32[64]{0:T(128)S(1)}, s32[64]{0:T(128)}, u32[]{:S(2)}) copy-start(s32[64]{0:T(128)} %counts_ref.3) | copy-start | bytes 772
  38.2 5.9 %collective-permute-start.4 = (bf16[64,3072]{1,0:T(8,128)(2,1)S(1)}, bf16[64,3072]{1,0:T(8,128)(2,1)S(1)}, u32[]{:S(2)}, u32[]{:S(2)}) collective-permute-start(bf16[64,3072]{1,0:T(8,128)(2,1)S(1)} %slice.19), channel_id=1, source_target_pairs={{0,2},{2,0},{4,6},{6,4},{8,10},{10,8},{12,14},{14,12},{1,3},{3,1},... | collective-permute-start | bytes 1179656 | tf_op jit(solution)/shard_map/ppermute | solution.py:448
  54.5 38.9 %copy-start = (f32[162,128]{1,0:T(8,128)S(1)}, f32[162,128]{1,0:T(8,128)}, u32[]{:S(2)}) copy-start(f32[162,128]{1,0:T(8,128)} %get-tuple-element.27.factor_ref) | copy-start | bytes 248836
  54.5 38.9 %copy-start.1 = (f32[162,128]{1,0:T(8,128)S(1)}, f32[162,128]{1,0:T(8,128)}, u32[]{:S(2)}) copy-start(f32[162,128]{1,0:T(8,128)} %get-tuple-element.28.base_ref) | copy-start | bytes 248836

commit v8 on v7

--- a/solution.py
+++ b/solution.py
@@ -116,16 +116,17 @@
         def _():
             even, odd = window(2 * which), window(2 * which + 1)
 
-            def store(at, carry):
-                first = at // ROW * 2 * ROW + lax.rem(at, ROW)
-                windows[first] = even
-                windows[first + ROW] = odd
-                return carry
-
-            lax.fori_loop(0, windows.shape[0] // 2, store, 0, unroll=4)
-
-    leave = pltpu.make_async_copy(windows, windows_hbm, sems.at[8])
-    leave.start()
+            for at in range(ROW):
+                windows[at] = even
+                windows[ROW + at] = odd
+
+    pair = 2 * ROW
+    leaves = [
+        pltpu.make_async_copy(windows, windows_hbm.at[pl.ds(at * pair, pair)], sems.at[8 + at])
+        for at in range(windows_hbm.shape[0] // pair)
+    ]
+    for leave in leaves:
+        leave.start()
     for load in head_loads:
         load.wait()
 
@@ -147,7 +148,8 @@
 
     for load in token_loads:
         load.wait()
-    leave.wait()
+    for leave in leaves:
+        leave.wait()
 
 
 def attention_part(heads):
@@ -462,9 +464,9 @@
             rows,
             pltpu.SMEM(shard_counts.shape, jnp.int32),
             pltpu.VMEM(probe_shards.shape, bf16),
-            pltpu.VMEM((shards, WINDOW, LANES), bf16),
+            pltpu.VMEM((2 * ROW, WINDOW, LANES), bf16),
             pltpu.VMEM((HEADS, *queries.shape), bf16),
-            pltpu.SemaphoreType.DMA((9,)),
+            pltpu.SemaphoreType.DMA((8 + shards // (2 * ROW),)),
         ),
         in_hbm=1,
     )

time: 95.3 us -> 95.2 us (level)
  the two profiles are of different devices: /device:TPU:260 before, /device:TPU:4 now
where the time goes in v8:
time: 95.2 us; the launch traced here: 94.7 us
  blocking collectives  38.4 us (40%)
  starting transfers between devices  28.9 us (30%)
  Pallas kernels  14.2 us (15%)
  waiting for transfers between devices  12.7 us (13%)
    all_to_all x1, blocking collectives, body(): terms = lax.all_to_all(term_windows, 'dp', 0, 0)  33.6 us
    pallas_call x5, Pallas kernels, call(): pl.pallas_call(kernel, out_shape=shapes, in_specs=specs, out_specs=[HBM]...  14.2 us
    all_to_all x1, starting transfers between devices, body(): pieces = lax.all_to_all(windows, 'dp', 0, 0)  12.9 us
    ppermute x2, starting transfers between devices, swap_copies(): return lax.ppermute(array, 'replica', [(0, 1), (1, 0)])  8.81 us
    ppermute x2, waiting for transfers between devices, swap_copies(): return lax.ppermute(array, 'replica', [(0, 1), (1, 0)])  8.08 us
    all_gather x1, blocking collectives, body(): sums = lax.all_gather(summed, 'replica', axis=0)  4.77 us
    all_to_all x1, waiting for transfers between devices, body(): pieces = lax.all_to_all(windows, 'dp', 0, 0)  4.61 us
    ppermute x2, starting transfers between devices, swap_cores(): lax.ppermute(array, 'tensor', [(one, one ^ 1) for one in range(lax.axis_s...  3.84 us
  transfers between devices with their start and end apart: 6, of which 2 were waited for; matrix products, arithmetic and copies ran while one was open for 0% of the time, Pallas kernels for 4%

profile of v8, /device:TPU:4, one launch (start us, length us, event | category | flops | bytes accessed | tf_op | source)
XLA Modules:
  0.0 94.7 jit_solution(9017591909322656434)
XLA Ops:
  0.0 0.1 pad_add_fusion.place_ref
  0.1 2.6 %pack.1 = (bf16[64,48,128]{2,1,0:T(8,128)(2,1)}, bf16[128,384]{1,0:T(8,128)(2,1)S(1)}, bf16[64,4608]{1,0:T(8,128)(2,1)S(1)}, bf16[64,3840]{1,0:T(8,128)(2,1)S(1)}) custom-call(s32[4]{0:T(128)S(1)} %pad_add_fusion.place_ref, s32[64]{0:T(128)} %counts_ref.3, bf16[1,20736]{1,0:T(2,128)(2,1)} %probe_hbm.3, bf16[128,3072]{1,0:T(8,128)(2,1)} %tokens_hbm.3, ...), custom_call_target="tpu_custom_call" | custom-call | tf_op jit(solution)/shard_map/pack/pallas_call | solution.py:420
  2.7 3.4 %collective-permute-start = (bf16[64,4608]{1,0:T(8,128)(2,1)S(1)}, bf16[64,4608]{1,0:T(8,128)(2,1)S(1)}, u32[]{:S(2)}, u32[]{:S(2)}) collective-permute-start(bf16[64,4608]{1,0:T(8,128)(2,1)S(1)} %get-tuple-element.18), channel_id=1, source_target_pairs={{0,128},{16,144},{32,160},{48,176},{64,192},{80,208},{96,224},{112... | collective-permute-start | bytes 1769480 | tf_op jit(solution)/shard_map/ppermute | solution.py:473
  6.1 5.2 %collective-permute-start.1 = (bf16[64,3840]{1,0:T(8,128)(2,1)S(1)}, bf16[64,3840]{1,0:T(8,128)(2,1)S(1)}, u32[]{:S(2)}, u32[]{:S(2)}) collective-permute-start(bf16[64,3840]{1,0:T(8,128)(2,1)S(1)} %get-tuple-element.19), channel_id=1, source_target_pairs={{0,1},{1,0},{2,3},{3,2},{4,5},{5,4},{6,7},{7,6},{8,9},{9,8},{10,11... | collective-permute-start | bytes 1474568 | tf_op jit(solution)/shard_map/ppermute | solution.py:447
  11.3 12.9 %all-to-all-start = ((bf16[64,48,128]{2,1,0:T(8,128)(2,1)}), bf16[64,48,128]{2,1,0:T(8,128)(2,1)S(1)}, u32[]{:S(2)}, u32[]{:S(2)}) async-start(bf16[64,48,128]{2,1,0:T(8,128)(2,1)} %get-tuple-element.22), calls=%async_computation | async-start | bytes 1572864 | tf_op jit(solution)/shard_map/all_to_all | solution.py:476
  24.2 0.0 collective-permute-done.1.copy_ref
  24.2 0.0 collective-permute-done.x_ref
  24.3 3.6 %collective-permute-start.3 = (bf16[64,3840]{1,0:T(8,128)(2,1)S(1)}, bf16[64,3840]{1,0:T(8,128)(2,1)S(1)}, u32[]{:S(2)}, u32[]{:S(2)}) collective-permute-start(bf16[64,3840]{1,0:T(8,128)(2,1)S(1)} %slice.18), channel_id=1, source_target_pairs={{0,1},{1,0},{2,3},{3,2},{4,5},{5,4},{6,7},{7,6},{8,9},{9,8},{10,11... | collective-permute-start | bytes 1474568 | tf_op jit(solution)/shard_map/ppermute | solution.py:447
  28.0 0.1 pad_maximum_fusion
  28.0 1.9 %collective-permute-start.2 = (bf16[128,3072]{1,0:T(8,128)(2,1)S(1)}, bf16[128,3072]{1,0:T(8,128)(2,1)S(1)}, u32[]{:S(2)}, u32[]{:S(2)}) collective-permute-start(bf16[128,3072]{1,0:T(8,128)(2,1)S(1)} %pad_maximum_fusion), channel_id=1, source_target_pairs={{0,2},{2,0},{4,6},{6,4},{8,10},{10,8},{12,14},{14,12},{1,3},{3,1},... | collective-permute-start | bytes 2359304 | tf_op jit(solution)/shard_map/ppermute | solution.py:450
  29.9 8.1 %collective-permute-done.3.relay_ref = bf16[64,3840]{1,0:T(8,128)(2,1)S(1)} collective-permute-done((bf16[64,3840]{1,0:T(8,128)(2,1)S(1)}, bf16[64,3840]{1,0:T(8,128)(2,1)S(1)}, u32[]{:S(2)}, u32[]{:S(2)}) %collective-permute-start.3) | collective-permute-done | bytes 491552 | tf_op jit(solution)/shard_map/ppermute | solution.py:447
  38.1 0.0 copy-start.2
  38.1 1.9 %collective-permute-start.4 = (bf16[64,3072]{1,0:T(8,128)(2,1)S(1)}, bf16[64,3072]{1,0:T(8,128)(2,1)S(1)}, u32[]{:S(2)}, u32[]{:S(2)}) collective-permute-start(bf16[64,3072]{1,0:T(8,128)(2,1)S(1)} %slice.19), channel_id=1, source_target_pairs={{0,2},{2,0},{4,6},{6,4},{8,10},{10,8},{12,14},{14,12},{1,3},{3,1},... | collective-permute-start | bytes 1179656 | tf_op jit(solution)/shard_map/ppermute | solution.py:450
  40.0 0.0 collective-permute-done.2.swapped_ref
  40.0 3.9 %prepare.1 = (bf16[384,3072]{1,0:T(8,128)(2,1)}, bf16[3072,384]{1,0:T(8,128)(2,1)}, f32[162,128]{1,0:T(8,128)}, f32[162,128]{1,0:T(8,128)}, bf16[3,128,128]{2,1,...) custom-call(s32[4]{0:T(128)S(1)} %pad_add_fusion.place_ref, ...), custom_call_target="tpu_custom_call" | custom-call | tf_op jit(solution)/shard_map/prepare/pallas_call | solution.py:420
  43.9 0.0 collective-permute-done.4.swapped_ref
  43.9 4.6 %all-to-all-done.pieces_ref = bf16[64,48,128]{2,1,0:T(8,128)(2,1)S(1)} async-done(((bf16[64,48,128]{2,1,0:T(8,128)(2,1)}), bf16[64,48,128]{2,1,0:T(8,128)(2,1)S(1)}, u32[]{:S(2)}, u32[]{:S(2)}) %all-to-all-start) | async-done | bytes 786464 | tf_op jit(solution)/shard_map/all_to_all | solution.py:476
  48.5 0.0 copy-done.2
  48.5 5.7 %middle_part.1 = bf16[64,48,128]{2,1,0:T(8,128)(2,1)S(1)} custom-call(s32[4]{0:T(128)S(1)} %pad_add_fusion.place_ref, s32[64]{0:T(128)S(1)} %copy-done.2, bf16[384,3072]{1,0:T(8,128)(2,1)} %get-tuple-element.20.tokens_hbm, bf16[3072,384]{1,0:T(8,128)(2,1)} %get-tuple-element.21.turned_hbm, bf16[64,48,128]{2,1,0:T(8,128)(2,1)S(1)} %all-to-all-done.pieces_ref, ...), custom_call_target="tpu_custom_call" | custom-call | tf_op jit(solution)/shard_map/middle_part/pallas_call | solution.py:420
  54.3 0.0 copy-start
  54.3 0.0 copy-start.1
  54.3 33.6 %all_to_all.10.terms_ref = bf16[64,48,128]{2,1,0:T(8,128)(2,1)S(1)} all-to-all(bf16[64,48,128]{2,1,0:T(8,128)(2,1)S(1)} %middle_part.1), channel_id=1, replica_groups=mesh['dp'=64,'tensor'=8,'replica'=2] {'dp'}, dimensions={0} | all-to-all | bytes 1572864 | tf_op jit(solution)/shard_map/all_to_all | solution.py:527
  88.0 0.4 add_groups.1
  88.4 4.8 %all-gather = f32[192,128]{1,0:T(8,128)S(1)} all-gather(f32[96,128]{1,0:T(8,128)S(1)} %add_groups.1), channel_id=2, replica_groups=mesh['dp'=64,'tensor'=8,'replica'=2] {'replica'}, dimensions={0}, use_global_device_ids=true | all-gather | bytes 147456 | tf_op jit(solution)/shard_map/all_gather | solution.py:529
  93.2 0.0 copy-done
  93.2 0.0 copy-done.1
  93.2 1.5 %update_shard.1 = f32[1,20736]{1,0:T(1,128)} custom-call(s32[4]{0:T(128)S(1)} %pad_add_fusion.place_ref, s32[64]{0:T(128)S(1)} %copy-done.2, f32[2,96,128]{2,1,0:T(8,128)S(1)} %bitcast.5, f32[162,128]{1,0:T(8,128)S(1)} %copy-done, f32[162,128]{1,0:T(8,128)S(1)} %copy-done.1), custom_call_target="tpu_custom_call" | custom-call | tf_op jit(solution)/shard_map/update_shard/pallas_call | solution.py:420
  (4 shorter events, 0.1 us)
Async XLA Ops:
  2.7 21.6 %collective-permute-start = (bf16[64,4608]{1,0:T(8,128)(2,1)S(1)}, bf16[64,4608]{1,0:T(8,128)(2,1)S(1)}, u32[]{:S(2)}, u32[]{:S(2)}) collective-permute-start(bf16[64,4608]{1,0:T(8,128)(2,1)S(1)} %get-tuple-element.18), channel_id=1, source_target_pairs={{0,128},{16,144},{32,160},{48,176},{64,192},{80,208},{96,224},{112... | collective-permute-start | bytes 1769480 | tf_op jit(solution)/shard_map/ppermute | solution.py:473
  6.1 18.1 %collective-permute-start.1 = (bf16[64,3840]{1,0:T(8,128)(2,1)S(1)}, bf16[64,3840]{1,0:T(8,128)(2,1)S(1)}, u32[]{:S(2)}, u32[]{:S(2)}) collective-permute-start(bf16[64,3840]{1,0:T(8,128)(2,1)S(1)} %get-tuple-element.19), channel_id=1, source_target_pairs={{0,1},{1,0},{2,3},{3,2},{4,5},{5,4},{6,7},{7,6},{8,9},{9,8},{10,11... | collective-permute-start | bytes 1474568 | tf_op jit(solution)/shard_map/ppermute | solution.py:447
  11.3 37.2 %all-to-all-start = ((bf16[64,48,128]{2,1,0:T(8,128)(2,1)}), bf16[64,48,128]{2,1,0:T(8,128)(2,1)S(1)}, u32[]{:S(2)}, u32[]{:S(2)}) async-start(bf16[64,48,128]{2,1,0:T(8,128)(2,1)} %get-tuple-element.22), calls=%async_computation | async-start | bytes 1572864 | tf_op jit(solution)/shard_map/all_to_all | solution.py:476
  24.3 13.7 %collective-permute-start.3 = (bf16[64,3840]{1,0:T(8,128)(2,1)S(1)}, bf16[64,3840]{1,0:T(8,128)(2,1)S(1)}, u32[]{:S(2)}, u32[]{:S(2)}) collective-permute-start(bf16[64,3840]{1,0:T(8,128)(2,1)S(1)} %slice.18), channel_id=1, source_target_pairs={{0,1},{1,0},{2,3},{3,2},{4,5},{5,4},{6,7},{7,6},{8,9},{9,8},{10,11... | collective-permute-start | bytes 1474568 | tf_op jit(solution)/shard_map/ppermute | solution.py:447
  28.0 12.0 %collective-permute-start.2 = (bf16[128,3072]{1,0:T(8,128)(2,1)S(1)}, bf16[128,3072]{1,0:T(8,128)(2,1)S(1)}, u32[]{:S(2)}, u32[]{:S(2)}) collective-permute-start(bf16[128,3072]{1,0:T(8,128)(2,1)S(1)} %pad_maximum_fusion), channel_id=1, source_target_pairs={{0,2},{2,0},{4,6},{6,4},{8,10},{10,8},{12,14},{14,12},{1,3},{3,1},... | collective-permute-start | bytes 2359304 | tf_op jit(solution)/shard_map/ppermute | solution.py:450
  38.1 10.5 %copy-start.2 = (s32[64]{0:T(128)S(1)}, s32[64]{0:T(128)}, u32[]{:S(2)}) copy-start(s32[64]{0:T(128)} %counts_ref.3) | copy-start | bytes 772
  38.1 5.9 %collective-permute-start.4 = (bf16[64,3072]{1,0:T(8,128)(2,1)S(1)}, bf16[64,3072]{1,0:T(8,128)(2,1)S(1)}, u32[]{:S(2)}, u32[]{:S(2)}) collective-permute-start(bf16[64,3072]{1,0:T(8,128)(2,1)S(1)} %slice.19), channel_id=1, source_target_pairs={{0,2},{2,0},{4,6},{6,4},{8,10},{10,8},{12,14},{14,12},{1,3},{3,1},... | collective-permute-start | bytes 1179656 | tf_op jit(solution)/shard_map/ppermute | solution.py:450
  54.3 38.9 %copy-start = (f32[162,128]{1,0:T(8,128)S(1)}, f32[162,128]{1,0:T(8,128)}, u32[]{:S(2)}) copy-start(f32[162,128]{1,0:T(8,128)} %get-tuple-element.27.factor_ref) | copy-start | bytes 248836
  54.3 38.9 %copy-start.1 = (f32[162,128]{1,0:T(8,128)S(1)}, f32[162,128]{1,0:T(8,128)}, u32[]{:S(2)}) copy-start(f32[162,128]{1,0:T(8,128)} %get-tuple-element.28.base_ref) | copy-start | bytes 248836
